TPU v7x, 128 devices: a whole 4x4x4 slice. The times are simulated.
128 devices in a mesh: ctx: 16 (over z, x_hi, core), fsdp: 8 (over x_lo, y).
Axes of the slice: x: 4 (x_hi: 2, x_lo: 2; x = x_hi * 2 + x_lo), y: 4, z: 4, core: 2. Of those that a mesh axis runs over, the one named last changes fastest.
Arguments:
- tokens: bfloat16 [8, 2048, 1024], P('fsdp', 'ctx'), may hold values from -6 to 6
- w_qkv: bfloat16 [1024, 3072], P('fsdp'), may hold values from -0.25 to 0.25
- w_out: bfloat16 [1024, 1024], P('fsdp'), may hold values from -0.75 to 0.75
- w_up: bfloat16 [1024, 4096], P('fsdp'), may hold values from -0.1875 to 0.1875
- w_down: bfloat16 [1024, 4096], P('fsdp'), may hold values from -0.125 to 0.125
- ln1_gain: bfloat16 [1024], P('fsdp'), may hold values from 0.5 to 1.5
- ln1_bias: bfloat16 [1024], P('fsdp'), may hold values from -2.5 to 2.5
- ln2_gain: bfloat16 [1024], P('fsdp'), may hold values from 0.5 to 1.5
- ln2_bias: bfloat16 [1024], P('fsdp'), may hold values from -2.5 to 2.5
- cotangent: bfloat16 [8, 2048, 1024], P('fsdp', 'ctx'), may hold values from -6 to 6
Outputs:
- layer_out: bfloat16 [8, 2048, 1024], P('fsdp', 'ctx')
- input_grad: float32 [8, 2048, 1024], P('fsdp', 'ctx')
- grad_w_qkv: float32 [1024, 3072], P('fsdp')
- grad_w_out: float32 [1024, 1024], P('fsdp')
- grad_w_up: float32 [1024, 4096], P('fsdp')
- grad_w_down: float32 [1024, 4096], P('fsdp')
- grad_ln1_gain: float32 [1024], P('fsdp')
- grad_ln1_bias: float32 [1024], P('fsdp')
- grad_ln2_gain: float32 [1024], P('fsdp')
- grad_ln2_bias: float32 [1024], P('fsdp')
All inputs are finite; a program needn't handle non-finite values.
Results may differ from a plain program's by a relative error of at most 0.023.
Values may be sent and summed in bfloat16 or wider, within the bound.
No kernel may reach another device: no remote copies, remote signals or barrier semaphores. Data moves between devices by JAX's collectives and lax.ppermute only.
A program may use at most 256 MiB of HBM per device.

v0:
```python
import jax
import jax.numpy as jnp
from jax import lax
from jax.sharding import PartitionSpec as P

HEADS = 16


epsilon = 1e-12


def from_behind(value, axis, by):
    count = lax.axis_size(axis)
    return lax.ppermute(value, axis, [(i, (i + by) % count) for i in range(count)])


def layer_norm(values, norm_gain, norm_bias):
    center = values - jnp.mean(values, axis=-1, keepdims=True)
    spread = jnp.mean(center * center, axis=-1, keepdims=True)
    return center * lax.rsqrt(spread + epsilon) * norm_gain + norm_bias


def exact_gelu(values):
    return jax.nn.gelu(values, approximate=False)


def plain_dot(left_side, right_side):
    return jnp.dot(left_side, right_side, preferred_element_type=jnp.float32)


def contract_rows(left_side, right_side):
    return lax.dot_general(
        left_side, right_side, (((0,), (0,)), ((), ())), preferred_element_type=jnp.float32
    )


def contract_cols(left_side, right_side):
    return lax.dot_general(
        left_side, right_side, (((1,), (1,)), ((), ())), preferred_element_type=jnp.float32
    )


def split_heads(matrix):
    return matrix.reshape(matrix.shape[0], HEADS, matrix.shape[1] // HEADS)


def block_length(total_rows, shard_rows):
    shards = total_rows // shard_rows
    chosen = max(
        [
            factor
            for factor in range(1, shards + 1)
            if shards % factor == 0 and factor * shard_rows <= 1024
        ]
        + [1]
    )
    return chosen * shard_rows


def fold_blocks(running, pieces, shard_rows, work):
    total_rows = pieces[0].shape[0]
    length = block_length(total_rows, shard_rows)
    number = total_rows // length
    stacked = tuple((member.reshape((number, length) + member.shape[1:]) for member in pieces))

    def advance(status, element):
        position, blocks = element
        return (work(status, blocks, position * length), None)

    status, unused = lax.scan(advance, running, (jnp.arange(number, dtype=jnp.int32), stacked))
    return status


def per_device(
    tokens, w_qkv, w_out, w_up, w_down, ln1_gain, ln1_bias, ln2_gain, ln2_bias, cotangent
):
    inputs = tokens[0]
    shard_rows = inputs.shape[0]
    model_width = inputs.shape[1]
    ff_cols = w_up.shape[1]
    qkv_cols = 3 * model_width
    ctx_count = lax.axis_size("ctx")
    shard_count = lax.axis_size("fsdp")
    score_scale = (model_width // HEADS) ** (-0.5)
    norm_rows = jnp.stack([ln1_gain, ln1_bias, ln2_gain, ln2_bias], axis=1)
    full_qkv, full_out, full_norms = (
        lax.all_gather(w_qkv, "fsdp", axis=0, tiled=True),
        lax.all_gather(w_out, "fsdp", axis=0, tiled=True),
        lax.all_gather(norm_rows, "fsdp", axis=0, tiled=True),
    )
    norm_params = full_norms.astype(jnp.float32)
    projected = plain_dot(inputs, full_qkv).astype(jnp.bfloat16)
    query_part = projected[:, :model_width]
    key_part = projected[:, model_width : 2 * model_width]
    value_part = projected[:, 2 * model_width :]
    query_heads = split_heads(query_part)

    def attend(running, blocks, offset):
        row_max, row_total, weighted = running
        key_heads = split_heads(blocks[0])
        value_heads = split_heads(blocks[1])
        scores = (
            jnp.einsum("qhd,khd->hqk", query_heads, key_heads, preferred_element_type=jnp.float32)
            * score_scale
        )
        new_max = jnp.maximum(row_max, jnp.max(scores, axis=2))
        weights = jnp.exp(scores - new_max[:, :, None])
        fading = jnp.exp(row_max - new_max)
        row_total = row_total * fading + jnp.sum(weights, axis=2)
        update = jnp.einsum(
            "hqk,khd->qhd",
            weights.astype(jnp.bfloat16),
            value_heads,
            preferred_element_type=jnp.float32,
        )
        weighted = weighted * jnp.transpose(fading)[:, :, None] + update
        return (new_max, row_total, weighted)

    start_state = (
        jnp.full((HEADS, shard_rows), -1e30, jnp.float32),
        jnp.zeros((HEADS, shard_rows), jnp.float32),
        jnp.zeros((shard_rows, HEADS, model_width // HEADS), jnp.float32),
    )
    row_max, row_total, weighted = fold_blocks(
        start_state,
        (
            lax.all_gather(key_part, "ctx", axis=0, tiled=True),
            lax.all_gather(value_part, "ctx", axis=0, tiled=True),
        ),
        shard_rows,
        attend,
    )
    attended = (weighted / jnp.transpose(row_total)[:, :, None]).reshape(shard_rows, model_width)
    log_total = row_max + jnp.log(row_total)
    attended_low = attended.astype(jnp.bfloat16)
    branch = plain_dot(attended_low, full_out)
    residual = inputs.astype(jnp.float32) + branch
    hidden, norm_one_pull = jax.vjp(layer_norm, residual, norm_params[:, 0], norm_params[:, 1])
    hidden_low = hidden.astype(jnp.bfloat16)
    columns = hidden_low
    upward = plain_dot(columns, lax.all_gather(w_up, "fsdp", axis=0, tiled=True))
    activated, gelu_pull = jax.vjp(exact_gelu, upward)
    activated_low = activated.astype(jnp.bfloat16)
    feed_forward = contract_cols(activated_low, lax.all_gather(w_down, "fsdp", axis=0, tiled=True))
    mixed_sum = hidden + feed_forward
    layer_value, norm_two_pull = jax.vjp(
        layer_norm, mixed_sum, norm_params[:, 2], norm_params[:, 3]
    )
    grad_mixed, gain_two_grad, bias_two_grad = norm_two_pull(cotangent[0].astype(jnp.float32))
    grad_mixed_low = grad_mixed.astype(jnp.bfloat16)
    columns = grad_mixed_low
    grad_activated = plain_dot(columns, lax.all_gather(w_down, "fsdp", axis=0, tiled=True))
    grad_upward = gelu_pull(grad_activated)[0]
    grad_upward_low = grad_upward.astype(jnp.bfloat16)
    grad_hidden = grad_mixed + contract_cols(
        grad_upward_low, lax.all_gather(w_up, "fsdp", axis=0, tiled=True)
    )
    grad_residual, gain_one_grad, bias_one_grad = norm_one_pull(grad_hidden)
    grad_residual_low = grad_residual.astype(jnp.bfloat16)
    grad_attended_low = contract_cols(grad_residual_low, full_out).astype(jnp.bfloat16)
    grad_heads = split_heads(grad_attended_low)
    delta_rows = jnp.transpose(
        jnp.sum(split_heads(grad_attended_low.astype(jnp.float32) * attended), axis=2)
    )

    def block_grads(key_block, value_block):
        key_count = key_block.shape[0]
        key_heads = split_heads(key_block)
        value_heads = split_heads(value_block)
        scores = (
            jnp.einsum("qhd,khd->hqk", query_heads, key_heads, preferred_element_type=jnp.float32)
            * score_scale
        )
        probabilities = jnp.exp(scores - log_total[:, :, None])
        grad_prob = jnp.einsum(
            "qhd,khd->hqk", grad_heads, value_heads, preferred_element_type=jnp.float32
        )
        grad_score = (probabilities * (grad_prob - delta_rows[:, :, None])).astype(jnp.bfloat16)
        query_update = jnp.einsum(
            "hqk,khd->qhd", grad_score, key_heads, preferred_element_type=jnp.float32
        ).reshape(shard_rows, model_width)
        key_update = jnp.einsum(
            "hqk,qhd->khd", grad_score, query_heads, preferred_element_type=jnp.float32
        ).reshape(key_count, model_width)
        value_update = jnp.einsum(
            "hqk,qhd->khd",
            probabilities.astype(jnp.bfloat16),
            grad_heads,
            preferred_element_type=jnp.float32,
        ).reshape(key_count, model_width)
        return (query_update, key_update, value_update)

    def cycle_turn(position, status):
        held_pair, grad_held, grad_query = status
        query_update, key_update, value_update = block_grads(held_pair[0], held_pair[1])
        grad_query = grad_query + query_update
        grad_held = grad_held + jnp.stack([key_update, value_update])
        held_pair = from_behind(held_pair, "ctx", 1)
        grad_held = from_behind(grad_held.astype(jnp.bfloat16), "ctx", 1).astype(grad_held.dtype)
        return (held_pair, grad_held, grad_query)

    cycle_start = (
        jnp.stack([key_part, value_part]),
        jnp.zeros((2, shard_rows, model_width), jnp.float32),
        jnp.zeros((shard_rows, model_width), jnp.float32),
    )
    unused_pair, grad_held, grad_query = lax.fori_loop(0, ctx_count, cycle_turn, cycle_start)
    grad_projected_low = jnp.concatenate(
        [grad_query * score_scale, grad_held[0] * score_scale, grad_held[1]], axis=1
    ).astype(jnp.bfloat16)
    input_grad = grad_residual + contract_cols(grad_projected_low, full_qkv)
    norm_partial = jnp.stack([gain_one_grad, bias_one_grad, gain_two_grad, bias_two_grad])
    norm_total = lax.psum(norm_partial, ("ctx", "fsdp"))
    shard_width = model_width // shard_count
    norm_share = lax.dynamic_slice_in_dim(
        norm_total, lax.axis_index("fsdp") * shard_width, shard_width, 1
    )
    piece_rows = model_width // (ctx_count * shard_count)

    def reorder(matrix):
        return (
            matrix.reshape(shard_rows, shard_count, ctx_count, piece_rows)
            .transpose(0, 2, 1, 3)
            .reshape(shard_rows, model_width)
        )

    pairs = (
        (reorder(inputs), grad_projected_low),
        (reorder(attended_low), grad_residual_low),
        (reorder(hidden_low), grad_upward_low),
        (reorder(grad_mixed_low), activated_low),
    )
    products = [contract_rows(left_side, right_side) for left_side, right_side in pairs]
    share = lax.psum_scatter(
        jnp.concatenate(products, axis=1), ("ctx", "fsdp"), scatter_dimension=0, tiled=True
    )
    summed = lax.all_gather(share.astype(jnp.bfloat16), "ctx", axis=0, tiled=True).astype(
        share.dtype
    )
    first_end = qkv_cols + model_width
    second_end = first_end + ff_cols
    return (
        layer_value.astype(jnp.bfloat16)[None],
        input_grad[None],
        summed[:, :qkv_cols],
        summed[:, qkv_cols:first_end],
        summed[:, first_end:second_end],
        summed[:, second_end:],
        norm_share[0],
        norm_share[1],
        norm_share[2],
        norm_share[3],
    )


def solution(mesh):
    return jax.shard_map(
        per_device,
        mesh=mesh,
        in_specs=(
            P("fsdp", "ctx", None),
            P("fsdp", None),
            P("fsdp", None),
            P("fsdp", None),
            P("fsdp", None),
            P("fsdp"),
            P("fsdp"),
            P("fsdp"),
            P("fsdp"),
            P("fsdp", "ctx", None),
        ),
        out_specs=(
            P("fsdp", "ctx", None),
            P("fsdp", "ctx", None),
            P("fsdp", None),
            P("fsdp", None),
            P("fsdp", None),
            P("fsdp", None),
            P("fsdp"),
            P("fsdp"),
            P("fsdp"),
            P("fsdp"),
        ),
        check_vma=False,
    )
```

profile of v0, /device:TPU:1, one launch (start us, length us, event | category | flops | bytes accessed | tf_op | source)
XLA Modules:
  0.0 1731.7 jit_solution(9594125196978262294)
XLA Ops:
  8.0 77.2 %all-gather.8.cloned.1.call-done = bf16[1024,3072]{1,0:T(8,128)(2,1)} async-done(((bf16[128,3072]{1,0:T(8,128)(2,1)}), bf16[1024,3072]{1,0:T(8,128)(2,1)}) %all-gather.8.cloned.1.call-update) | async-done | bytes 6291472 | tf_op jit(solution)/shard_map/all_gather | solution.py:87
  85.2 3.9 convolution_convert_fusion
  93.6 12.6 all_gather.30
  107.4 37.4 %all-gather.12.cloned.1.call-done = bf16[2048,1024]{1,0:T(8,128)(2,1)} async-done(((bf16[128,1024]{1,0:T(8,128)(2,1)}), bf16[2048,1024]{1,0:T(8,128)(2,1)}) %all-gather.12.cloned.1.call-update) | async-done | bytes 4194320 | tf_op jit(solution)/shard_map/all_gather | solution.py:128
  144.8 56.3 %all-gather.10.cloned.1.call-done = bf16[2048,1024]{1,0:T(8,128)(2,1)} async-done(((bf16[128,1024]{1,0:T(8,128)(2,1)}), bf16[2048,1024]{1,0:T(8,128)(2,1)}) %all-gather.10.cloned.1.call-update) | async-done | bytes 4194320 | tf_op jit(solution)/shard_map/all_gather | solution.py:127
  201.1 31.6 %while.30 = (s32[]{:T(128)}, f32[16,128]{1,0:T(8,128)S(1)}, f32[16,128]{1,0:T(8,128)S(1)}, f32[128,16,64]{0,2,1:T(8,128)S(1)}, bf16[2,1024,1024]{2,1,0:T(8,128)(...) while((s32[]{:T(128)}, f32[16,128]{1,0:T(8,128)S(1)}, ...), condition=%wide.region_3.4_spmd.clone, body=%wide.region_0.3_spmd.clone.sunk | while | flops 554053632 | bytes 47579248 | solution.py:70
  201.1 4.0 constant_dynamic-slice_fusion.4
  205.1 2.5 copy.53
  207.6 2.9 copy.54
  210.5 3.1 bitcast_reduce_fusion.3
  216.9 4.0 constant_dynamic-slice_fusion.4
  220.9 2.5 copy.53
  223.4 2.9 copy.54
  226.3 3.1 bitcast_reduce_fusion.3
  239.7 94.5 %all-gather.16.cloned.1.call-done = bf16[1024,4096]{1,0:T(8,128)(2,1)} async-done(((bf16[128,4096]{1,0:T(8,128)(2,1)}), bf16[1024,4096]{1,0:T(8,128)(2,1)}) %all-gather.16.cloned.1.call-update) | async-done | bytes 8388624 | tf_op jit(solution)/shard_map/all_gather | solution.py:141
  334.2 9.0 multiply_convert_fusion
  343.2 83.2 %all-gather.18.cloned.1.call-done = bf16[1024,4096]{1,0:T(8,128)(2,1)} async-done(((bf16[128,4096]{1,0:T(8,128)(2,1)}), bf16[1024,4096]{1,0:T(8,128)(2,1)}) %all-gather.18.cloned.1.call-update) | async-done | bytes 8388624 | tf_op jit(solution)/shard_map/all_gather | solution.py:144
  426.4 6.4 fusion.55
  435.3 6.7 add_convert_fusion
  442.1 6.9 multiply_reduce_fusion
  452.2 352.4 %while.31 = (s32[]{:T(128)}, bf16[2,128,1024]{1,2,0:T(8,128)(2,1)}, f32[2,128,1024]{1,2,0:T(8,128)}, f32[128,1024]{0,1:T(8,128)S(1)}, bf16[128,16,64]{0,2,1:T(8,...) while((s32[]{:T(128)}, bf16[2,128,1024]{1,2,0:T(8,128)(2,1)}, ...), condition=%wide.region_14.15_spmd.clone, body=%wide.region_13.14_spmd.clone.sunk | while | flops 170917888 | bytes 20201664 | solution.py:207
  455.8 3.0 collective-permute-start.1
  459.4 5.8 collective-permute-done.1
  466.3 4.5 collective-permute-done
  475.6 4.1 collective-permute-start.1
  480.3 5.8 collective-permute-done.1
  487.2 4.5 collective-permute-done
  496.5 4.1 collective-permute-start.1
  501.2 5.8 collective-permute-done.1
  508.0 4.5 collective-permute-done
  517.3 4.1 collective-permute-start.1
  522.0 5.8 collective-permute-done.1
  528.9 4.5 collective-permute-done
  538.2 4.1 collective-permute-start.1
  543.4 7.3 collective-permute-done.1
  551.8 2.4 collective-permute-done
  559.1 4.1 collective-permute-start.1
  565.2 8.6 collective-permute-done.1
  580.0 4.1 collective-permute-start.1
  584.0 2.4 collective-permute-start
  587.0 9.8 collective-permute-done.1
  604.9 3.3 collective-permute-start
  608.7 11.0 collective-permute-done.1
  625.8 4.1 collective-permute-start
  630.5 12.2 collective-permute-done.1
  648.6 3.1 collective-permute-start
  652.3 13.4 collective-permute-done.1
  674.1 14.6 collective-permute-done.1
  695.8 15.8 collective-permute-done.1
  718.1 16.5 collective-permute-done.1
  741.1 16.5 collective-permute-done.1
  764.0 16.5 collective-permute-done.1
  787.0 16.5 collective-permute-done.1
  809.0 2.7 fusion.46
  811.7 6.3 convolution_bitcast_fusion
  818.1 12.7 copy.45
  830.8 8.0 fusion.59
  838.8 8.2 fusion.58
  847.0 33.2 %pad_maximum_fusion = f32[1024,12288]{1,0:T(8,128)} fusion(f32[1024,4096]{1,0:T(8,128)} %fusion.59, f32[1024,4096]{1,0:T(8,128)} %fusion.58, f32[1024,1024]{1,0:T(8,128)} %fusion.46, f32[1024,3072]{1,0:T(8,128)} %copy.45), kind=kLoop, calls=%fused_computation.30 | loop fusion | flops 37748736 | bytes 100663296 | tf_op jit(solution)/shard_map/concatenate | solution.py:235
  880.3 748.4 %reduce-scatter.2.cloned.1.call-done = f32[8,12288]{1,0:T(8,128)} async-done(((f32[1024,12288]{1,0:T(8,128)}), f32[8,12288]{1,0:T(8,128)}) %reduce-scatter.2.cloned.1.call-update) | async-done | bytes 393232 | tf_op jit(solution)/shard_map/reduce_scatter | solution.py:234
  1630.4 81.2 %psum.7 = f32[4,1024]{1,0:T(4,128)S(1)} all-reduce(f32[4,1024]{1,0:T(4,128)S(1)} %pad_maximum_fusion.5), channel_id=1, replica_groups=mesh['ctx'=16,'fsdp'=8] {'ctx','fsdp'}, use_global_device_ids=true, to_apply=%region_20.21 | all-reduce | flops 4096 | bytes 32768 | tf_op jit(solution)/shard_map/psum | solution.py:213
  1712.2 5.8 fusion.29
  1719.9 2.4 slice.85
  1722.3 2.5 fusion.52
  (310 shorter events, 143.2 us)
Async XLA Ops:
  7.2 78.0 %all-gather.8.cloned.1.call-start = ((), (), s32[]{:S(2)}) async-start(), calls=%async_computation.1 | async-start | bytes 7077888 | tf_op jit(solution)/shard_map/all_gather | solution.py:87
  7.9 136.9 %all-gather.12.cloned.1.call-start = ((), (), s32[]{:S(2)}) async-start(), calls=%async_computation.3 | async-start | bytes 4456448 | tf_op jit(solution)/shard_map/all_gather | solution.py:128
  89.0 3.5 copy-start.9
  90.0 3.6 copy-start.16
  90.0 3.6 copy-start.17
  90.0 3.6 copy-start.18
  90.0 3.6 copy-start.19
  90.0 111.1 %all-gather.10.cloned.1.call-start = ((), (), s32[]{:S(2)}) async-start(), calls=%async_computation.2 | async-start | bytes 4456448 | tf_op jit(solution)/shard_map/all_gather | solution.py:127
  90.8 145.6 %all-gather.14.cloned.1.call-start = ((), (), s32[]{:S(2)}) async-start(), calls=%async_computation.4 | async-start | bytes 2359296 | tf_op jit(solution)/shard_map/all_gather | solution.py:88
  91.3 242.8 %all-gather.16.cloned.1.call-start = ((), (), s32[]{:S(2)}) async-start(), calls=%async_computation.5 | async-start | bytes 9437184 | tf_op jit(solution)/shard_map/all_gather | solution.py:141
  91.9 334.5 %all-gather.18.cloned.1.call-start = ((), (), s32[]{:S(2)}) async-start(), calls=%async_computation.6 | async-start | bytes 9437184 | tf_op jit(solution)/shard_map/all_gather | solution.py:144
  92.5 1536.1 %reduce-scatter.2.cloned.1.call-start = ((), (), s32[]{:S(2)}) async-start(), calls=%async_computation.7 | async-start | bytes 50724864 | tf_op jit(solution)/shard_map/reduce_scatter | solution.py:234
  232.7 3.6 copy-start.10
  343.2 89.6 %copy-start.5 = (bf16[128,4096]{1,0:T(8,128)(2,1)}, bf16[128,4096]{1,0:T(8,128)(2,1)S(1)}, u32[]{:S(2)}) copy-start(bf16[128,4096]{1,0:T(8,128)(2,1)S(1)} %get-tuple-element.221) | copy-start | bytes 3145732
  426.4 6.6 copy-start.11
  434.3 1.0 copy-start.4
  442.0 6.9 copy-start.7
  442.1 7.2 copy-start.1
  442.1 7.2 copy-start.13
  449.3 1.6 copy-start.2
  455.8 9.4 collective-permute-start.1
  458.8 12.0 collective-permute-start
  475.6 10.5 collective-permute-start.1
  479.7 12.0 collective-permute-start
  496.5 10.5 collective-permute-start.1
  500.6 12.0 collective-permute-start
  517.3 10.5 collective-permute-start.1
  521.4 12.0 collective-permute-start
  538.2 12.6 collective-permute-start.1
  542.3 12.0 collective-permute-start
  559.1 14.7 collective-permute-start.1
  563.2 12.0 collective-permute-start
  580.0 16.8 collective-permute-start.1
  584.0 13.7 collective-permute-start
  602.6 17.1 collective-permute-start.1
  604.9 15.8 collective-permute-start
  625.6 17.1 collective-permute-start.1
  625.8 17.9 %collective-permute-start = (bf16[2,128,1024]{1,2,0:T(8,128)(2,1)S(1)}, bf16[2,128,1024]{1,2,0:T(8,128)(2,1)}, u32[]{:S(2)}, u32[]{:S(2)}) collective-permute-start(bf16[2,128,1024]{1,2,0:T(8,128)(2,1)S(1)} %copy.72), channel_id=1, source_target_pairs={{0,8},{8,16},{16,24},{24,32},{32,40},{40,48},{48,56},{56,64},{64,7... | collective-permute-start | bytes 1572872 | tf_op jit(solution)/shard_map/while/body/eval_jaxpr/ppermute | solution.py:14
  648.6 17.1 collective-permute-start.1
  648.6 18.1 %collective-permute-start = (bf16[2,128,1024]{1,2,0:T(8,128)(2,1)S(1)}, bf16[2,128,1024]{1,2,0:T(8,128)(2,1)}, u32[]{:S(2)}, u32[]{:S(2)}) collective-permute-start(bf16[2,128,1024]{1,2,0:T(8,128)(2,1)S(1)} %copy.72), channel_id=1, source_target_pairs={{0,8},{8,16},{16,24},{24,32},{32,40},{40,48},{48,56},{56,64},{64,7... | collective-permute-start | bytes 1572872 | tf_op jit(solution)/shard_map/while/body/eval_jaxpr/ppermute | solution.py:14
  671.5 17.1 collective-permute-start.1
  671.5 18.1 %collective-permute-start = (bf16[2,128,1024]{1,2,0:T(8,128)(2,1)S(1)}, bf16[2,128,1024]{1,2,0:T(8,128)(2,1)}, u32[]{:S(2)}, u32[]{:S(2)}) collective-permute-start(bf16[2,128,1024]{1,2,0:T(8,128)(2,1)S(1)} %copy.72), channel_id=1, source_target_pairs={{0,8},{8,16},{16,24},{24,32},{32,40},{40,48},{48,56},{56,64},{64,7... | collective-permute-start | bytes 1572872 | tf_op jit(solution)/shard_map/while/body/eval_jaxpr/ppermute | solution.py:14
  694.5 17.1 collective-permute-start.1
  694.5 18.1 %collective-permute-start = (bf16[2,128,1024]{1,2,0:T(8,128)(2,1)S(1)}, bf16[2,128,1024]{1,2,0:T(8,128)(2,1)}, u32[]{:S(2)}, u32[]{:S(2)}) collective-permute-start(bf16[2,128,1024]{1,2,0:T(8,128)(2,1)S(1)} %copy.72), channel_id=1, source_target_pairs={{0,8},{8,16},{16,24},{24,32},{32,40},{40,48},{48,56},{56,64},{64,7... | collective-permute-start | bytes 1572872 | tf_op jit(solution)/shard_map/while/body/eval_jaxpr/ppermute | solution.py:14
  717.5 17.1 collective-permute-start.1
  717.5 18.1 %collective-permute-start = (bf16[2,128,1024]{1,2,0:T(8,128)(2,1)S(1)}, bf16[2,128,1024]{1,2,0:T(8,128)(2,1)}, u32[]{:S(2)}, u32[]{:S(2)}) collective-permute-start(bf16[2,128,1024]{1,2,0:T(8,128)(2,1)S(1)} %copy.72), channel_id=1, source_target_pairs={{0,8},{8,16},{16,24},{24,32},{32,40},{40,48},{48,56},{56,64},{64,7... | collective-permute-start | bytes 1572872 | tf_op jit(solution)/shard_map/while/body/eval_jaxpr/ppermute | solution.py:14
  740.5 17.1 collective-permute-start.1
  740.5 18.1 %collective-permute-start = (bf16[2,128,1024]{1,2,0:T(8,128)(2,1)S(1)}, bf16[2,128,1024]{1,2,0:T(8,128)(2,1)}, u32[]{:S(2)}, u32[]{:S(2)}) collective-permute-start(bf16[2,128,1024]{1,2,0:T(8,128)(2,1)S(1)} %copy.72), channel_id=1, source_target_pairs={{0,8},{8,16},{16,24},{24,32},{32,40},{40,48},{48,56},{56,64},{64,7... | collective-permute-start | bytes 1572872 | tf_op jit(solution)/shard_map/while/body/eval_jaxpr/ppermute | solution.py:14
  763.5 17.1 collective-permute-start.1
  763.5 18.1 %collective-permute-start = (bf16[2,128,1024]{1,2,0:T(8,128)(2,1)S(1)}, bf16[2,128,1024]{1,2,0:T(8,128)(2,1)}, u32[]{:S(2)}, u32[]{:S(2)}) collective-permute-start(bf16[2,128,1024]{1,2,0:T(8,128)(2,1)S(1)} %copy.72), channel_id=1, source_target_pairs={{0,8},{8,16},{16,24},{24,32},{32,40},{40,48},{48,56},{56,64},{64,7... | collective-permute-start | bytes 1572872 | tf_op jit(solution)/shard_map/while/body/eval_jaxpr/ppermute | solution.py:14
  786.5 17.1 collective-permute-start.1
  786.5 18.1 %collective-permute-start = (bf16[2,128,1024]{1,2,0:T(8,128)(2,1)S(1)}, bf16[2,128,1024]{1,2,0:T(8,128)(2,1)}, u32[]{:S(2)}, u32[]{:S(2)}) collective-permute-start(bf16[2,128,1024]{1,2,0:T(8,128)(2,1)S(1)} %copy.72), channel_id=1, source_target_pairs={{0,8},{8,16},{16,24},{24,32},{32,40},{40,48},{48,56},{56,64},{64,7... | collective-permute-start | bytes 1572872 | tf_op jit(solution)/shard_map/while/body/eval_jaxpr/ppermute | solution.py:14
  804.6 4.3 copy-start.15
  804.6 4.4 copy-start.3
  809.0 2.7 copy-start.14
  818.1 12.7 copy-start.6
  830.8 8.0 copy-start.8
  880.2 750.2 %copy-start.12 = (bf16[1,128,1024]{2,1,0:T(8,128)(2,1)S(1)}, bf16[1,128,1024]{2,1,0:T(8,128)(2,1)}, u32[]{:S(2)}) copy-start(bf16[1,128,1024]{2,1,0:T(8,128)(2,1)} %param.23) | copy-start | bytes 786436
  880.2 837.7 %all-gather.20.cloned.1.call-start = ((), (), s32[]{:S(2)}) async-start(), calls=%async_computation.8 | async-start | bytes 3342336 | tf_op jit(solution)/shard_map/all_gather | solution.py:237
  1718.0 4.4 copy-start
Sparse Core Ops, SparseCore 0:
  9.7 75.4 all-gather.7
  90.2 54.6 all-gather.11
  147.9 53.1 all-gather.9
  202.6 33.6 all-gather.13
  237.8 96.3 all-gather.15
  335.7 90.6 all-gather.17
  880.3 748.2 reduce-scatter.1
  1631.7 63.6 all-gather.19
where the time goes:
time: 1730 us
  waiting for transfers between devices  1300 us (75%)
  matrix products  110 us (6%)
  blocking collectives  93.8 us (5%)
  other arithmetic  93.6 us (5%)
  local copies, waits for them, and re-layouts  66.5 us (4%)
  starting transfers between devices  48.1 us (3%)
    reduce_scatter x1, waiting for transfers between devices, per_device(): lax.psum_scatter(jnp.concatenate(products, axis=1), ('ctx', 'fsdp'), scat...  748 us
    ppermute x32, waiting for transfers between devices, from_behind(): lax.ppermute(value, axis, [(i, (i + by) % count) for i in range(count)])  203 us
    all_gather x1, waiting for transfers between devices, per_device(): lax.all_gather(w_up, 'fsdp', axis=0, tiled=True)  94.5 us
    all_gather x1, waiting for transfers between devices, per_device(): lax.all_gather(w_down, 'fsdp', axis=0, tiled=True)  83.2 us
    psum x1, blocking collectives, per_device(): norm_total = lax.psum(norm_partial, ('ctx', 'fsdp'))  81.2 us
    all_gather x1, waiting for transfers between devices, per_device(): lax.all_gather(w_qkv, 'fsdp', axis=0, tiled=True)  77.2 us
    all_gather x1, waiting for transfers between devices, per_device(): lax.all_gather(key_part, 'ctx', axis=0, tiled=True)  56.3 us
    ppermute x32, starting transfers between devices, from_behind(): lax.ppermute(value, axis, [(i, (i + by) % count) for i in range(count)])  47.7 us
  transfers between devices with their start and end apart: 40, of which 29 were waited for; matrix products, arithmetic and copies ran while one was open for 5% of the time, Pallas kernels for 0%

commit v1 on v0

v1 whole, which is shorter than its diff:
```python
import math

import jax
import jax.numpy as jnp
from jax import lax
from jax.experimental import pallas as pl
from jax.experimental.pallas import tpu as pltpu
from jax.sharding import Mesh, PartitionSpec as P

HEADS = 16
HEAD_DIM = 64
BLOCK = 128
EPSILON = 1e-12
LOW = jnp.bfloat16
FULL = jnp.float32

CTX = ("zh", "zl", "xh", "core")
FSDP = ("xl", "y")
Z = ("zh", "zl")
SCALE = HEAD_DIM**-0.5
QUERY_BLOCK = 256
PARTS = QUERY_BLOCK // BLOCK


def dot(left, right, left_dim, right_dim):
    return lax.dot_general(
        left, right, (((left_dim,), (right_dim,)), ((), ())), preferred_element_type=FULL
    )


def swap(value, axis):
    return lax.ppermute(value, axis, [(0, 1), (1, 0)])


def exchange(value, axes, mask):
    return lax.ppermute(value, axes, [(i, i ^ mask) for i in range(4)])


def with_pair(value, axis):
    return jnp.concatenate([value, swap(value, axis)], axis=0)


def with_four(value, axes):
    moved = {mask: exchange(value, axes, mask) for mask in (1, 3, 2)}
    return jnp.concatenate([value, moved[1], moved[2], moved[3]], axis=0)


def forward_kernel(place, q_ref, k_ref, v_ref, low_ref, out_ref, log_ref, keys):
    step = pl.program_id(0)

    @pl.when(step == 0)
    def _():
        keys[...] = k_ref[...].astype(FULL).T.astype(LOW)

    queries = q_ref[...] * LOW(SCALE)
    scores = dot(keys[...], queries, 1, 0)
    top = jnp.max(scores, axis=0, keepdims=True)
    weights = jnp.exp(scores - top)
    total = jnp.sum(weights, axis=0, keepdims=True)
    attended = dot(v_ref[...], weights.astype(LOW), 1, 0) / total
    out_ref[...] = attended
    log_ref[...] = top + jnp.log(total)
    low = attended.astype(LOW)
    for part in range(PARTS):
        low_ref[place[step * PARTS + part]] = low[:, part * BLOCK : (part + 1) * BLOCK]


def attention_forward(place, projected):
    length = projected.shape[1]
    return pl.pallas_call(
        forward_kernel,
        grid_spec=pltpu.PrefetchScalarGridSpec(
            num_scalar_prefetch=1,
            grid=(length // QUERY_BLOCK,),
            in_specs=[
                pl.BlockSpec((HEAD_DIM, QUERY_BLOCK), lambda i, p: (0, i)),
                pl.BlockSpec((HEAD_DIM, length), lambda i, p: (1, 0)),
                pl.BlockSpec((HEAD_DIM, length), lambda i, p: (2, 0)),
            ],
            out_specs=[
                pl.BlockSpec((length // BLOCK, HEAD_DIM, BLOCK), lambda i, p: (0, 0, 0)),
                pl.BlockSpec((HEAD_DIM, QUERY_BLOCK), lambda i, p: (0, i)),
                pl.BlockSpec((1, QUERY_BLOCK), lambda i, p: (0, i)),
            ],
            scratch_shapes=[pltpu.VMEM((length, HEAD_DIM), LOW)],
        ),
        out_shape=[
            jax.ShapeDtypeStruct((length // BLOCK, HEAD_DIM, BLOCK), LOW),
            jax.ShapeDtypeStruct((HEAD_DIM, length), FULL),
            jax.ShapeDtypeStruct((1, length), FULL),
        ],
        compiler_params=pltpu.CompilerParams(vmem_limit_bytes=40 * 1024 * 1024),
        cost_estimate=pl.CostEstimate(
            flops=16 * length * length * HEAD_DIM,
            bytes_accessed=10 * length * HEAD_DIM,
            transcendentals=length * length,
        ),
        name="attention_forward",
    )(place, projected, projected, projected)


def backward_kernel(
    place, q_ref, k_ref, v_ref, grad_ref, out_ref, log_ref, dq_ref, dk_ref, dv_ref,
    keys, values, dk, dv,
):
    step = pl.program_id(0)

    @pl.when(step == 0)
    def _():
        keys[...] = k_ref[...].astype(FULL).T.astype(LOW)
        values[...] = v_ref[...].astype(FULL).T.astype(LOW)
        dk[...] = jnp.zeros_like(dk)
        dv[...] = jnp.zeros_like(dv)

    queries = q_ref[...] * LOW(SCALE)
    grad = jnp.concatenate([grad_ref[place[step * PARTS + p]] for p in range(PARTS)], axis=1)
    delta = jnp.sum(grad.astype(FULL) * out_ref[...], axis=0, keepdims=True)
    scores = dot(keys[...], queries, 1, 0)
    probs = jnp.exp(scores - log_ref[...])
    grad_probs = dot(values[...], grad, 1, 0)
    grad_scores = (probs * (grad_probs - delta)).astype(LOW)
    dv[...] += dot(grad, probs.astype(LOW), 1, 1)
    dk[...] += dot(queries, grad_scores, 1, 1)
    dq_ref[...] = (dot(k_ref[...], grad_scores, 1, 0) * SCALE).astype(LOW)

    @pl.when(step == pl.num_programs(0) - 1)
    def _():
        dk_ref[...] = dk[...].astype(LOW)
        dv_ref[...] = dv[...].astype(LOW)


def attention_backward(place, projected, grad_blocks, attended, log_total):
    length = projected.shape[1]
    whole = jax.ShapeDtypeStruct((HEAD_DIM, length), LOW)
    return pl.pallas_call(
        backward_kernel,
        grid_spec=pltpu.PrefetchScalarGridSpec(
            num_scalar_prefetch=1,
            grid=(length // QUERY_BLOCK,),
            in_specs=[
                pl.BlockSpec((HEAD_DIM, QUERY_BLOCK), lambda i, p: (0, i)),
                pl.BlockSpec((HEAD_DIM, length), lambda i, p: (1, 0)),
                pl.BlockSpec((HEAD_DIM, length), lambda i, p: (2, 0)),
                pl.BlockSpec((length // BLOCK, HEAD_DIM, BLOCK), lambda i, p: (0, 0, 0)),
                pl.BlockSpec((HEAD_DIM, QUERY_BLOCK), lambda i, p: (0, i)),
                pl.BlockSpec((1, QUERY_BLOCK), lambda i, p: (0, i)),
            ],
            out_specs=[
                pl.BlockSpec((HEAD_DIM, QUERY_BLOCK), lambda i, p: (0, i)),
                pl.BlockSpec((HEAD_DIM, length), lambda i, p: (0, 0)),
                pl.BlockSpec((HEAD_DIM, length), lambda i, p: (0, 0)),
            ],
            scratch_shapes=[
                pltpu.VMEM((length, HEAD_DIM), LOW),
                pltpu.VMEM((length, HEAD_DIM), LOW),
                pltpu.VMEM((HEAD_DIM, length), FULL),
                pltpu.VMEM((HEAD_DIM, length), FULL),
            ],
        ),
        out_shape=[whole, whole, whole],
        compiler_params=pltpu.CompilerParams(vmem_limit_bytes=48 * 1024 * 1024),
        cost_estimate=pl.CostEstimate(
            flops=40 * length * length * HEAD_DIM,
            bytes_accessed=20 * length * HEAD_DIM,
            transcendentals=length * length,
        ),
        name="attention_backward",
    )(place, projected, projected, projected, grad_blocks, attended, log_total)


def assemble_kernel(spots, *refs):
    pieces, (up_ref, down_ref, out_ref, norm_ref, norm_rows) = refs[:4], refs[4:]
    part = up_ref.shape[1] // 4
    out_part = out_ref.shape[1] // 4
    rows = up_ref.shape[0] // 4
    for mask in range(4):
        place = pl.ds(pl.multiple_of(spots[mask] * rows, rows), rows)
        total = jnp.zeros((rows, BLOCK), FULL)
        for which, piece in enumerate(pieces):
            group = spots[4 + which]
            wide = pl.ds(pl.multiple_of(group * part, part), part)
            narrow = pl.ds(pl.multiple_of(group * out_part, out_part), out_part)
            source = slice(mask * rows, (mask + 1) * rows)
            up_ref[place, wide] = piece[source, :part].astype(FULL)
            down_ref[place, wide] = piece[source, part : 2 * part].astype(FULL)
            out_ref[place, narrow] = piece[source, 2 * part : 2 * part + out_part].astype(FULL)
            total += piece[source, 2 * part + out_part :].astype(FULL)
        norm_rows[place, :] = total
    norm_ref[...] = norm_rows[...].T[:8]


def assemble(spots, pieces, width, units):
    shapes = [(BLOCK, units), (BLOCK, units), (BLOCK, width), (8, BLOCK)]
    return pl.pallas_call(
        assemble_kernel,
        grid_spec=pltpu.PrefetchScalarGridSpec(
            num_scalar_prefetch=1,
            grid=(1,),
            in_specs=[pl.BlockSpec(p.shape, lambda i, s: (0, 0)) for p in pieces],
            out_specs=[pl.BlockSpec(s, lambda i, s: (0, 0)) for s in shapes],
            scratch_shapes=[pltpu.VMEM((BLOCK, BLOCK), FULL)],
        ),
        out_shape=[jax.ShapeDtypeStruct(s, FULL) for s in shapes],
        compiler_params=pltpu.CompilerParams(vmem_limit_bytes=32 * 1024 * 1024),
        name="assemble",
    )(spots, *pieces)


def assemble_qkv_kernel(spots, own_ref, pair_ref, out_ref):
    rows = BLOCK // 2
    width = out_ref.shape[1] // 3
    for core, piece in enumerate((own_ref, pair_ref)):
        for z in range(4):
            lane = spots[2 + core * 4 + z] * BLOCK
            for half in range(2):
                place = pl.ds(pl.multiple_of(spots[half] * rows, rows), rows)
                source = slice((z * 2 + half) * rows, (z * 2 + half + 1) * rows)
                for which in range(3):
                    columns = pl.ds(pl.multiple_of(which * width + lane, BLOCK), BLOCK)
                    out_ref[place, columns] = piece[
                        source, which * BLOCK : (which + 1) * BLOCK
                    ].astype(FULL)


def assemble_qkv(spots, own, pair, width):
    return pl.pallas_call(
        assemble_qkv_kernel,
        grid_spec=pltpu.PrefetchScalarGridSpec(
            num_scalar_prefetch=1,
            grid=(1,),
            in_specs=[pl.BlockSpec(own.shape, lambda i, s: (0, 0))] * 2,
            out_specs=pl.BlockSpec((BLOCK, 3 * width), lambda i, s: (0, 0)),
        ),
        out_shape=jax.ShapeDtypeStruct((BLOCK, 3 * width), FULL),
        compiler_params=pltpu.CompilerParams(vmem_limit_bytes=32 * 1024 * 1024),
        name="assemble_qkv",
    )(spots, own, pair)


def norm_forward(values):
    center = values - jnp.mean(values, axis=-1, keepdims=True)
    spread = jnp.mean(center * center, axis=-1, keepdims=True)
    inverse = lax.rsqrt(spread + EPSILON)
    return center * inverse, inverse


def norm_backward(grad, normal, inverse, gain):
    scaled = grad * gain
    result = inverse * (
        scaled
        - jnp.mean(scaled, axis=-1, keepdims=True)
        - normal * jnp.mean(scaled * normal, axis=-1, keepdims=True)
    )
    return result, jnp.sum(grad * normal, axis=0), jnp.sum(grad, axis=0)


def gather_group(value):
    return with_pair(with_pair(value, "zl"), "core")


def product_group(left, right, left_dim, right_dim):
    half = left.shape[0] // 2
    theirs = swap(dot(left[half:], right, left_dim, right_dim).astype(LOW), "core")
    near = dot(left[:half], right, left_dim, right_dim) + theirs.astype(FULL)
    return near[: half // 2] + swap(near[half // 2 :].astype(LOW), "zl").astype(FULL)


def per_device(
    tokens, w_qkv, w_out, w_up, w_down, ln1_gain, ln1_bias, ln2_gain, ln2_bias, cotangent
):
    inputs = tokens[0]
    width = inputs.shape[1]
    units = w_up.shape[1]
    ff_part = units // 4
    out_part = width // 4
    z, zh, zl, xh, core = (lax.axis_index(a) for a in (Z, "zh", "zl", "xh", "core"))
    group = zl * 2 + core
    pair = z * 2 + core
    place = jnp.stack(
        [
            ((z ^ dz) * 2 + (xh ^ dx)) * 2 + (core ^ dc)
            for dx in range(2)
            for dc in range(2)
            for dz in range(4)
        ]
    ).astype(jnp.int32)

    norm_rows = jnp.pad(
        jnp.stack([ln1_gain, ln1_bias, ln2_gain, ln2_bias], axis=1), ((0, 0), (0, BLOCK - 4))
    )
    up_mine = lax.dynamic_slice_in_dim(w_up, group * ff_part, ff_part, 1)
    down_mine = lax.dynamic_slice_in_dim(w_down, group * ff_part, ff_part, 1)
    rest = lax.all_gather(
        jnp.concatenate([w_out, up_mine, down_mine, norm_rows], axis=1), FSDP, axis=0, tiled=True
    )
    qkv_mine = jnp.concatenate(
        [
            lax.dynamic_slice_in_dim(w_qkv, which * width + pair * BLOCK, BLOCK, 1)
            for which in range(3)
        ],
        axis=1,
    )
    qkv_part = lax.all_to_all(
        jnp.broadcast_to(qkv_mine[None], (8,) + qkv_mine.shape),
        FSDP,
        split_axis=0,
        concat_axis=0,
        tiled=True,
    ).reshape(width, 3 * BLOCK)
    full_out = rest[:, :width]
    up_part = rest[:, width : width + ff_part]
    down_part = rest[:, width + ff_part : width + 2 * ff_part]
    norms = rest[:, width + 2 * ff_part : width + 2 * ff_part + 4].astype(FULL).T
    gain_one, bias_one, gain_two, bias_two = (norms[i : i + 1] for i in range(4))

    near = with_pair(with_four(inputs, Z), "core")
    projected = dot(qkv_part, near, 0, 1).astype(LOW).reshape(3, 2, HEAD_DIM, 8 * BLOCK)
    mine = lax.dynamic_index_in_dim(projected, xh, 1, keepdims=False).reshape(3 * HEAD_DIM, -1)
    other = lax.dynamic_index_in_dim(projected, 1 - xh, 1, keepdims=False)
    head = jnp.concatenate([mine, swap(other.reshape(3 * HEAD_DIM, -1), "xh")], axis=1)

    low_blocks, attended, log_total = attention_forward(place, head)
    attended_low = lax.all_to_all(low_blocks, CTX, split_axis=0, concat_axis=0, tiled=True)
    attended_low = (
        attended_low.reshape(4, 2, 2, HEAD_DIM, BLOCK)
        .transpose(0, 2, 1, 3, 4)
        .reshape(width, BLOCK)
    )

    residual = inputs.astype(FULL) + dot(attended_low, full_out, 0, 0)
    normal_one, inverse_one = norm_forward(residual)
    hidden = normal_one * gain_one + bias_one
    hidden_low = gather_group(hidden.astype(LOW))
    upward = dot(hidden_low, up_part, 1, 0)
    cdf = 0.5 * (1.0 + lax.erf(upward * math.sqrt(0.5)))
    pdf = jnp.exp(-0.5 * upward * upward) * (1.0 / math.sqrt(2.0 * math.pi))
    activated_low = (upward * cdf).astype(LOW)
    slope = cdf + upward * pdf
    mixed = hidden + product_group(activated_low, down_part, 1, 1)
    normal_two, inverse_two = norm_forward(mixed)
    layer_out = (normal_two * gain_two + bias_two).astype(LOW)

    grad_mixed, gain_two_grad, bias_two_grad = norm_backward(
        cotangent[0].astype(FULL), normal_two, inverse_two, gain_two
    )
    grad_mixed_low = gather_group(grad_mixed.astype(LOW))
    grad_upward_low = (dot(grad_mixed_low, down_part, 1, 0) * slope).astype(LOW)
    grad_hidden = grad_mixed + product_group(grad_upward_low, up_part, 1, 1)
    ff_terms = jnp.concatenate(
        [dot(hidden_low, grad_upward_low, 0, 0), dot(grad_mixed_low, activated_low, 0, 0)], axis=1
    ).astype(LOW)
    ff_share = lax.psum_scatter(ff_terms, FSDP, scatter_dimension=0, tiled=True)

    grad_residual, gain_one_grad, bias_one_grad = norm_backward(
        grad_hidden, normal_one, inverse_one, gain_one
    )
    grad_residual_low = grad_residual.astype(LOW)
    grad_attended = dot(full_out, grad_residual_low, 1, 1).astype(LOW)
    grad_blocks = lax.all_to_all(
        grad_attended.reshape(4, 2, 2, HEAD_DIM, BLOCK)
        .transpose(0, 2, 1, 3, 4)
        .reshape(HEADS, HEAD_DIM, BLOCK),
        CTX,
        split_axis=0,
        concat_axis=0,
        tiled=True,
    )

    attended_group = gather_group(attended_low.reshape(1, width, BLOCK))
    residual_group = gather_group(grad_residual_low)
    residual_part = lax.dynamic_slice_in_dim(residual_group, group * out_part, out_part, 1)
    out_terms = sum(
        dot(attended_group[i], residual_part[i * BLOCK : (i + 1) * BLOCK], 1, 0) for i in range(4)
    )
    norm_terms = jnp.stack([gain_one_grad, bias_one_grad, gain_two_grad, bias_two_grad], axis=1)
    out_terms = jnp.concatenate(
        [out_terms.astype(LOW), jnp.pad(norm_terms.astype(LOW), ((0, 0), (0, BLOCK - 4)))], axis=1
    )
    out_share = lax.all_to_all(
        out_terms.reshape(8, BLOCK, -1), FSDP, split_axis=0, concat_axis=0, tiled=True
    )
    out_share = jnp.sum(out_share.astype(FULL), axis=0)

    dq, dk, dv = attention_backward(place, head, grad_blocks, attended, log_total)
    grad_head = jnp.stack([dq, dk, dv])
    mine = grad_head[:, :, : 8 * BLOCK]
    theirs = swap(grad_head[:, :, 8 * BLOCK :].reshape(3 * HEAD_DIM, -1), "xh").reshape(mine.shape)
    grad_projected = jnp.stack(
        [jnp.where(xh == 0, mine, theirs), jnp.where(xh == 0, theirs, mine)], axis=1
    ).reshape(3 * BLOCK, 8 * BLOCK)
    qkv_terms = dot(near, grad_projected, 0, 1).astype(LOW)
    half = 4 * BLOCK
    theirs = swap(dot(grad_projected[:, half:], qkv_part, 0, 1).astype(LOW), "core")
    input_near = dot(grad_projected[:, :half], qkv_part, 0, 1) + theirs.astype(FULL)
    input_grad = grad_residual + input_near[:BLOCK]
    for mask in (1, 3, 2):
        sent = input_near[mask * BLOCK : (mask + 1) * BLOCK].astype(LOW)
        input_grad = input_grad + exchange(sent, Z, mask).astype(FULL)

    late = ("zh", "xh")
    me = zh * 2 + xh
    ff_share = jnp.concatenate([ff_share, out_share.astype(LOW)], axis=1)
    ff_share = ff_share.reshape(4, BLOCK // 4, -1)
    ff_sum = lax.dynamic_index_in_dim(ff_share, me, 0, keepdims=False).astype(FULL)
    for mask in (1, 2, 3):
        sent = lax.dynamic_index_in_dim(ff_share, me ^ mask, 0, keepdims=False)
        ff_sum = ff_sum + exchange(sent, late, mask).astype(FULL)
    ff_own = with_four(ff_sum.astype(LOW), late)
    ff_zl = swap(ff_own, "zl")
    ff_core = swap(ff_own, "core")
    ff_both = swap(ff_zl, "core")
    spots = [me ^ m for m in range(4)] + [
        (zl ^ dl) * 2 + (core ^ dc) for dl, dc in ((0, 0), (1, 0), (0, 1), (1, 1))
    ]
    grad_w_up, grad_w_down, grad_w_out, norm_grads = assemble(
        jnp.stack(spots).astype(jnp.int32), [ff_own, ff_zl, ff_core, ff_both], width, units
    )

    qkv_share = lax.all_to_all(
        qkv_terms.reshape(16, BLOCK // 2, -1), ("xl", "y", "xh"), split_axis=0, concat_axis=0, tiled=True
    )
    qkv_share = jnp.sum(qkv_share.astype(FULL), axis=0).astype(LOW)
    qkv_own = with_four(with_pair(qkv_share, "xh"), Z)
    qkv_pair = swap(qkv_own, "core")
    spots = [xh, 1 - xh] + [(z ^ dz) * 2 + (core ^ dc) for dc in range(2) for dz in range(4)]
    grad_w_qkv = assemble_qkv(jnp.stack(spots).astype(jnp.int32), qkv_own, qkv_pair, width)

    return (
        layer_out[None],
        input_grad[None],
        grad_w_qkv,
        grad_w_out,
        grad_w_up,
        grad_w_down,
        norm_grads[0],
        norm_grads[1],
        norm_grads[2],
        norm_grads[3],
    )


def solution(mesh):
    fine = Mesh(mesh.devices.reshape(2, 2, 2, 2, 2, 4), ("zh", "zl", "xh", "core", "xl", "y"))
    block = P(FSDP, CTX, None)
    rows = P(FSDP, None)
    row = P(FSDP)
    return jax.shard_map(
        per_device,
        mesh=fine,
        in_specs=(block, rows, rows, rows, rows, row, row, row, row, block),
        out_specs=(block, block, rows, rows, rows, rows, row, row, row, row),
        check_vma=False,
    )
```

time: 1730 us -> 328 us (0.19)
  waiting for transfers between devices: 1300 us -> 121 us
  blocking collectives: 93.8 us -> 13.7 us
  matrix products: 110 us -> 33.2 us
  other arithmetic: 93.6 us -> 21.7 us
  local copies, waits for them, and re-layouts: 66.5 us -> 27.4 us
  Pallas kernels: 0 us -> 28.5 us
  starting transfers between devices: 48.1 us -> 65.9 us
    reduce_scatter x1 -> x0, waiting for transfers between devices: 748 us -> none  [per_device(): lax.psum_scatter(jnp.concatenate(products, axis=1), ('ctx', 'fsdp'), scat...]
    all_gather x7 -> x1, waiting for transfers between devices: 350 us -> 0.02 us  [per_device(): lax.all_gather(jnp.concatenate([w_out, up_mine, down_mine, norm_rows], ax...]
    ppermute x32 -> x36, waiting for transfers between devices: 203 us -> 92 us  [the longest x21 55.5 us: swap(): return lax.ppermute(value, axis, [(0, 1), (1, 0)])]
    psum x1 -> x0, blocking collectives: 81.2 us -> none  [per_device(): norm_total = lax.psum(norm_partial, ('ctx', 'fsdp'))]
    dot_general x96 -> x18, matrix products: 110 us -> 33.2 us  [dot(): lax.dot_general(left, right, (((left_dim,), (right_dim,)), ((), ())), pre...]
    convert_element_type x36 -> x4, other arithmetic: 52.5 us -> 2.51 us  [the longest x1 1.09 us: per_device(): ff_own = with_four(ff_sum.astype(LOW), late)]
    all_to_all x0 -> x4, waiting for transfers between devices: none -> 29.1 us  [the longest x1 16.3 us: per_device(): lax.all_to_all(jnp.broadcast_to(qkv_mine[None], (8,) + qkv_mine.shape), F...]
    pallas_call x0 -> x4, Pallas kernels: none -> 28.5 us  [the longest x1 12.7 us: attention_backward(): pl.pallas_call(backward_kernel, grid_spec=pltpu.PrefetchScalarGridSpec(nu...]
  transfers between devices with their start and end apart: 40 -> 42, of which waited for: 29 -> 24; matrix products, arithmetic and copies ran while one was open for 5% -> 17% of each run, Pallas kernels for 0% -> 8%
where the time goes in v1:
time: 328 us; the launch traced here: 326 us
  waiting for transfers between devices  121 us (37%)
  starting transfers between devices  65.9 us (20%)
  matrix products  33.2 us (10%)
  Pallas kernels  28.5 us (9%)
  local copies, waits for them, and re-layouts  27.4 us (8%)
  other arithmetic  21.7 us (7%)
  between operations  14.6 us (4%)
  blocking collectives  13.7 us (4%)
    ppermute x21, waiting for transfers between devices, swap(): return lax.ppermute(value, axis, [(0, 1), (1, 0)])  55.5 us
    ppermute x15, waiting for transfers between devices, exchange(): return lax.ppermute(value, axes, [(i, i ^ mask) for i in range(4)])  36.5 us
    dot_general x18, matrix products, dot(): lax.dot_general(left, right, (((left_dim,), (right_dim,)), ((), ())), pre...  33.2 us
    ppermute x21, starting transfers between devices, swap(): return lax.ppermute(value, axis, [(0, 1), (1, 0)])  23.5 us
    ppermute x15, starting transfers between devices, exchange(): return lax.ppermute(value, axes, [(i, i ^ mask) for i in range(4)])  20.9 us
    all_to_all x1, waiting for transfers between devices, per_device(): lax.all_to_all(jnp.broadcast_to(qkv_mine[None], (8,) + qkv_mine.shape), F...  16.3 us
    unnamed x41, local copies, waits for them, and re-layouts  15.5 us
    all_to_all x1, blocking collectives, per_device(): lax.all_to_all(low_blocks, CTX, split_axis=0, concat_axis=0, tiled=True)  13.7 us
  transfers between devices with their start and end apart: 42, of which 24 were waited for; matrix products, arithmetic and copies ran while one was open for 17% of the time, Pallas kernels for 8%

profile of v1, /device:TPU:1, one launch (start us, length us, event | category | flops | bytes accessed | tf_op | source)
XLA Modules:
  0.0 326.2 jit_solution(17074412839963675297)
XLA Ops:
  9.2 1.9 fusion.36
  11.1 2.5 collective-permute-start
  13.7 3.3 %collective-permute-start.1 = (bf16[128,1024]{1,0:T(8,128)(2,1)S(1)}, bf16[128,1024]{1,0:T(8,128)(2,1)S(1)}, u32[]{:S(2)}, u32[]{:S(2)}) collective-permute-start(bf16[128,1024]{1,0:T(8,128)(2,1)S(1)} %bitcast.147), channel_id=1, source_target_pairs={{0,64},{32,96},{64,0},{96,32},{1,65},{33,97},{65,1},{97,33},{2,66}... | collective-permute-start | bytes 786440 | tf_op jit(solution)/shard_map/ppermute | solution.py:36
  17.0 2.7 collective-permute-done
  19.7 8.8 %collective-permute-done.1 = bf16[128,1024]{1,0:T(8,128)(2,1)S(1)} collective-permute-done((bf16[128,1024]{1,0:T(8,128)(2,1)S(1)}, bf16[128,1024]{1,0:T(8,128)(2,1)S(1)}, u32[]{:S(2)}, u32[]{:S(2)}) %collective-permute-start.1) | collective-permute-done | bytes 262176 | tf_op jit(solution)/shard_map/ppermute | solution.py:36
  28.5 2.0 collective-permute-done.2
  30.5 2.1 collective-permute-start.3
  34.5 5.1 %all-to-all-start = ((bf16[8,128,384]{2,1,0:T(8,128)(2,1)}), bf16[8,128,384]{2,1,0:T(8,128)(2,1)S(1)}, u32[]{:S(2)}, u32[]{:S(2)}) async-start(bf16[8,128,384]{2,1,0:T(8,128)(2,1)} %broadcast_in_dim.6), calls=%async_computation | async-start | bytes 1572864 | tf_op jit(solution)/shard_map/all_to_all | solution.py:303
  41.1 1.7 constant_dynamic-update-slice_fusion.2
  42.7 1.7 constant_dynamic-update-slice_fusion.1
  45.5 16.3 %all-to-all-done = bf16[8,128,384]{2,1,0:T(8,128)(2,1)S(1)} async-done(((bf16[8,128,384]{2,1,0:T(8,128)(2,1)}), bf16[8,128,384]{2,1,0:T(8,128)(2,1)S(1)}, u32[]{:S(2)}, u32[]{:S(2)}) %all-to-all-start) | async-done | bytes 786464 | tf_op jit(solution)/shard_map/all_to_all | solution.py:303
  61.7 2.9 convolution_convert_fusion.4
  64.7 2.5 collective-permute-start.4
  67.4 18.3 %collective-permute-done.4 = bf16[192,1024]{1,0:T(8,128)(2,1)S(1)} collective-permute-done((bf16[192,1024]{1,0:T(8,128)(2,1)S(1)}, bf16[192,1024]{1,0:T(8,128)(2,1)S(1)}, u32[]{:S(2)}, u32[]{:S(2)}) %collective-permute-start.4) | collective-permute-done | bytes 393248 | tf_op jit(solution)/shard_map/ppermute | solution.py:32
  85.7 10.9 %attention_forward.1 = (bf16[16,64,128]{2,1,0:T(8,128)(2,1)S(1)}, f32[64,2048]{1,0:T(8,128)S(1)}, f32[1,2048]{1,0:T(1,128)S(1)}) custom-call(s32[16]{0:T(128)S(1)} %stack.183.place, bf16[192,2048]{1,0:T(8,128)(2,1)S(1)} %pad_maximum_fusion.4.q_ref.k_ref.v_ref, bf16[192,2048]{1,0:T(8,128)(2,1)S(1)} %pad_maximum_fusion.4.q_ref.k_ref.v_ref, ...), custom_call_target="tpu_custom_call" | custom-call | flops 4294967296 | bytes 1310720 | tf_op jit(solution)/shard_map/attention_forward/pallas_call | solution.py:70
  96.6 13.7 %all_to_all.25 = bf16[16,64,128]{2,1,0:T(8,128)(2,1)S(1)} all-to-all(bf16[16,64,128]{2,1,0:T(8,128)(2,1)S(1)} %get-tuple-element.20), channel_id=1, replica_groups=mesh['zh'=2,'zl'=2,'xh'=2,'core'=2,'xl'=2,'y'=4] {'zh','zl','xh','core'}, dimensions={0} | all-to-all | bytes 524288 | tf_op jit(solution)/shard_map/all_to_all | solution.py:323
  110.4 2.3 fusion.98
  115.6 6.5 %collective-permute-done.5 = bf16[128,1024]{1,0:T(8,128)(2,1)S(1)} collective-permute-done((bf16[128,1024]{1,0:T(8,128)(2,1)S(1)}, bf16[128,1024]{1,0:T(8,128)(2,1)S(1)}, u32[]{:S(2)}, u32[]{:S(2)}) %collective-permute-start.5) | collective-permute-done | bytes 262176 | tf_op jit(solution)/shard_map/ppermute | solution.py:32
  122.1 2.0 collective-permute-start.6
  130.9 7.2 %collective-permute-done.8 = bf16[128,1024]{1,0:T(8,128)(2,1)S(1)} collective-permute-done((bf16[128,1024]{1,0:T(8,128)(2,1)S(1)}, bf16[128,1024]{1,0:T(8,128)(2,1)S(1)}, u32[]{:S(2)}, u32[]{:S(2)}) %collective-permute-start.8) | collective-permute-done | bytes 262176 | tf_op jit(solution)/shard_map/ppermute | solution.py:32
  139.6 6.3 %collective-permute-done.9 = bf16[128,1024]{1,0:T(8,128)(2,1)S(1)} collective-permute-done((bf16[128,1024]{1,0:T(8,128)(2,1)S(1)}, bf16[128,1024]{1,0:T(8,128)(2,1)S(1)}, u32[]{:S(2)}, u32[]{:S(2)}) %collective-permute-start.9) | collective-permute-done | bytes 262176 | tf_op jit(solution)/shard_map/ppermute | solution.py:32
  146.0 2.4 collective-permute-start.10
  151.2 1.7 fusion.5
  155.1 2.5 pad_maximum_fusion
  157.6 6.5 %copy.40 = bf16[1024,2048]{1,0:T(8,128)(2,1)} copy(bf16[1024,2048]{0,1:T(8,128)(2,1)} %pad_maximum_fusion) | data formatting | bytes 8388608
  164.2 2.6 fusion.24
  167.2 1.5 collective-permute-done.11
  168.8 2.7 convert_add_fusion.1
  173.2 1.5 collective-permute-start.25
  174.8 6.2 %collective-permute-done.12 = bf16[128,1024]{1,0:T(8,128)(2,1)} collective-permute-done((bf16[128,1024]{1,0:T(8,128)(2,1)}, bf16[128,1024]{1,0:T(8,128)(2,1)}, u32[]{:S(2)}, u32[]{:S(2)}) %collective-permute-start.12) | collective-permute-done | bytes 262176 | tf_op jit(solution)/shard_map/ppermute | solution.py:32
  181.0 2.4 multiply_reduce_fusion
  184.4 2.3 fusion.33
  187.5 6.7 %all-to-all-start.2 = ((bf16[16,64,128]{2,1,0:T(8,128)(2,1)}), bf16[16,64,128]{2,1,0:T(8,128)(2,1)S(1)}, u32[]{:S(2)}, u32[]{:S(2)}) async-start(bf16[16,64,128]{2,1,0:T(8,128)(2,1)} %bitcast.33), calls=%async_computation.2 | async-start | bytes 524288 | tf_op jit(solution)/shard_map/all_to_all | solution.py:359
  194.2 1.8 pad_maximum_fusion.12
  197.5 8.5 %all-to-all-done.2.grad_ref = bf16[16,64,128]{2,1,0:T(8,128)(2,1)S(1)} async-done(((bf16[16,64,128]{2,1,0:T(8,128)(2,1)}), bf16[16,64,128]{2,1,0:T(8,128)(2,1)S(1)}, u32[]{:S(2)}, u32[]{:S(2)}) %all-to-all-start.2) | async-done | bytes 262176 | tf_op jit(solution)/shard_map/all_to_all | solution.py:359
  206.0 12.7 %attention_backward.1 = (bf16[64,2048]{1,0:T(8,128)(2,1)S(1)}, bf16[64,2048]{1,0:T(8,128)(2,1)S(1)}, bf16[64,2048]{1,0:T(8,128)(2,1)S(1)}) custom-call(s32[16]{0:T(128)S(1)} %stack.183.place, bf16[192,2048]{1,0:T(8,128)(2,1)S(1)} %pad_maximum_fusion.4.q_ref.k_ref.v_ref, bf16[192,2048]{1,0:T(8,128)(2,1)S(1)} %pad_maximum_fusion.4.q_ref.k_ref.v_ref, ...), custom_call_target="tpu_custom_call" | custom-call | flops 10737418240 | bytes 2621440 | tf_op jit(solution)/shard_map/attention_backward/pallas_call | solution.py:135
  225.7 3.5 %all-to-all-start.4 = ((bf16[8,128,384]{1,2,0:T(8,128)(2,1)}), bf16[8,128,384]{1,2,0:T(8,128)(2,1)S(1)}, u32[]{:S(2)}, u32[]{:S(2)}) async-start(bf16[8,128,384]{1,2,0:T(8,128)(2,1)} %copy_bitcast_fusion), calls=%async_computation.4 | async-start | bytes 1572864 | tf_op jit(solution)/shard_map/all_to_all | solution.py:379
  229.3 1.9 collective-permute-done.13
  232.4 4.1 %convolution_convert_fusion.3 = bf16[1024,384]{1,0:T(8,128)(2,1)} fusion(bf16[1024,1024]{1,0:T(8,128)(2,1)} %constant_dynamic-update-slice_fusion, bf16[384,1024]{1,0:T(8,128)(2,1)S(1)} %bitcast.141), kind=kOutput, calls=%fused_computation.31 | convolution fusion | flops 805699584 | bytes 3670016 | tf_op jit(solution)/shard_map/dot_general | solution.py:26
  236.5 4.3 %all-to-all-done.4 = bf16[8,128,384]{1,2,0:T(8,128)(2,1)S(1)} async-done(((bf16[8,128,384]{1,2,0:T(8,128)(2,1)}), bf16[8,128,384]{1,2,0:T(8,128)(2,1)S(1)}, u32[]{:S(2)}, u32[]{:S(2)}) %all-to-all-start.4) | async-done | bytes 786464 | tf_op jit(solution)/shard_map/all_to_all | solution.py:379
  240.8 6.1 %all-to-all-start.3 = ((bf16[16,64,384]{2,1,0:T(8,128)(2,1)}), bf16[16,64,384]{2,1,0:T(8,128)(2,1)S(1)}, u32[]{:S(2)}, u32[]{:S(2)}) async-start(bf16[16,64,384]{2,1,0:T(8,128)(2,1)} %bitcast.152), calls=%async_computation.3 | async-start | bytes 1572864 | tf_op jit(solution)/shard_map/all_to_all | solution.py:419
  247.0 2.0 copy.41
  251.3 1.8 dynamic-slice_bitcast_fusion.2
  253.0 3.1 collective-permute-start.29
  256.2 2.4 collective-permute-start.28
  258.7 1.7 convolution_convert_fusion.2
  260.4 2.0 collective-permute-start.14
  262.5 3.2 collective-permute-start.18
  267.8 2.1 collective-permute-start.32
  270.1 3.5 %collective-permute-start.30 = (bf16[32,2432]{1,0:T(8,128)(2,1)S(1)}, bf16[32,2432]{1,0:T(8,128)(2,1)S(1)}, u32[]{:S(2)}, u32[]{:S(2)}) collective-permute-start(bf16[32,2432]{1,0:T(8,128)(2,1)S(1)} %fusion.74), channel_id=1, source_target_pairs={{0,16},{16,0},{64,80},{80,64},{1,17},{17,1},{65,81},{81,65},{2,18}... | collective-permute-start | bytes 466952 | tf_op jit(solution)/shard_map/ppermute | solution.py:36
  273.7 3.1 collective-permute-done.32
  277.0 3.4 %collective-permute-done.31 = bf16[32,2432]{1,0:T(8,128)(2,1)S(1)} collective-permute-done((bf16[32,2432]{1,0:T(8,128)(2,1)S(1)}, bf16[32,2432]{1,0:T(8,128)(2,1)S(1)}, u32[]{:S(2)}, u32[]{:S(2)}) %collective-permute-start.31) | collective-permute-done | bytes 155680 | tf_op jit(solution)/shard_map/ppermute | solution.py:36
  280.6 3.5 %collective-permute-done.20 = bf16[128,384]{1,0:T(8,128)(2,1)S(1)} collective-permute-done((bf16[128,384]{1,0:T(8,128)(2,1)S(1)}, bf16[128,384]{1,0:T(8,128)(2,1)S(1)}, u32[]{:S(2)}, u32[]{:S(2)}) %collective-permute-start.20) | collective-permute-done | bytes 98336 | tf_op jit(solution)/shard_map/ppermute | solution.py:36
  284.1 1.8 collective-permute-done.21
  285.9 1.8 collective-permute-start.22
  287.7 3.3 %fusion.99 = (bf16[512,1024]{1,0:T(8,128)(2,1)S(1)}, f32[512,1024]{1,0:T(8,128)}) fusion(bf16[512,1024]{1,0:T(8,128)(2,1)} %collective-permute-done.14, bf16[1024,384]{1,0:T(8,128)(2,1)S(1)} %bitcast.136, bf16[384,1024]{1,0:T(8,128)(2,1)S(1)} %bitcast.143), kind=kOutput, calls=%fused_computation.174 | convolution fusion | flops 404226048 | bytes 5373952 | tf_op jit(solution)/shard_map/dot_general | solution.py:26
  291.0 2.8 collective-permute-done.33.refs_1_
  293.9 3.2 collective-permute-start.35
  298.0 2.3 collective-permute-start.17
  301.5 1.9 assemble_qkv.1
  303.4 4.3 %collective-permute-done.17 = bf16[128,1024]{1,0:T(8,128)(2,1)S(1)} collective-permute-done((bf16[128,1024]{1,0:T(8,128)(2,1)}, bf16[128,1024]{1,0:T(8,128)(2,1)S(1)}, u32[]{:S(2)}, u32[]{:S(2)}) %collective-permute-start.17) | collective-permute-done | bytes 262176 | tf_op jit(solution)/shard_map/ppermute | solution.py:36
  307.7 6.0 %collective-permute-done.16 = bf16[128,1024]{1,0:T(8,128)(2,1)} collective-permute-done((bf16[128,1024]{1,0:T(8,128)(2,1)}, bf16[128,1024]{1,0:T(8,128)(2,1)}, u32[]{:S(2)}, u32[]{:S(2)}) %collective-permute-start.16) | collective-permute-done | bytes 262176 | tf_op jit(solution)/shard_map/ppermute | solution.py:36
  313.7 2.2 fusion.51
  315.8 3.0 assemble.1
  (151 shorter events, 44.4 us)
Async XLA Ops:
  7.2 3.9 %copy-start.7 = (bf16[1,128,1024]{2,1,0:T(8,128)(2,1)S(1)}, bf16[1,128,1024]{2,1,0:T(8,128)(2,1)}, u32[]{:S(2)}) copy-start(bf16[1,128,1024]{2,1,0:T(8,128)(2,1)} %param.10) | copy-start | bytes 786436
  7.2 103.2 %all-gather.2.cloned.1.call-start = ((), (), s32[]{:S(2)}) async-start(), calls=%async_computation.6 | async-start | bytes 7372800 | tf_op jit(solution)/shard_map/all_gather | solution.py:293
  11.1 8.6 %collective-permute-start = (bf16[128,1024]{1,0:T(8,128)(2,1)S(1)}, bf16[128,1024]{1,0:T(8,128)(2,1)S(1)}, u32[]{:S(2)}, u32[]{:S(2)}) collective-permute-start(bf16[128,1024]{1,0:T(8,128)(2,1)S(1)} %bitcast.146), channel_id=1, source_target_pairs={{0,32},{32,0},{64,96},{96,64},{1,33},{33,1},{65,97},{97,65},{2,34}... | collective-permute-start | bytes 786440 | tf_op jit(solution)/shard_map/ppermute | solution.py:36
  13.7 14.8 %collective-permute-start.1 = (bf16[128,1024]{1,0:T(8,128)(2,1)S(1)}, bf16[128,1024]{1,0:T(8,128)(2,1)S(1)}, u32[]{:S(2)}, u32[]{:S(2)}) collective-permute-start(bf16[128,1024]{1,0:T(8,128)(2,1)S(1)} %bitcast.147), channel_id=1, source_target_pairs={{0,64},{32,96},{64,0},{96,32},{1,65},{33,97},{65,1},{97,33},{2,66}... | collective-permute-start | bytes 786440 | tf_op jit(solution)/shard_map/ppermute | solution.py:36
  17.0 13.5 %collective-permute-start.2 = (bf16[128,1024]{1,0:T(8,128)(2,1)S(1)}, bf16[128,1024]{1,0:T(8,128)(2,1)S(1)}, u32[]{:S(2)}, u32[]{:S(2)}) collective-permute-start(bf16[128,1024]{1,0:T(8,128)(2,1)S(1)} %bitcast.148), channel_id=1, source_target_pairs={{0,96},{32,64},{64,32},{96,0},{1,97},{33,65},{65,33},{97,1},{2,98}... | collective-permute-start | bytes 786440 | tf_op jit(solution)/shard_map/ppermute | solution.py:36
  28.5 6.0 %copy-start.9 = (bf16[128,1024]{1,0:T(8,128)(2,1)}, bf16[128,1024]{1,0:T(8,128)(2,1)S(1)}, u32[]{:S(2)}) copy-start(bf16[128,1024]{1,0:T(8,128)(2,1)S(1)} %collective-permute-done.1) | copy-start | bytes 786436
  30.5 4.0 %copy-start.10 = (bf16[128,1024]{1,0:T(8,128)(2,1)}, bf16[128,1024]{1,0:T(8,128)(2,1)S(1)}, u32[]{:S(2)}) copy-start(bf16[128,1024]{1,0:T(8,128)(2,1)S(1)} %collective-permute-done.2) | copy-start | bytes 786436
  30.5 13.9 %collective-permute-start.3 = (bf16[512,1024]{1,0:T(8,128)(2,1)S(1)}, bf16[512,1024]{1,0:T(8,128)(2,1)S(1)}, u32[]{:S(2)}, u32[]{:S(2)}) collective-permute-start(bf16[512,1024]{1,0:T(8,128)(2,1)S(1)} %pad_maximum_fusion.1), channel_id=1, source_target_pairs={{0,8},{8,0},{1,9},{9,1},{2,10},{10,2},{3,11},{11,3},{4,12},{12,4},... | collective-permute-start | bytes 3145736 | tf_op jit(solution)/shard_map/ppermute | solution.py:32
  34.5 27.3 %all-to-all-start = ((bf16[8,128,384]{2,1,0:T(8,128)(2,1)}), bf16[8,128,384]{2,1,0:T(8,128)(2,1)S(1)}, u32[]{:S(2)}, u32[]{:S(2)}) async-start(bf16[8,128,384]{2,1,0:T(8,128)(2,1)} %broadcast_in_dim.6), calls=%async_computation | async-start | bytes 1572864 | tf_op jit(solution)/shard_map/all_to_all | solution.py:303
  39.6 207.5 %reduce-scatter.4.cloned.1.call-start = ((), (), s32[]{:S(2)}) async-start(), calls=%async_computation.7 | async-start | bytes 4718592
  61.7 196.9 %copy-start = (bf16[8,128,384]{2,1,0:T(8,128)(2,1)}, bf16[8,128,384]{2,1,0:T(8,128)(2,1)S(1)}, u32[]{:S(2)}) copy-start(bf16[8,128,384]{2,1,0:T(8,128)(2,1)S(1)} %all-to-all-done) | copy-start | bytes 2359300
  64.7 20.9 %collective-permute-start.4 = (bf16[192,1024]{1,0:T(8,128)(2,1)S(1)}, bf16[192,1024]{1,0:T(8,128)(2,1)S(1)}, u32[]{:S(2)}, u32[]{:S(2)}) collective-permute-start(bf16[192,1024]{1,0:T(8,128)(2,1)S(1)} %bitcast.154), channel_id=1, source_target_pairs={{0,16},{16,0},{1,17},{17,1},{2,18},{18,2},{3,19},{19,3},{4,20},{20... | collective-permute-start | bytes 1179656 | tf_op jit(solution)/shard_map/ppermute | solution.py:32
  110.4 3.6 %copy-start.3 = (bf16[4,2,2,64,128]{4,3,1,2,0:T(8,128)(2,1)}, bf16[4,2,2,64,128]{4,3,1,2,0:T(8,128)(2,1)S(1)}, u32[]{:S(2)}) copy-start(bf16[4,2,2,64,128]{4,3,1,2,0:T(8,128)(2,1)S(1)} %copy.34) | copy-start | bytes 786436
  110.4 15.3 %copy-start.11 = (bf16[1024,3200]{1,0:T(8,128)(2,1)S(1)}, bf16[1024,3200]{1,0:T(8,128)(2,1)}, u32[]{:S(2)}) copy-start(bf16[1024,3200]{1,0:T(8,128)(2,1)} %all-gather.2.cloned.1.call-done) | copy-start | bytes 19660804
  115.2 6.9 %collective-permute-start.5 = (bf16[128,1024]{1,0:T(8,128)(2,1)S(1)}, bf16[128,1024]{1,0:T(8,128)(2,1)S(1)}, u32[]{:S(2)}, u32[]{:S(2)}) collective-permute-start(bf16[128,1024]{1,0:T(8,128)(2,1)S(1)} %fusion.66), channel_id=1, source_target_pairs={{0,32},{32,0},{1,33},{33,1},{2,34},{34,2},{3,35},{35,3},{4,36},{36... | collective-permute-start | bytes 786440 | tf_op jit(solution)/shard_map/ppermute | solution.py:32
  122.1 3.5 %collective-permute-start.6 = (bf16[256,1024]{1,0:T(8,128)(2,1)S(1)}, bf16[256,1024]{1,0:T(8,128)(2,1)S(1)}, u32[]{:S(2)}, u32[]{:S(2)}) collective-permute-start(bf16[256,1024]{1,0:T(8,128)(2,1)S(1)} %pad_maximum_fusion.9), channel_id=1, source_target_pairs={{0,8},{8,0},{1,9},{9,1},{2,10},{10,2},{3,11},{11,3},{4,12},{12,4},... | collective-permute-start | bytes 1572872 | tf_op jit(solution)/shard_map/ppermute | solution.py:32
  127.8 2.0 collective-permute-start.7
  130.5 8.2 %copy-start.2 = (bf16[1,128,1024]{2,1,0:T(8,128)(2,1)S(1)}, bf16[1,128,1024]{2,1,0:T(8,128)(2,1)}, u32[]{:S(2)}) copy-start(bf16[1,128,1024]{2,1,0:T(8,128)(2,1)} %param.19) | copy-start | bytes 786436
  130.6 7.6 %collective-permute-start.8 = (bf16[128,1024]{1,0:T(8,128)(2,1)S(1)}, bf16[128,1024]{1,0:T(8,128)(2,1)S(1)}, u32[]{:S(2)}, u32[]{:S(2)}) collective-permute-start(bf16[128,1024]{1,0:T(8,128)(2,1)S(1)} %slice.258), channel_id=1, source_target_pairs={{0,32},{32,0},{1,33},{33,1},{2,34},{34,2},{3,35},{35,3},{4,36},{36... | collective-permute-start | bytes 786440 | tf_op jit(solution)/shard_map/ppermute | solution.py:32
  139.2 6.7 %collective-permute-start.9 = (bf16[128,1024]{1,0:T(8,128)(2,1)S(1)}, bf16[128,1024]{1,0:T(8,128)(2,1)S(1)}, u32[]{:S(2)}, u32[]{:S(2)}) collective-permute-start(bf16[128,1024]{1,0:T(8,128)(2,1)S(1)} %fusion.92), channel_id=1, source_target_pairs={{0,32},{32,0},{1,33},{33,1},{2,34},{34,2},{3,35},{35,3},{4,36},{36... | collective-permute-start | bytes 786440 | tf_op jit(solution)/shard_map/ppermute | solution.py:32
  146.0 3.9 %collective-permute-start.10 = (bf16[256,1024]{1,0:T(8,128)(2,1)S(1)}, bf16[256,1024]{1,0:T(8,128)(2,1)S(1)}, u32[]{:S(2)}, u32[]{:S(2)}) collective-permute-start(bf16[256,1024]{1,0:T(8,128)(2,1)S(1)} %pad_maximum_fusion.10), channel_id=1, source_target_pairs={{0,8},{8,0},{1,9},{9,1},{2,10},{10,2},{3,11},{11,3},{4,12},{12,4},... | collective-permute-start | bytes 1572872 | tf_op jit(solution)/shard_map/ppermute | solution.py:32
  152.9 1.0 copy-start.13
  164.2 4.6 %copy-start.14 = (bf16[512,1024]{1,0:T(8,128)(2,1)S(1)}, bf16[512,1024]{1,0:T(8,128)(2,1)}, u32[]{:S(2)}) copy-start(bf16[512,1024]{1,0:T(8,128)(2,1)} %copy-done.13) | copy-start | bytes 3145732
  166.8 2.0 collective-permute-start.11
  171.4 1.0 copy-start.12
  173.1 7.8 %collective-permute-start.12 = (bf16[128,1024]{1,0:T(8,128)(2,1)}, bf16[128,1024]{1,0:T(8,128)(2,1)}, u32[]{:S(2)}, u32[]{:S(2)}) collective-permute-start(bf16[128,1024]{1,0:T(8,128)(2,1)} %slice.257), channel_id=1, source_target_pairs={{0,32},{32,0},{1,33},{33,1},{2,34},{34,2},{3,35},{35,3},{4,36},{36... | collective-permute-start | bytes 786440 | tf_op jit(solution)/shard_map/ppermute | solution.py:32
  173.2 21.0 %collective-permute-start.25 = (bf16[1,1024,128]{2,1,0:T(8,128)(2,1)}, bf16[1,1024,128]{2,1,0:T(8,128)(2,1)}, u32[]{:S(2)}, u32[]{:S(2)}) collective-permute-start(bf16[1,1024,128]{2,1,0:T(8,128)(2,1)} %bitcast.138), channel_id=1, source_target_pairs={{0,32},{32,0},{1,33},{33,1},{2,34},{34,2},{3,35},{35,3},{4,36},{36... | collective-permute-start | bytes 786440 | tf_op jit(solution)/shard_map/ppermute | solution.py:32
  184.4 9.9 %copy-start.4 = (bf16[4,2,2,64,128]{4,3,1,2,0:T(8,128)(2,1)S(1)}, bf16[4,2,2,64,128]{4,3,1,2,0:T(8,128)(2,1)}, u32[]{:S(2)}) copy-start(bf16[4,2,2,64,128]{4,3,1,2,0:T(8,128)(2,1)} %copy-done.3) | copy-start | bytes 786436
  184.4 11.8 %collective-permute-start.23 = (bf16[128,1024]{1,0:T(8,128)(2,1)S(1)}, bf16[128,1024]{1,0:T(8,128)(2,1)S(1)}, u32[]{:S(2)}, u32[]{:S(2)}) collective-permute-start(bf16[128,1024]{1,0:T(8,128)(2,1)S(1)} %get-tuple-element.41), channel_id=1, source_target_pairs={{0,32},{32,0},{1,33},{33,1},{2,34},{34,2},{3,35},{35,3},{4,36},{36... | collective-permute-start | bytes 786440 | tf_op jit(solution)/shard_map/ppermute | solution.py:32
  187.5 18.5 %all-to-all-start.2 = ((bf16[16,64,128]{2,1,0:T(8,128)(2,1)}), bf16[16,64,128]{2,1,0:T(8,128)(2,1)S(1)}, u32[]{:S(2)}, u32[]{:S(2)}) async-start(bf16[16,64,128]{2,1,0:T(8,128)(2,1)} %bitcast.33), calls=%async_computation.2 | async-start | bytes 524288 | tf_op jit(solution)/shard_map/all_to_all | solution.py:359
  196.0 25.7 %collective-permute-start.26 = (bf16[2,1024,128]{2,1,0:T(8,128)(2,1)}, bf16[2,1024,128]{2,1,0:T(8,128)(2,1)}, u32[]{:S(2)}, u32[]{:S(2)}) collective-permute-start(bf16[2,1024,128]{2,1,0:T(8,128)(2,1)} %pad_maximum_fusion.12), channel_id=1, source_target_pairs={{0,8},{8,0},{1,9},{9,1},{2,10},{10,2},{3,11},{11,3},{4,12},{12,4},... | collective-permute-start | bytes 1572872 | tf_op jit(solution)/shard_map/ppermute | solution.py:32
  197.1 22.5 %collective-permute-start.24 = (bf16[256,1024]{1,0:T(8,128)(2,1)}, bf16[256,1024]{1,0:T(8,128)(2,1)}, u32[]{:S(2)}, u32[]{:S(2)}) collective-permute-start(bf16[256,1024]{1,0:T(8,128)(2,1)} %pad_maximum_fusion.11), channel_id=1, source_target_pairs={{0,8},{8,0},{1,9},{9,1},{2,10},{10,2},{3,11},{11,3},{4,12},{12,4},... | collective-permute-start | bytes 1572872 | tf_op jit(solution)/shard_map/ppermute | solution.py:32
  219.6 11.7 %collective-permute-start.13 = (bf16[192,1024]{1,0:T(8,128)(2,1)}, bf16[192,1024]{1,0:T(8,128)(2,1)}, u32[]{:S(2)}, u32[]{:S(2)}) collective-permute-start(bf16[192,1024]{1,0:T(8,128)(2,1)} %bitcast.37), channel_id=1, source_target_pairs={{0,16},{16,0},{1,17},{17,1},{2,18},{18,2},{3,19},{19,3},{4,20},{20... | collective-permute-start | bytes 1179656 | tf_op jit(solution)/shard_map/ppermute | solution.py:32
  225.7 15.1 %all-to-all-start.4 = ((bf16[8,128,384]{1,2,0:T(8,128)(2,1)}), bf16[8,128,384]{1,2,0:T(8,128)(2,1)S(1)}, u32[]{:S(2)}, u32[]{:S(2)}) async-start(bf16[8,128,384]{1,2,0:T(8,128)(2,1)} %copy_bitcast_fusion), calls=%async_computation.4 | async-start | bytes 1572864 | tf_op jit(solution)/shard_map/all_to_all | solution.py:379
  232.4 26.3 %copy-start.5 = (bf16[3,2,64,1024]{3,2,1,0:T(8,128)(2,1)}, bf16[3,2,64,1024]{3,2,1,0:T(8,128)(2,1)S(1)}, u32[]{:S(2)}) copy-start(bf16[3,2,64,1024]{3,2,1,0:T(8,128)(2,1)S(1)} %copy.37) | copy-start | bytes 2359300
  240.8 21.6 %all-to-all-start.3 = ((bf16[16,64,384]{2,1,0:T(8,128)(2,1)}), bf16[16,64,384]{2,1,0:T(8,128)(2,1)S(1)}, u32[]{:S(2)}, u32[]{:S(2)}) async-start(bf16[16,64,384]{2,1,0:T(8,128)(2,1)} %bitcast.152), calls=%async_computation.3 | async-start | bytes 1572864 | tf_op jit(solution)/shard_map/all_to_all | solution.py:419
  253.0 12.7 %collective-permute-start.29 = (bf16[32,2432]{1,0:T(8,128)(2,1)}, bf16[32,2432]{1,0:T(8,128)(2,1)S(1)}, u32[]{:S(2)}, u32[]{:S(2)}) collective-permute-start(bf16[32,2432]{1,0:T(8,128)(2,1)} %get-tuple-element.57), channel_id=1, source_target_pairs={{0,80},{16,64},{64,16},{80,0},{1,81},{17,65},{65,17},{81,1},{2,82}... | collective-permute-start | bytes 466952 | tf_op jit(solution)/shard_map/ppermute | solution.py:36
  256.2 10.6 %collective-permute-start.28 = (bf16[32,2432]{1,0:T(8,128)(2,1)S(1)}, bf16[32,2432]{1,0:T(8,128)(2,1)S(1)}, u32[]{:S(2)}, u32[]{:S(2)}) collective-permute-start(bf16[32,2432]{1,0:T(8,128)(2,1)S(1)} %get-tuple-element.58), channel_id=1, source_target_pairs={{0,64},{16,80},{64,0},{80,16},{1,65},{17,81},{65,1},{81,17},{2,66}... | collective-permute-start | bytes 466952 | tf_op jit(solution)/shard_map/ppermute | solution.py:36
  258.6 8.2 %collective-permute-start.27 = (bf16[32,2432]{1,0:T(8,128)(2,1)S(1)}, bf16[32,2432]{1,0:T(8,128)(2,1)}, u32[]{:S(2)}, u32[]{:S(2)}) collective-permute-start(bf16[32,2432]{1,0:T(8,128)(2,1)S(1)} %get-tuple-element.56), channel_id=1, source_target_pairs={{0,16},{16,0},{64,80},{80,64},{1,17},{17,1},{65,81},{81,65},{2,18}... | collective-permute-start | bytes 466952 | tf_op jit(solution)/shard_map/ppermute | solution.py:36
  260.4 27.3 %copy-start.1 = (bf16[8,128,384]{2,1,0:T(8,128)(2,1)S(1)}, bf16[8,128,384]{2,1,0:T(8,128)(2,1)}, u32[]{:S(2)}) copy-start(bf16[8,128,384]{2,1,0:T(8,128)(2,1)} %copy-done) | copy-start | bytes 2359300
  260.4 27.3 %collective-permute-start.14 = (bf16[512,1024]{1,0:T(8,128)(2,1)}, bf16[512,1024]{1,0:T(8,128)(2,1)}, u32[]{:S(2)}, u32[]{:S(2)}) collective-permute-start(bf16[512,1024]{1,0:T(8,128)(2,1)} %convolution_convert_fusion.2), channel_id=1, source_target_pairs={{0,8},{8,0},{1,9},{9,1},{2,10},{10,2},{3,11},{11,3},{4,12},{12,4},... | collective-permute-start | bytes 3145736 | tf_op jit(solution)/shard_map/ppermute | solution.py:32
  262.5 25.2 %copy-start.6 = (bf16[3,2,64,1024]{3,2,1,0:T(8,128)(2,1)S(1)}, bf16[3,2,64,1024]{3,2,1,0:T(8,128)(2,1)}, u32[]{:S(2)}) copy-start(bf16[3,2,64,1024]{3,2,1,0:T(8,128)(2,1)} %copy-done.5) | copy-start | bytes 2359300
  262.5 11.1 %collective-permute-start.18 = (bf16[64,384]{1,0:T(8,128)(2,1)S(1)}, bf16[64,384]{1,0:T(8,128)(2,1)S(1)}, u32[]{:S(2)}, u32[]{:S(2)}) collective-permute-start(bf16[64,384]{1,0:T(8,128)(2,1)S(1)} %reduce_sum.140), channel_id=1, source_target_pairs={{0,16},{16,0},{1,17},{17,1},{2,18},{18,2},{3,19},{19,3},{4,20},{20... | collective-permute-start | bytes 147464 | tf_op jit(solution)/shard_map/ppermute | solution.py:32
  267.8 8.9 %collective-permute-start.32 = (bf16[32,2432]{1,0:T(8,128)(2,1)S(1)}, bf16[32,2432]{1,0:T(8,128)(2,1)S(1)}, u32[]{:S(2)}, u32[]{:S(2)}) collective-permute-start(bf16[32,2432]{1,0:T(8,128)(2,1)S(1)} %fusion.74), channel_id=1, source_target_pairs={{0,80},{16,64},{64,16},{80,0},{1,81},{17,65},{65,17},{81,1},{2,82}... | collective-permute-start | bytes 466952 | tf_op jit(solution)/shard_map/ppermute | solution.py:36
  270.0 10.4 %collective-permute-start.31 = (bf16[32,2432]{1,0:T(8,128)(2,1)S(1)}, bf16[32,2432]{1,0:T(8,128)(2,1)S(1)}, u32[]{:S(2)}, u32[]{:S(2)}) collective-permute-start(bf16[32,2432]{1,0:T(8,128)(2,1)S(1)} %fusion.74), channel_id=1, source_target_pairs={{0,64},{16,80},{64,0},{80,16},{1,65},{17,81},{65,1},{81,17},{2,66}... | collective-permute-start | bytes 466952 | tf_op jit(solution)/shard_map/ppermute | solution.py:36
  270.1 10.3 %collective-permute-start.30 = (bf16[32,2432]{1,0:T(8,128)(2,1)S(1)}, bf16[32,2432]{1,0:T(8,128)(2,1)S(1)}, u32[]{:S(2)}, u32[]{:S(2)}) collective-permute-start(bf16[32,2432]{1,0:T(8,128)(2,1)S(1)} %fusion.74), channel_id=1, source_target_pairs={{0,16},{16,0},{64,80},{80,64},{1,17},{17,1},{65,81},{81,65},{2,18}... | collective-permute-start | bytes 466952 | tf_op jit(solution)/shard_map/ppermute | solution.py:36
  273.6 6.9 %collective-permute-start.19 = (bf16[128,384]{1,0:T(8,128)(2,1)S(1)}, bf16[128,384]{1,0:T(8,128)(2,1)S(1)}, u32[]{:S(2)}, u32[]{:S(2)}) collective-permute-start(bf16[128,384]{1,0:T(8,128)(2,1)S(1)} %pad_maximum_fusion.18), channel_id=1, source_target_pairs={{0,32},{32,0},{64,96},{96,64},{1,33},{33,1},{65,97},{97,65},{2,34}... | collective-permute-start | bytes 294920 | tf_op jit(solution)/shard_map/ppermute | solution.py:36
  276.8 7.3 %collective-permute-start.20 = (bf16[128,384]{1,0:T(8,128)(2,1)S(1)}, bf16[128,384]{1,0:T(8,128)(2,1)S(1)}, u32[]{:S(2)}, u32[]{:S(2)}) collective-permute-start(bf16[128,384]{1,0:T(8,128)(2,1)S(1)} %pad_maximum_fusion.18), channel_id=1, source_target_pairs={{0,64},{32,96},{64,0},{96,32},{1,65},{33,97},{65,1},{97,33},{2,66}... | collective-permute-start | bytes 294920 | tf_op jit(solution)/shard_map/ppermute | solution.py:36
  280.4 5.5 %collective-permute-start.21 = (bf16[128,384]{1,0:T(8,128)(2,1)S(1)}, bf16[128,384]{1,0:T(8,128)(2,1)S(1)}, u32[]{:S(2)}, u32[]{:S(2)}) collective-permute-start(bf16[128,384]{1,0:T(8,128)(2,1)S(1)} %pad_maximum_fusion.18), channel_id=1, source_target_pairs={{0,96},{32,64},{64,32},{96,0},{1,97},{33,65},{65,33},{97,1},{2,98}... | collective-permute-start | bytes 294920 | tf_op jit(solution)/shard_map/ppermute | solution.py:36
  280.4 13.4 %collective-permute-start.33 = (bf16[128,2432]{1,0:T(8,128)(2,1)S(1)}, bf16[128,2432]{1,0:T(8,128)(2,1)S(1)}, u32[]{:S(2)}, u32[]{:S(2)}) collective-permute-start(bf16[128,2432]{1,0:T(8,128)(2,1)S(1)} %pad_maximum_fusion.8.refs_0_), channel_id=1, source_target_pairs={{0,32},{32,0},{1,33},{33,1},{2,34},{34,2},{3,35},{35,3},{4,36},{36... | collective-permute-start | bytes 1867784 | tf_op jit(solution)/shard_map/ppermute | solution.py:32
  285.9 15.4 %collective-permute-start.22 = (bf16[512,384]{1,0:T(8,128)(2,1)S(1)}, bf16[512,384]{1,0:T(8,128)(2,1)S(1)}, u32[]{:S(2)}, u32[]{:S(2)}) collective-permute-start(bf16[512,384]{1,0:T(8,128)(2,1)S(1)} %constant_dynamic-update-slice_fusion.5.own_ref), channel_id=1, source_target_pairs={{0,8},{8,0},{1,9},{9,1},{2,10},{10,2},{3,11},{11,3},{4,12},{12,4},... | collective-permute-start | bytes 1179656 | tf_op jit(solution)/shard_map/ppermute | solution.py:32
  291.0 24.8 %collective-permute-start.34 = (bf16[128,2432]{1,0:T(8,128)(2,1)S(1)}, bf16[128,2432]{1,0:T(8,128)(2,1)S(1)}, u32[]{:S(2)}, u32[]{:S(2)}) collective-permute-start(bf16[128,2432]{1,0:T(8,128)(2,1)S(1)} %pad_maximum_fusion.8.refs_0_), channel_id=1, source_target_pairs={{0,8},{8,0},{1,9},{9,1},{2,10},{10,2},{3,11},{11,3},{4,12},{12,4},... | collective-permute-start | bytes 1867784 | tf_op jit(solution)/shard_map/ppermute | solution.py:32
  293.9 22.0 %collective-permute-start.35 = (bf16[128,2432]{1,0:T(8,128)(2,1)S(1)}, bf16[128,2432]{1,0:T(8,128)(2,1)S(1)}, u32[]{:S(2)}, u32[]{:S(2)}) collective-permute-start(bf16[128,2432]{1,0:T(8,128)(2,1)S(1)} %collective-permute-done.33.refs_1_), channel_id=1, source_target_pairs={{0,8},{8,0},{1,9},{9,1},{2,10},{10,2},{3,11},{11,3},{4,12},{12,4},... | collective-permute-start | bytes 1867784 | tf_op jit(solution)/shard_map/ppermute | solution.py:32
  298.0 9.7 %collective-permute-start.17 = (bf16[128,1024]{1,0:T(8,128)(2,1)}, bf16[128,1024]{1,0:T(8,128)(2,1)S(1)}, u32[]{:S(2)}, u32[]{:S(2)}) collective-permute-start(bf16[128,1024]{1,0:T(8,128)(2,1)} %get-tuple-element.49), channel_id=1, source_target_pairs={{0,64},{32,96},{64,0},{96,32},{1,65},{33,97},{65,1},{97,33},{2,66}... | collective-permute-start | bytes 786440 | tf_op jit(solution)/shard_map/ppermute | solution.py:36
  300.2 13.4 %collective-permute-start.16 = (bf16[128,1024]{1,0:T(8,128)(2,1)}, bf16[128,1024]{1,0:T(8,128)(2,1)}, u32[]{:S(2)}, u32[]{:S(2)}) collective-permute-start(bf16[128,1024]{1,0:T(8,128)(2,1)} %get-tuple-element.50), channel_id=1, source_target_pairs={{0,96},{32,64},{64,32},{96,0},{1,97},{33,65},{65,33},{97,1},{2,98}... | collective-permute-start | bytes 786440 | tf_op jit(solution)/shard_map/ppermute | solution.py:36
  301.3 12.4 %collective-permute-start.15 = (bf16[128,1024]{1,0:T(8,128)(2,1)}, bf16[128,1024]{1,0:T(8,128)(2,1)}, u32[]{:S(2)}, u32[]{:S(2)}) collective-permute-start(bf16[128,1024]{1,0:T(8,128)(2,1)} %get-tuple-element.48), channel_id=1, source_target_pairs={{0,32},{32,0},{64,96},{96,64},{1,33},{33,1},{65,97},{97,65},{2,34}... | collective-permute-start | bytes 786440 | tf_op jit(solution)/shard_map/ppermute | solution.py:36
  301.5 12.2 %copy-start.8 = (f32[128,1024]{1,0:T(8,128)S(1)}, f32[128,1024]{1,0:T(8,128)}, u32[]{:S(2)}) copy-start(f32[128,1024]{1,0:T(8,128)} %get-tuple-element.42) | copy-start | bytes 1572868
Sparse Core Ops, SparseCore 0:
  11.2 97.4 all-gather.1
  164.3 52.3 reduce-scatter.3

commit v2 on v1

v2 whole, which is shorter than its diff:
```python
import math

import jax
import jax.numpy as jnp
from jax import lax
from jax.experimental import pallas as pl
from jax.experimental.pallas import tpu as pltpu
from jax.sharding import Mesh, PartitionSpec as P

HEADS = 16
HEAD_DIM = 64
BLOCK = 128
EPSILON = 1e-12
LOW = jnp.bfloat16
FULL = jnp.float32

CTX = ("zh", "zl", "xh", "core")
FSDP = ("xl", "y")
Z = ("zh", "zl")
SCALE = HEAD_DIM**-0.5
QUERY_BLOCK = 256
PARTS = QUERY_BLOCK // BLOCK


def dot(left, right, left_dim, right_dim):
    return lax.dot_general(
        left, right, (((left_dim,), (right_dim,)), ((), ())), preferred_element_type=FULL
    )


def swap(value, axis):
    return lax.ppermute(value, axis, [(0, 1), (1, 0)])


def exchange(value, axes, mask):
    return lax.ppermute(value, axes, [(i, i ^ mask) for i in range(4)])


def with_pair(value, axis):
    return jnp.concatenate([value, swap(value, axis)], axis=0)


def with_four(value, axes):
    moved = {mask: exchange(value, axes, mask) for mask in (1, 3, 2)}
    return jnp.concatenate([value, moved[1], moved[2], moved[3]], axis=0)


def forward_kernel(place, q_ref, k_ref, v_ref, low_ref, out_ref, log_ref, keys):
    step = pl.program_id(0)

    @pl.when(step == 0)
    def _():
        keys[...] = k_ref[...].astype(FULL).T.astype(LOW)

    queries = q_ref[...] * LOW(SCALE)
    scores = dot(keys[...], queries, 1, 0)
    top = jnp.max(scores, axis=0, keepdims=True)
    weights = jnp.exp(scores - top)
    total = jnp.sum(weights, axis=0, keepdims=True)
    attended = dot(v_ref[...], weights.astype(LOW), 1, 0) / total
    out_ref[...] = attended
    log_ref[...] = top + jnp.log(total)
    low = attended.astype(LOW)
    for part in range(PARTS):
        low_ref[place[step * PARTS + part]] = low[:, part * BLOCK : (part + 1) * BLOCK]


def attention_forward(place, projected):
    length = projected.shape[1]
    return pl.pallas_call(
        forward_kernel,
        grid_spec=pltpu.PrefetchScalarGridSpec(
            num_scalar_prefetch=1,
            grid=(length // QUERY_BLOCK,),
            in_specs=[
                pl.BlockSpec((HEAD_DIM, QUERY_BLOCK), lambda i, p: (0, i)),
                pl.BlockSpec((HEAD_DIM, length), lambda i, p: (1, 0)),
                pl.BlockSpec((HEAD_DIM, length), lambda i, p: (2, 0)),
            ],
            out_specs=[
                pl.BlockSpec((length // BLOCK, HEAD_DIM, BLOCK), lambda i, p: (0, 0, 0)),
                pl.BlockSpec((HEAD_DIM, QUERY_BLOCK), lambda i, p: (0, i)),
                pl.BlockSpec((1, QUERY_BLOCK), lambda i, p: (0, i)),
            ],
            scratch_shapes=[pltpu.VMEM((length, HEAD_DIM), LOW)],
        ),
        out_shape=[
            jax.ShapeDtypeStruct((length // BLOCK, HEAD_DIM, BLOCK), LOW),
            jax.ShapeDtypeStruct((HEAD_DIM, length), FULL),
            jax.ShapeDtypeStruct((1, length), FULL),
        ],
        compiler_params=pltpu.CompilerParams(vmem_limit_bytes=40 * 1024 * 1024),
        cost_estimate=pl.CostEstimate(
            flops=16 * length * length * HEAD_DIM,
            bytes_accessed=10 * length * HEAD_DIM,
            transcendentals=length * length,
        ),
        name="attention_forward",
    )(place, projected, projected, projected)


def backward_kernel(
    place, q_ref, k_ref, v_ref, grad_ref, out_ref, log_ref, near_ref, far_ref, blocks_ref,
    keys, values, dk, dv,
):
    step = pl.program_id(0)

    @pl.when(step == 0)
    def _():
        keys[...] = k_ref[...].astype(FULL).T.astype(LOW)
        values[...] = v_ref[...].astype(FULL).T.astype(LOW)
        dk[...] = jnp.zeros_like(dk)
        dv[...] = jnp.zeros_like(dv)

    queries = q_ref[...] * LOW(SCALE)
    grad = jnp.concatenate([grad_ref[place[step * PARTS + p]] for p in range(PARTS)], axis=1)
    delta = jnp.sum(grad.astype(FULL) * out_ref[...], axis=0, keepdims=True)
    scores = dot(keys[...], queries, 1, 0)
    probs = jnp.exp(scores - log_ref[...])
    grad_probs = dot(values[...], grad, 1, 0)
    grad_scores = (probs * (grad_probs - delta)).astype(LOW)
    dv[...] += dot(grad, probs.astype(LOW), 1, 1)
    dk[...] += dot(queries, grad_scores, 1, 1)
    dq = (dot(k_ref[...], grad_scores, 1, 0) * SCALE).astype(LOW)
    steps = pl.num_programs(0)
    half = near_ref.shape[1]
    start = pl.multiple_of(lax.rem(step, steps // 2) * QUERY_BLOCK, QUERY_BLOCK)

    for part in range(PARTS):
        blocks_ref[place[step * PARTS + part], :HEAD_DIM] = dq[:, part * BLOCK : (part + 1) * BLOCK]

    @pl.when(step < steps // 2)
    def _():
        near_ref[:HEAD_DIM, pl.ds(start, QUERY_BLOCK)] = dq

    @pl.when(step >= steps // 2)
    def _():
        far_ref[:HEAD_DIM, pl.ds(start, QUERY_BLOCK)] = dq

    @pl.when(step == steps - 1)
    def _():
        for part, total in ((1, dk), (2, dv)):
            rows = slice(part * HEAD_DIM, (part + 1) * HEAD_DIM)
            near_ref[rows, :] = total[:, :half].astype(LOW)
            far_ref[rows, :] = total[:, half:].astype(LOW)
            for block in range(HEADS):
                blocks_ref[place[block], rows] = total[
                    :, block * BLOCK : (block + 1) * BLOCK
                ].astype(LOW)


def attention_backward(place, projected, grad_blocks, attended, log_total):
    length = projected.shape[1]
    half = jax.ShapeDtypeStruct((3 * HEAD_DIM, length // 2), LOW)
    blocks = jax.ShapeDtypeStruct((length // BLOCK, 3 * HEAD_DIM, BLOCK), LOW)
    return pl.pallas_call(
        backward_kernel,
        grid_spec=pltpu.PrefetchScalarGridSpec(
            num_scalar_prefetch=1,
            grid=(length // QUERY_BLOCK,),
            in_specs=[
                pl.BlockSpec((HEAD_DIM, QUERY_BLOCK), lambda i, p: (0, i)),
                pl.BlockSpec((HEAD_DIM, length), lambda i, p: (1, 0)),
                pl.BlockSpec((HEAD_DIM, length), lambda i, p: (2, 0)),
                pl.BlockSpec((length // BLOCK, HEAD_DIM, BLOCK), lambda i, p: (0, 0, 0)),
                pl.BlockSpec((HEAD_DIM, QUERY_BLOCK), lambda i, p: (0, i)),
                pl.BlockSpec((1, QUERY_BLOCK), lambda i, p: (0, i)),
            ],
            out_specs=[pl.BlockSpec(half.shape, lambda i, p: (0, 0))] * 2
            + [pl.BlockSpec(blocks.shape, lambda i, p: (0, 0, 0))],
            scratch_shapes=[
                pltpu.VMEM((length, HEAD_DIM), LOW),
                pltpu.VMEM((length, HEAD_DIM), LOW),
                pltpu.VMEM((HEAD_DIM, length), FULL),
                pltpu.VMEM((HEAD_DIM, length), FULL),
            ],
        ),
        out_shape=[half, half, blocks],
        compiler_params=pltpu.CompilerParams(vmem_limit_bytes=58 * 1024 * 1024),
        cost_estimate=pl.CostEstimate(
            flops=40 * length * length * HEAD_DIM,
            bytes_accessed=20 * length * HEAD_DIM,
            transcendentals=length * length,
        ),
        name="attention_backward",
    )(place, projected, projected, projected, grad_blocks, attended, log_total)


def assemble_kernel(spots, own_ref, pair_ref, up_ref, down_ref):
    part = up_ref.shape[1] // 4
    rows = up_ref.shape[0]
    for core, piece in enumerate((own_ref, pair_ref)):
        for zl in range(2):
            lane = pl.multiple_of(spots[core * 2 + zl] * part, part)
            source = slice(zl * rows, (zl + 1) * rows)
            up_ref[:, pl.ds(lane, part)] = piece[source, :part].astype(FULL)
            down_ref[:, pl.ds(lane, part)] = piece[source, part:].astype(FULL)


def assemble(spots, pieces, units):
    shape = jax.ShapeDtypeStruct((BLOCK, units), FULL)
    return local_call(assemble_kernel, spots, pieces, [shape, shape], [], "assemble")


def terms_kernel(spots, near_ref, far_ref, part_0, part_1, part_2, part_3, block_0, block_1, block_2,
                 block_3, first_ref, second_ref, out_ref, total):
    size = near_ref.shape[0]
    count = part_0.shape[0]
    length = near_ref.shape[1]
    columns = out_ref.shape[1] - size - 16
    lanes = pl.ds(pl.multiple_of(spots[0] * columns, columns), columns)
    out = jnp.zeros((columns, length), FULL)
    for block in (block_0, block_1, block_2, block_3):
        out += dot(block[:BLOCK, lanes].astype(FULL).T.astype(LOW), block[BLOCK:], 1, 0)
    total[...] = jnp.zeros_like(total)
    for index, part in enumerate((part_0, part_1, part_2, part_3)):
        source = (near_ref, far_ref)[index // 2]
        start = index % 2 * count
        total[...] += dot(source[:, start : start + count], part[...], 1, 0)
    for block in range(out_ref.shape[0]):
        rows = slice(block * BLOCK, (block + 1) * BLOCK)
        out_ref[block, :size] = total[:, rows].astype(LOW)
        out_ref[block, size : size + columns] = out[:, rows].astype(LOW)
        norms = jnp.concatenate(
            [first_ref[:, rows], second_ref[:, rows], jnp.zeros((12, BLOCK), FULL)], axis=0
        )
        out_ref[block, size + columns :] = norms.astype(LOW)


def weight_terms(spots, near, far, parts, blocks, first, second):
    size, length = near.shape
    columns = length // 4
    outs = [jax.ShapeDtypeStruct((length // BLOCK, size + columns + 16, BLOCK), LOW)]
    arrays = [near, far, *parts, *blocks, first, second]
    scratch = [pltpu.VMEM((size, length), FULL)]
    return local_call(terms_kernel, spots, arrays, outs, scratch, "weight_terms")[0]


def assemble_rest_kernel(spots, own_ref, pair_ref, qkv_ref, out_ref, norm_ref):
    width = out_ref.shape[1]
    part = width // 4
    size = 3 * HEAD_DIM
    step = own_ref.shape[0] // 2
    flip = spots[12] == 1
    total = jnp.zeros((16, BLOCK), FULL)
    for core, piece in enumerate((own_ref, pair_ref)):
        for zl in range(2):
            for zh in range(2):
                start = zl * step + zh * 2 * size
                lane = spots[(core * 2 + zl) * 2 + zh] * BLOCK
                near = piece[start : start + size].astype(FULL)
                far = piece[start + size : start + 2 * size].astype(FULL)
                first = jnp.where(flip, far, near)
                second = jnp.where(flip, near, far)
                for which in range(3):
                    rows = slice(which * HEAD_DIM, (which + 1) * HEAD_DIM)
                    columns = pl.ds(pl.multiple_of(which * width + lane, BLOCK), BLOCK)
                    qkv_ref[:, columns] = jnp.concatenate([first[rows], second[rows]], axis=0).T
            start = zl * step + 4 * size
            lane = pl.multiple_of(spots[8 + core * 2 + zl] * part, part)
            out_ref[:, pl.ds(lane, part)] = piece[start : start + part].astype(FULL).T
            total += piece[start + part : start + part + 16].astype(FULL)
    norm_ref[...] = total


def assemble_rest(spots, own, pair, width):
    outs = [
        jax.ShapeDtypeStruct((BLOCK, 3 * width), FULL),
        jax.ShapeDtypeStruct((BLOCK, width), FULL),
        jax.ShapeDtypeStruct((16, BLOCK), FULL),
    ]
    return local_call(assemble_rest_kernel, spots, [own, pair], outs, [], "assemble_rest")


def input_kernel(spots, every_ref, own_ref, pair_ref, base_ref, out_ref, grads):
    half = own_ref.shape[1]

    @pl.when(pl.program_id(0) == 0)
    def _():
        for which in range(3):
            for head in range(HEADS):
                start = (which * HEADS + head) * HEAD_DIM
                grads[start : start + HEAD_DIM, :] = every_ref[
                    head_place(head), which * HEAD_DIM : (which + 1) * HEAD_DIM
                ]

    total = jnp.zeros((own_ref.shape[0], BLOCK), FULL)
    for core, part in enumerate((own_ref, pair_ref)):
        rows = pl.ds(pl.multiple_of(spots[core] * half, half), half)
        total += dot(part[...], grads[rows, :], 1, 0)
    out_ref[...] = base_ref[...] + total.T


def input_product(spots, every, own, pair, base):
    rows, width = base.shape
    tile = 512
    weights = pl.BlockSpec((tile, own.shape[1]), lambda i, s: (i, 0))
    block = pl.BlockSpec((rows, tile), lambda i, s: (0, i))
    return pl.pallas_call(
        input_kernel,
        grid_spec=pltpu.PrefetchScalarGridSpec(
            num_scalar_prefetch=1,
            grid=(width // tile,),
            in_specs=[pl.BlockSpec(every.shape, lambda i, s: (0, 0, 0)), weights, weights, block],
            out_specs=block,
            scratch_shapes=[pltpu.VMEM((2 * own.shape[1], rows), LOW)],
        ),
        out_shape=jax.ShapeDtypeStruct((rows, width), FULL),
        compiler_params=pltpu.CompilerParams(vmem_limit_bytes=58 * 1024 * 1024),
        name="input_product",
    )(spots, every, own, pair, base)


def head_place(index):
    return (index // 4) * 4 + (index % 2) * 2 + (index // 2) % 2


def out_kernel(spots, att_ref, out_ref, x_ref, norms_ref, att_out_ref, low_ref, hid_ref,
               normal_ref, inverse_ref, rows_scratch):
    for head in range(HEADS):
        rows_scratch[head * HEAD_DIM : (head + 1) * HEAD_DIM, :] = att_ref[head_place(head)]
    attended = rows_scratch[...].astype(FULL).T.astype(LOW)
    att_out_ref[...] = attended
    residual = x_ref[...].astype(FULL) + dot(attended, out_ref[...], 1, 0)
    normal, inverse = norm_forward(residual)
    hidden = normal * norms_ref[0:1] + norms_ref[1:2]
    hid_ref[...] = hidden
    low_ref[...] = hidden.astype(LOW)
    normal_ref[...] = normal
    inverse_ref[...] = jnp.broadcast_to(inverse, (BLOCK, BLOCK))


def whole_specs(shapes):
    return [pl.BlockSpec(s, lambda i, p, n=len(s): (0,) * n) for s in shapes]


def local_call(kernel, spots, arrays, outs, scratch, name, specs=None, limit=40):
    return pl.pallas_call(
        kernel,
        grid_spec=pltpu.PrefetchScalarGridSpec(
            num_scalar_prefetch=1,
            grid=(1,),
            in_specs=specs or whole_specs([a.shape for a in arrays]),
            out_specs=whole_specs([o.shape for o in outs]),
            scratch_shapes=scratch,
        ),
        out_shape=outs,
        compiler_params=pltpu.CompilerParams(vmem_limit_bytes=limit * 1024 * 1024),
        name=name,
    )(spots, *arrays)


def out_last(arrays, index):
    specs = whole_specs([a.shape for a in arrays])
    width = arrays[index].shape[0]
    last = arrays[index].shape[1] // width - 1
    specs[index] = pl.BlockSpec((width, width), lambda i, p: (0, last))
    return specs


def out_and_norm(spots, blocks, rest, inputs, norms):
    rows, width = inputs.shape
    arrays = [blocks, rest, inputs, norms]
    shape = jax.ShapeDtypeStruct
    return local_call(
        out_kernel,
        spots,
        arrays,
        [
            shape((rows, width), LOW),
            shape((rows, width), LOW),
            shape((rows, width), FULL),
            shape((rows, width), FULL),
            shape((rows, BLOCK), FULL),
        ],
        [pltpu.VMEM((width, rows), LOW)],
        "out_and_norm",
        out_last(arrays, 1),
        58,
    )


def norm_one_kernel(spots, base_ref, late_ref, normal_ref, inverse_ref, norms_ref, out_ref,
                    grad_ref, low_ref, blocks_ref, sums_ref, total):
    grad = base_ref[...] + late_ref[...].astype(FULL)
    normal = normal_ref[...]
    result, gain_sum, bias_sum = norm_backward(grad, normal, inverse_ref[:, :1], norms_ref[0:1])
    grad_ref[...] = result
    low_ref[...] = result.astype(LOW)
    sums_ref[0:1, :] = gain_sum[None]
    sums_ref[1:2, :] = bias_sum[None]
    total[...] = dot(out_ref[...], low_ref[...], 1, 1)
    for head in range(HEADS):
        rows = slice(head * HEAD_DIM, (head + 1) * HEAD_DIM)
        blocks_ref[head_place(head)] = total[rows, :].astype(LOW)


def norm_one_back(spots, base, late, normal, inverse, norms, rest):
    rows, width = base.shape
    arrays = [base, late, normal, inverse, norms, rest]
    shape = jax.ShapeDtypeStruct
    return local_call(
        norm_one_kernel,
        spots,
        arrays,
        [
            shape((rows, width), FULL),
            shape((rows, width), LOW),
            shape((HEADS, HEAD_DIM, rows), LOW),
            shape((2, width), FULL),
        ],
        [pltpu.VMEM((width, rows), FULL)],
        "norm_one_back",
        out_last(arrays, 5),
        58,
    )


def ff_terms_kernel(hid_a, hid_b, up_a, up_b, mixed_a, mixed_b, act_a, act_b, out_ref, left):
    step = pl.program_id(0)
    steps = pl.num_programs(0) // 2
    half = hid_a.shape[0]

    @pl.when(step == 0)
    def _():
        left[:, :half] = hid_a[...].astype(FULL).T.astype(LOW)
        left[:, half:] = hid_b[...].astype(FULL).T.astype(LOW)

    @pl.when(step == steps)
    def _():
        left[:, :half] = mixed_a[...].astype(FULL).T.astype(LOW)
        left[:, half:] = mixed_b[...].astype(FULL).T.astype(LOW)

    @pl.when(step < steps)
    def _():
        right = jnp.concatenate([up_a[...], up_b[...]], axis=0)
        out_ref[...] = dot(left[...], right, 1, 0).astype(LOW)

    @pl.when(step >= steps)
    def _():
        right = jnp.concatenate([act_a[...], act_b[...]], axis=0)
        out_ref[...] = dot(left[...], right, 1, 0).astype(LOW)


def ff_products(hidden, grad_upward, grad_mixed, activated):
    count, width = hidden[0].shape
    units = activated[0].shape[1]
    tile = 512
    steps = units // tile
    whole = pl.BlockSpec((count, width), lambda i: (0, 0))
    early = pl.BlockSpec((count, tile), lambda i: (0, jnp.minimum(i, steps - 1)))
    later = pl.BlockSpec((count, tile), lambda i: (0, jnp.maximum(i - steps, 0)))
    return pl.pallas_call(
        ff_terms_kernel,
        grid=(2 * steps,),
        in_specs=[whole, whole, early, early, whole, whole, later, later],
        out_specs=pl.BlockSpec((width, tile), lambda i: (0, i)),
        out_shape=jax.ShapeDtypeStruct((width, 2 * units), LOW),
        scratch_shapes=[pltpu.VMEM((width, 2 * count), LOW)],
        compiler_params=pltpu.CompilerParams(vmem_limit_bytes=58 * 1024 * 1024),
        cost_estimate=pl.CostEstimate(
            flops=8 * count * width * units, bytes_accessed=8 * width * units, transcendentals=0
        ),
        name="ff_products",
    )(*hidden, *grad_upward, *grad_mixed, *activated)


def norm_forward(values):
    center = values - jnp.mean(values, axis=-1, keepdims=True)
    spread = jnp.mean(center * center, axis=-1, keepdims=True)
    inverse = lax.rsqrt(spread + EPSILON)
    return center * inverse, inverse


def norm_backward(grad, normal, inverse, gain):
    scaled = grad * gain
    result = inverse * (
        scaled
        - jnp.mean(scaled, axis=-1, keepdims=True)
        - normal * jnp.mean(scaled * normal, axis=-1, keepdims=True)
    )
    return result, jnp.sum(grad * normal, axis=0), jnp.sum(grad, axis=0)


def gather_group(value):
    late = swap(value, "zl")
    near = with_pair(value, "core")
    return near, with_pair(late, "core")


def product_group(parts, right, left_dim, right_dim):
    near, far = parts
    half = far.shape[0] // 2
    term = dot(far, right, left_dim, right_dim)
    sent = term[:half] + swap(term[half:].astype(LOW), "core").astype(FULL)
    sent, near = lax.optimization_barrier((sent.astype(LOW), near))
    late = swap(sent, "zl")
    term = dot(near, right, left_dim, right_dim)
    return term[:half] + swap(term[half:].astype(LOW), "core").astype(FULL), late, sent


def per_device(
    tokens, w_qkv, w_out, w_up, w_down, ln1_gain, ln1_bias, ln2_gain, ln2_bias, cotangent
):
    inputs = tokens[0]
    width = inputs.shape[1]
    units = w_up.shape[1]
    ff_part = units // 4
    out_part = width // 4
    z, zh, zl, xh, core = (lax.axis_index(a) for a in (Z, "zh", "zl", "xh", "core"))
    group = zl * 2 + core
    pair = z * 2 + core
    place = jnp.stack(
        [
            ((z ^ dz) * 2 + (xh ^ dx)) * 2 + (core ^ dc)
            for dx in range(2)
            for dc in range(2)
            for dz in (0, 1, 3, 2)
        ]
    ).astype(jnp.int32)
    cores = jnp.stack([core, 1 - core]).astype(jnp.int32)
    groups = jnp.stack(
        [(zl ^ dl) * 2 + (core ^ dc) for dc in range(2) for dl in range(2)]
    ).astype(jnp.int32)

    heads = [
        lax.dynamic_slice_in_dim(w_qkv, which * width + pair * BLOCK, BLOCK, 1) for which in range(3)
    ]
    first = jnp.concatenate([h[:, :HEAD_DIM] for h in heads], axis=1)
    second = jnp.concatenate([h[:, HEAD_DIM:] for h in heads], axis=1)
    own_mine = jnp.where(xh == 0, first, second)
    norm_rows = jnp.pad(
        jnp.stack([ln1_gain, ln1_bias, ln2_gain, ln2_bias]), ((0, 12), (0, BLOCK))
    )
    early = jnp.concatenate([jnp.pad(own_mine, ((0, 0), (0, HEAD_DIM))), norm_rows], axis=0)
    together = lax.optimization_barrier
    early, inputs = together((jnp.broadcast_to(early[None], (8,) + early.shape), inputs))
    early = lax.all_to_all(early, FSDP, split_axis=0, concat_axis=0, tiled=True)
    up_mine = lax.dynamic_slice_in_dim(w_up, group * ff_part, ff_part, 1)
    down_mine = lax.dynamic_slice_in_dim(w_down, group * ff_part, ff_part, 1)
    rest = jnp.concatenate([up_mine, down_mine, w_out], axis=1)
    rest = lax.all_gather(rest, FSDP, axis=0, tiled=True)
    far, one = together((swap(inputs, "xh"), exchange(inputs, Z, 1)))
    near_two = jnp.concatenate([inputs, one], axis=0)
    near_rest, far_one = together((exchange(near_two, Z, 3), exchange(far, Z, 1)))
    near_half, early = together((jnp.concatenate([near_two, near_rest], axis=0), early))
    far_two = jnp.concatenate([far, far_one], axis=0)
    far_rest = exchange(far_two, Z, 3)
    near_core = swap(near_half, "core")
    far_half = jnp.concatenate([far_two, far_rest], axis=0)
    parts = [near_half, near_core, far_half, swap(far_half, "core")]
    own_qkv = early[:, :BLOCK, : 3 * HEAD_DIM].reshape(width, 3 * HEAD_DIM)
    norms = early[:, BLOCK : BLOCK + 4, :BLOCK].astype(FULL).transpose(1, 0, 2).reshape(4, width)
    gain_two, bias_two = norms[2:3], norms[3:4]
    head = jnp.concatenate([dot(own_qkv, p, 0, 1).astype(LOW) for p in parts], axis=1)

    low_blocks, attended, log_total = attention_forward(place, head)
    low_blocks = lax.all_to_all(low_blocks, CTX, split_axis=0, concat_axis=0, tiled=True)
    qkv_mine = lax.dynamic_slice_in_dim(w_qkv, core * (3 * width // 2), 3 * width // 2, 1)
    rest, qkv_mine, low_blocks = together((rest, qkv_mine, low_blocks))
    up_part = rest[:, :ff_part]
    down_part = rest[:, ff_part : 2 * ff_part]
    qkv_own = lax.all_gather(qkv_mine, FSDP, axis=0, tiled=True)
    attended_low, hidden_low, hidden, normal_one, inverse_one = out_and_norm(
        cores, low_blocks, rest, inputs, norms
    )
    hidden_low = gather_group(hidden_low)
    upward = [dot(h, up_part, 1, 0) for h in hidden_low]
    cdf = [0.5 * (1.0 + lax.erf(u * math.sqrt(0.5))) for u in upward]
    activated_low = [(u * c).astype(LOW) for u, c in zip(upward, cdf)]
    slope = [
        c + u * jnp.exp(-0.5 * u * u) * (1.0 / math.sqrt(2.0 * math.pi))
        for u, c in zip(upward, cdf)
    ]
    near, late, _ = product_group(activated_low, down_part, 1, 1)
    mixed = hidden + near + late.astype(FULL)
    normal_two, inverse_two = norm_forward(mixed)
    layer_out = (normal_two * gain_two + bias_two).astype(LOW)

    grad_mixed, gain_two_grad, bias_two_grad = norm_backward(
        cotangent[0].astype(FULL), normal_two, inverse_two, gain_two
    )
    grad_mixed_low = gather_group(grad_mixed.astype(LOW))
    grad_upward_low = [
        (dot(g, down_part, 1, 0) * k).astype(LOW) for g, k in zip(grad_mixed_low, slope)
    ]
    near, late, sent = product_group(grad_upward_low, up_part, 1, 1)
    late, qkv_own = together((late, qkv_own))
    qkv_pair = swap(qkv_own, "core")
    near, *held = together((near, *hidden_low))
    ff_terms = ff_products(held, grad_upward_low, grad_mixed_low, activated_low)
    ff_share = lax.psum_scatter(ff_terms, FSDP, scatter_dimension=0, tiled=True)

    grad_residual, grad_residual_low, grad_blocks, norm_one_sums = norm_one_back(
        cores, grad_mixed + near, late, normal_one, inverse_one, norms, rest
    )
    grad_blocks = lax.all_to_all(grad_blocks, CTX, split_axis=0, concat_axis=0, tiled=True)
    pairs = jnp.concatenate([grad_residual_low, attended_low], axis=0)
    late_pairs = swap(pairs, "zl")
    blocks = [pairs, swap(pairs, "core"), late_pairs, swap(late_pairs, "core")]

    grad_near, grad_far, grad_out = attention_backward(
        place, head, grad_blocks, attended, log_total
    )
    norm_two_sums = jnp.stack([gain_two_grad, bias_two_grad])
    terms = weight_terms(
        groups[:1], grad_near, grad_far, parts, blocks, norm_one_sums, norm_two_sums
    )
    shares = lax.all_to_all(terms, FSDP, split_axis=0, concat_axis=0, tiled=True)

    def sum_pair(value, axis):
        return (value.astype(FULL) + swap(value, axis).astype(FULL)).astype(LOW)

    size = 3 * HEAD_DIM
    def spread(qkv_part, out_part, axis):
        theirs = swap(jnp.concatenate([qkv_part, out_part], axis=0), axis)
        count = qkv_part.shape[0]
        summed = out_part.astype(FULL) + theirs[count:].astype(FULL)
        return jnp.concatenate([qkv_part, theirs[:count]], axis=0), summed.astype(LOW)

    ff_share, grad_out = together((ff_share, grad_out, terms))[:2]
    ff_sum, shares = together((sum_pair(ff_share, "zh"), shares))
    shares = jnp.sum(shares.astype(FULL), axis=0).astype(LOW)
    every = lax.all_to_all(grad_out, CTX, split_axis=0, concat_axis=0, tiled=True)
    ff_sum, every, *sums = together(
        (sum_pair(ff_sum, "xh"), every, *spread(shares[:size], shares[size:], "xh"))
    )
    input_grad = input_product(cores, every, qkv_own, qkv_pair, grad_residual)
    rest_sum = jnp.concatenate(spread(*sums, "zh"), axis=0)
    ff_sum, input_grad, rest_sum = together(
        (with_pair(ff_sum, "zl"), input_grad, with_pair(rest_sum, "zl"))
    )
    ff_pair, rest_pair = swap(ff_sum, "core"), swap(rest_sum, "core")
    spots = [
        ((zh ^ dh) * 2 + (zl ^ dl)) * 2 + (core ^ dc)
        for dc in range(2)
        for dl in range(2)
        for dh in range(2)
    ]
    spots = jnp.concatenate([jnp.stack(spots).astype(jnp.int32), groups, xh[None].astype(jnp.int32)])
    grad_w_qkv, grad_w_out, norm_grads = assemble_rest(spots, rest_sum, rest_pair, width)
    grad_w_up, grad_w_down = assemble(groups, [ff_sum, ff_pair], units)

    return (
        layer_out[None],
        input_grad[None],
        grad_w_qkv,
        grad_w_out,
        grad_w_up,
        grad_w_down,
        norm_grads[0],
        norm_grads[1],
        norm_grads[2],
        norm_grads[3],
    )


def solution(mesh):
    fine = Mesh(mesh.devices.reshape(2, 2, 2, 2, 2, 4), ("zh", "zl", "xh", "core", "xl", "y"))
    block = P(FSDP, CTX, None)
    rows = P(FSDP, None)
    row = P(FSDP)
    return jax.shard_map(
        per_device,
        mesh=fine,
        in_specs=(block, rows, rows, rows, rows, row, row, row, row, block),
        out_specs=(block, block, rows, rows, rows, rows, row, row, row, row),
        check_vma=False,
    )
```

time: 328 us -> 301 us (0.918)
  Pallas kernels: 28.5 us -> 58.3 us
  matrix products: 33.2 us -> 11.7 us
  blocking collectives: 13.7 us -> 0 us
  other arithmetic: 21.7 us -> 10.2 us
  waiting for transfers between devices: 121 us -> 112 us
  local copies, waits for them, and re-layouts: 27.4 us -> 23.5 us
    ppermute x15 -> x4, waiting for transfers between devices: 36.5 us -> 7.7 us  [exchange(): return lax.ppermute(value, axes, [(i, i ^ mask) for i in range(4)])]
    pallas_call x2 -> x7, Pallas kernels: 4.91 us -> 31.6 us  [the longest x5 18.4 us: local_call(): pl.pallas_call(kernel, grid_spec=pltpu.PrefetchScalarGridSpec(num_scalar_...]
    dot_general x18 -> x12, matrix products: 33.2 us -> 11.7 us  [dot(): lax.dot_general(left, right, (((left_dim,), (right_dim,)), ((), ())), pre...]
    all_to_all x1 -> x0, blocking collectives: 13.7 us -> none  [per_device(): lax.all_to_all(low_blocks, CTX, split_axis=0, concat_axis=0, tiled=True)]
    ppermute x15 -> x4, starting transfers between devices: 20.9 us -> 7.59 us  [exchange(): return lax.ppermute(value, axes, [(i, i ^ mask) for i in range(4)])]
    ppermute x21 -> x27, starting transfers between devices: 23.5 us -> 35.1 us  [swap(): return lax.ppermute(value, axis, [(0, 1), (1, 0)])]
    all_to_all x4 -> x5, waiting for transfers between devices: 29.1 us -> 37.6 us  [the longest x1 9.27 us: per_device(): lax.all_to_all(grad_out, CTX, split_axis=0, concat_axis=0, tiled=True)]
    all_gather x1 -> x2, waiting for transfers between devices: 0.02 us -> 4.85 us  [the longest x1 4.85 us: per_device(): rest = lax.all_gather(rest, FSDP, axis=0, tiled=True)]
  transfers between devices with their start and end apart: 42 -> 39, of which waited for: 24 -> 25; matrix products, arithmetic and copies ran while one was open for 17% -> 13% of each run, Pallas kernels for 8% -> 17%
where the time goes in v2:
time: 301 us; the launch traced here: 299 us
  waiting for transfers between devices  112 us (37%)
  starting transfers between devices  69.1 us (23%)
  Pallas kernels  58.3 us (19%)
  local copies, waits for them, and re-layouts  23.5 us (8%)
  between operations  14.5 us (5%)
  matrix products  11.7 us (4%)
  other arithmetic  10.2 us (3%)
    ppermute x27, waiting for transfers between devices, swap(): return lax.ppermute(value, axis, [(0, 1), (1, 0)])  60.1 us
    ppermute x27, starting transfers between devices, swap(): return lax.ppermute(value, axis, [(0, 1), (1, 0)])  35.1 us
    pallas_call x5, Pallas kernels, local_call(): pl.pallas_call(kernel, grid_spec=pltpu.PrefetchScalarGridSpec(num_scalar_...  18.4 us
    pallas_call x1, Pallas kernels, attention_backward(): pl.pallas_call(backward_kernel, grid_spec=pltpu.PrefetchScalarGridSpec(nu...  15.3 us
    dot_general x12, matrix products, dot(): lax.dot_general(left, right, (((left_dim,), (right_dim,)), ((), ())), pre...  11.7 us
    pallas_call x1, Pallas kernels, attention_forward(): pl.pallas_call(forward_kernel, grid_spec=pltpu.PrefetchScalarGridSpec(num...  11.5 us
    unnamed x67, local copies, waits for them, and re-layouts  10.9 us
    all_to_all x1, waiting for transfers between devices, per_device(): lax.all_to_all(grad_out, CTX, split_axis=0, concat_axis=0, tiled=True)  9.27 us
  transfers between devices with their start and end apart: 39, of which 25 were waited for; matrix products, arithmetic and copies ran while one was open for 13% of the time, Pallas kernels for 17%

profile of v2, /device:TPU:1, one launch (start us, length us, event | category | flops | bytes accessed | tf_op | source)
XLA Modules:
  0.0 299.3 jit_solution(14029488253186989940)
XLA Ops:
  8.4 1.9 pad_maximum_fusion.2
  12.5 3.6 %collective-permute-start = (bf16[128,1024]{1,0:T(8,128)(2,1)S(1)}, bf16[128,1024]{1,0:T(8,128)(2,1)S(1)}, u32[]{:S(2)}, u32[]{:S(2)}) collective-permute-start(bf16[128,1024]{1,0:T(8,128)(2,1)S(1)} %bitcast.105), channel_id=1, source_target_pairs={{0,16},{16,0},{1,17},{17,1},{2,18},{18,2},{3,19},{19,3},{4,20},{20... | collective-permute-start | bytes 786440 | tf_op jit(solution)/shard_map/ppermute | solution.py:32
  16.0 1.6 collective-permute-start.1
  17.6 4.0 %collective-permute-done = bf16[128,1024]{1,0:T(8,128)(2,1)S(1)} collective-permute-done((bf16[128,1024]{1,0:T(8,128)(2,1)S(1)}, bf16[128,1024]{1,0:T(8,128)(2,1)S(1)}, u32[]{:S(2)}, u32[]{:S(2)}) %collective-permute-start) | collective-permute-done | bytes 262176 | tf_op jit(solution)/shard_map/ppermute | solution.py:32
  21.6 1.5 collective-permute-done.1
  23.1 3.6 %collective-permute-start.2 = (bf16[256,1024]{1,0:T(8,128)(2,1)S(1)}, bf16[256,1024]{1,0:T(8,128)(2,1)S(1)}, u32[]{:S(2)}, u32[]{:S(2)}) collective-permute-start(bf16[256,1024]{1,0:T(8,128)(2,1)S(1)} %pad_maximum_fusion.5), channel_id=1, source_target_pairs={{0,96},{32,64},{64,32},{96,0},{1,97},{33,65},{65,33},{97,1},{2,98}... | collective-permute-start | bytes 1572872 | tf_op jit(solution)/shard_map/ppermute | solution.py:36
  26.8 4.3 %all-to-all-start = ((bf16[8,144,256]{2,1,0:T(8,128)(2,1)}), bf16[8,144,256]{2,1,0:T(8,128)(2,1)}, u32[]{:S(2)}, u32[]{:S(2)}) async-start(bf16[8,144,256]{2,1,0:T(8,128)(2,1)} %broadcast_in_dim.8), calls=%async_computation | async-start | bytes 1179648 | tf_op jit(solution)/shard_map/all_to_all | solution.py:538
  31.1 1.5 collective-permute-done.3
  32.5 4.7 %collective-permute-done.2 = bf16[256,1024]{1,0:T(8,128)(2,1)S(1)} collective-permute-done((bf16[256,1024]{1,0:T(8,128)(2,1)S(1)}, bf16[256,1024]{1,0:T(8,128)(2,1)S(1)}, u32[]{:S(2)}, u32[]{:S(2)}) %collective-permute-start.2) | collective-permute-done | bytes 524320 | tf_op jit(solution)/shard_map/ppermute | solution.py:36
  38.1 2.4 collective-permute-start.5
  40.6 9.2 %all-to-all-done = bf16[8,144,256]{2,1,0:T(8,128)(2,1)} async-done(((bf16[8,144,256]{2,1,0:T(8,128)(2,1)}), bf16[8,144,256]{2,1,0:T(8,128)(2,1)}, u32[]{:S(2)}, u32[]{:S(2)}) %all-to-all-start) | async-done | bytes 589856 | tf_op jit(solution)/shard_map/all_to_all | solution.py:538
  52.4 1.1 constant_dynamic-update-slice_fusion.part_2
  53.4 1.7 collective-permute-start.6
  55.2 1.8 constant_dynamic-slice_fusion.6
  59.7 1.7 convolution_convert_fusion
  61.5 11.5 %attention_forward.1 = (bf16[16,64,128]{2,1,0:T(8,128)(2,1)}, f32[64,2048]{1,0:T(8,128)S(1)}, f32[1,2048]{1,0:T(1,128)S(1)}) custom-call(s32[16]{0:T(128)S(1)} %stack.142.place, bf16[192,2048]{1,0:T(8,128)(2,1)S(1)} %pad_maximum_fusion.3.q_ref.k_ref.v_ref, bf16[192,2048]{1,0:T(8,128)(2,1)S(1)} %pad_maximum_fusion.3.q_ref.k_ref.v_ref, ...), custom_call_target="tpu_custom_call" | custom-call | flops 4294967296 | bytes 1310720 | tf_op jit(solution)/shard_map/attention_forward/pallas_call | solution.py:70
  74.4 4.5 %all-to-all-start.1 = ((bf16[16,64,128]{2,1,0:T(8,128)(2,1)}), bf16[16,64,128]{2,1,0:T(8,128)(2,1)S(1)}, u32[]{:S(2)}, u32[]{:S(2)}) async-start(bf16[16,64,128]{2,1,0:T(8,128)(2,1)} %get-tuple-element.69), calls=%async_computation.1 | async-start | bytes 524288 | tf_op jit(solution)/shard_map/all_to_all | solution.py:558
  79.6 1.2 copy.24
  81.5 9.1 %all-to-all-done.1.att_ref = bf16[16,64,128]{2,1,0:T(8,128)(2,1)S(1)} async-done(((bf16[16,64,128]{2,1,0:T(8,128)(2,1)}), bf16[16,64,128]{2,1,0:T(8,128)(2,1)S(1)}, u32[]{:S(2)}, u32[]{:S(2)}) %all-to-all-start.1) | async-done | bytes 262176 | tf_op jit(solution)/shard_map/all_to_all | solution.py:558
  90.5 4.9 %all-gather.3.cloned.1.call-done.out_ref = bf16[1024,3072]{1,0:T(8,128)(2,1)} async-done(((bf16[128,3072]{1,0:T(8,128)(2,1)}), bf16[1024,3072]{1,0:T(8,128)(2,1)}) %all-gather.3.cloned.1.call-update) | async-done | bytes 6291472 | tf_op jit(solution)/shard_map/all_gather | solution.py:542
  95.4 4.1 %out_and_norm.1 = (bf16[128,1024]{1,0:T(8,128)(2,1)}, bf16[128,1024]{1,0:T(8,128)(2,1)}, f32[128,1024]{1,0:T(8,128)}, f32[128,1024]{1,0:T(8,128)}, f32[128,128]{1,0:T(8,128)}) custom-call(s32[2]{0:T(128)} %pad_add_fusion.spots, bf16[16,64,128]{2,1,0:T(8,128)(2,1)} %copy-done.16, bf16[1024,3072]{1,0:T(8,128)(2,1)} %all-gather.3.cloned.1.call-done.out_ref, ...), custom_call_target="tpu_custom_call" | custom-call | tf_op jit(solution)/shard_map/out_and_norm/pallas_call | solution.py:338
  99.5 1.3 collective-permute-start.7
  101.8 5.1 %collective-permute-done.7 = bf16[128,1024]{1,0:T(8,128)(2,1)S(1)} collective-permute-done((bf16[128,1024]{1,0:T(8,128)(2,1)}, bf16[128,1024]{1,0:T(8,128)(2,1)S(1)}, u32[]{:S(2)}, u32[]{:S(2)}) %collective-permute-start.7) | collective-permute-done | bytes 262176 | tf_op jit(solution)/shard_map/ppermute | solution.py:32
  106.9 1.6 collective-permute-start.8
  108.5 1.7 constant_dynamic-update-slice_fusion.6
  110.3 1.8 constant_dynamic-update-slice_fusion.5.hid_a
  113.2 2.6 multiply_convert_fusion.1
  118.4 1.4 collective-permute-start.12
  121.3 5.0 %collective-permute-done.12 = bf16[128,1024]{1,0:T(8,128)(2,1)S(1)} collective-permute-done((bf16[128,1024]{1,0:T(8,128)(2,1)S(1)}, bf16[128,1024]{1,0:T(8,128)(2,1)S(1)}, u32[]{:S(2)}, u32[]{:S(2)}) %collective-permute-start.12) | collective-permute-done | bytes 262176 | tf_op jit(solution)/shard_map/ppermute | solution.py:32
  127.6 1.4 collective-permute-start.13
  129.0 5.7 %collective-permute-done.13 = bf16[128,1024]{1,0:T(8,128)(2,1)S(1)} collective-permute-done((bf16[128,1024]{1,0:T(8,128)(2,1)S(1)}, bf16[128,1024]{1,0:T(8,128)(2,1)S(1)}, u32[]{:S(2)}, u32[]{:S(2)}) %collective-permute-start.13) | collective-permute-done | bytes 262176 | tf_op jit(solution)/shard_map/ppermute | solution.py:32
  134.7 1.6 collective-permute-start.14
  136.4 1.1 collective-permute-done.14
  145.1 7.0 %ff_products.1 = bf16[1024,2048]{1,0:T(8,128)(2,1)} custom-call(bf16[256,1024]{1,0:T(8,128)(2,1)} %constant_dynamic-update-slice_fusion.5.hid_a, bf16[256,1024]{1,0:T(8,128)(2,1)} %copy-done.14, bf16[256,1024]{1,0:T(8,128)(2,1)} %copy-done.24, bf16[256,1024]{1,0:T(8,128)(2,1)} %copy-done.23, bf16[256,1024]{1,0:T(8,128)(2,1)} %pad_maximum_fusion.7.mixed_a, ...), custom_call_target="tpu_custom_call" | custom-call | flops 2147483648 | bytes 8388608 | tf_op jit(solution)/shard_map/ff_products/pallas_call | solution.py:453
  152.1 1.4 collective-permute-start.18
  153.5 2.3 fusion.56
  155.9 4.1 %collective-permute-done.18.late_ref = bf16[128,1024]{1,0:T(8,128)(2,1)} collective-permute-done((bf16[128,1024]{1,0:T(8,128)(2,1)}, bf16[128,1024]{1,0:T(8,128)(2,1)}, u32[]{:S(2)}, u32[]{:S(2)}) %collective-permute-start.18) | collective-permute-done | bytes 262176 | tf_op jit(solution)/shard_map/ppermute | solution.py:32
  160.0 4.6 %norm_one_back.1 = (f32[128,1024]{1,0:T(8,128)}, bf16[128,1024]{1,0:T(8,128)(2,1)}, bf16[16,64,128]{2,1,0:T(8,128)(2,1)}, f32[2,1024]{1,0:T(2,128)}) custom-call(s32[2]{0:T(128)} %pad_add_fusion.spots, f32[128,1024]{1,0:T(8,128)} %get-tuple-element.125.base_ref, bf16[128,1024]{1,0:T(8,128)(2,1)} %collective-permute-done.18.late_ref, ...), custom_call_target="tpu_custom_call" | custom-call | tf_op jit(solution)/shard_map/norm_one_back/pallas_call | solution.py:338
  164.6 1.7 constant_dynamic-update-slice_fusion.10
  167.0 1.4 collective-permute-start.20
  168.3 7.8 %all-to-all-start.2 = ((bf16[16,64,128]{2,1,0:T(8,128)(2,1)}), bf16[16,64,128]{2,1,0:T(8,128)(2,1)}, u32[]{:S(2)}, u32[]{:S(2)}) async-start(bf16[16,64,128]{2,1,0:T(8,128)(2,1)} %get-tuple-element.85), calls=%async_computation.3 | async-start | bytes 524288 | tf_op jit(solution)/shard_map/all_to_all | solution.py:597
  176.8 2.7 collective-permute-done.20.block_2
  179.5 3.2 %collective-permute-start.21 = (bf16[256,1024]{1,0:T(8,128)(2,1)}, bf16[256,1024]{1,0:T(8,128)(2,1)}, u32[]{:S(2)}, u32[]{:S(2)}) collective-permute-start(bf16[256,1024]{1,0:T(8,128)(2,1)} %collective-permute-done.20.block_2), channel_id=1, source_target_pairs={{0,8},{8,0},{1,9},{9,1},{2,10},{10,2},{3,11},{11,3},{4,12},{12,4},... | collective-permute-start | bytes 1572872 | tf_op jit(solution)/shard_map/ppermute | solution.py:32
  182.7 4.9 %all-to-all-done.2.grad_ref = bf16[16,64,128]{2,1,0:T(8,128)(2,1)} async-done(((bf16[16,64,128]{2,1,0:T(8,128)(2,1)}), bf16[16,64,128]{2,1,0:T(8,128)(2,1)}, u32[]{:S(2)}, u32[]{:S(2)}) %all-to-all-start.2) | async-done | bytes 262176 | tf_op jit(solution)/shard_map/all_to_all | solution.py:597
  187.6 15.3 %attention_backward.1 = (bf16[192,1024]{1,0:T(8,128)(2,1)}, bf16[192,1024]{1,0:T(8,128)(2,1)}, bf16[16,192,128]{2,1,0:T(8,128)(2,1)}) custom-call(s32[16]{0:T(128)} %copy-done.5, bf16[192,2048]{1,0:T(8,128)(2,1)} %copy-done.1, bf16[192,2048]{1,0:T(8,128)(2,1)} %copy-done.1, bf16[192,2048]{1,0:T(8,128)(2,1)} %copy-done.1, ...), custom_call_target="tpu_custom_call" | custom-call | flops 10737418240 | bytes 2621440 | tf_op jit(solution)/shard_map/attention_backward/pallas_call | solution.py:156
  204.8 3.4 %weight_terms.1 = bf16[8,464,128]{2,1,0:T(8,128)(2,1)S(1)} custom-call(s32[1]{0:T(128)} %bitcast.29.spots, bf16[192,1024]{1,0:T(8,128)(2,1)S(1)} %copy-done.2, bf16[192,1024]{1,0:T(8,128)(2,1)S(1)} %copy-done.3, bf16[512,1024]{1,0:T(8,128)(2,1)S(1)} %pad_maximum_fusion.part_0, bf16[512,1024]{1,0:T(8,128)(2,1)S(1)} %collective-permute-done.4.part_1, ...), custom_call_target="tpu_custom_call" | custom-call | tf_op jit(solution)/shard_map/weight_terms/pallas_call | solution.py:338
  209.2 1.6 reduce-scatter.2.cloned.1.call-done
  210.8 2.9 collective-permute-start.22
  213.6 3.6 %all-to-all-start.3 = ((bf16[8,464,128]{2,1,0:T(8,128)(2,1)}), bf16[8,464,128]{2,1,0:T(8,128)(2,1)S(1)}, u32[]{:S(2)}, u32[]{:S(2)}) async-start(bf16[8,464,128]{2,1,0:T(8,128)(2,1)} %copy-done), calls=%async_computation.4 | async-start | bytes 1900544 | tf_op jit(solution)/shard_map/all_to_all | solution.py:609
  217.2 8.1 %collective-permute-done.22 = bf16[128,2048]{1,0:T(8,128)(2,1)S(1)} collective-permute-done((bf16[128,2048]{1,0:T(8,128)(2,1)}, bf16[128,2048]{1,0:T(8,128)(2,1)S(1)}, u32[]{:S(2)}, u32[]{:S(2)}) %collective-permute-start.22) | collective-permute-done | bytes 524320 | tf_op jit(solution)/shard_map/ppermute | solution.py:32
  225.5 5.3 %all-to-all-done.3 = bf16[8,464,128]{2,1,0:T(8,128)(2,1)S(1)} async-done(((bf16[8,464,128]{2,1,0:T(8,128)(2,1)}), bf16[8,464,128]{2,1,0:T(8,128)(2,1)S(1)}, u32[]{:S(2)}, u32[]{:S(2)}) %all-to-all-start.3) | async-done | bytes 950304 | tf_op jit(solution)/shard_map/all_to_all | solution.py:609
  230.8 2.4 collective-permute-start.23
  234.0 6.1 %all-to-all-start.4 = ((bf16[16,192,128]{2,1,0:T(8,128)(2,1)}), bf16[16,192,128]{2,1,0:T(8,128)(2,1)S(1)}, u32[]{:S(2)}, u32[]{:S(2)}) async-start(bf16[16,192,128]{2,1,0:T(8,128)(2,1)} %get-tuple-element.96), calls=%async_computation.5 | async-start | bytes 1572864 | tf_op jit(solution)/shard_map/all_to_all | solution.py:624
  240.1 7.2 %collective-permute-done.24 = bf16[464,128]{1,0:T(8,128)(2,1)S(1)} collective-permute-done((bf16[464,128]{1,0:T(8,128)(2,1)S(1)}, bf16[464,128]{1,0:T(8,128)(2,1)S(1)}, u32[]{:S(2)}, u32[]{:S(2)}) %collective-permute-start.24) | collective-permute-done | bytes 118816 | tf_op jit(solution)/shard_map/ppermute | solution.py:32
  247.4 9.3 %all-to-all-done.4.every_ref = bf16[16,192,128]{2,1,0:T(8,128)(2,1)S(1)} async-done(((bf16[16,192,128]{2,1,0:T(8,128)(2,1)}), bf16[16,192,128]{2,1,0:T(8,128)(2,1)S(1)}, u32[]{:S(2)}, u32[]{:S(2)}) %all-to-all-start.4) | async-done | bytes 786464 | tf_op jit(solution)/shard_map/all_to_all | solution.py:624
  256.7 1.4 collective-permute-start.27
  258.1 4.4 %collective-permute-done.27 = bf16[656,128]{1,0:T(8,128)(2,1)S(1)} collective-permute-done((bf16[656,128]{1,0:T(8,128)(2,1)S(1)}, bf16[656,128]{1,0:T(8,128)(2,1)S(1)}, u32[]{:S(2)}, u32[]{:S(2)}) %collective-permute-start.27) | collective-permute-done | bytes 167968 | tf_op jit(solution)/shard_map/ppermute | solution.py:32
  263.0 1.1 collective-permute-start.25
  264.1 6.2 %input_product.1 = f32[128,1024]{1,0:T(8,128)} custom-call(s32[2]{0:T(128)} %pad_add_fusion.spots, bf16[16,192,128]{2,1,0:T(8,128)(2,1)} %copy-done.11, bf16[1024,1536]{1,0:T(8,128)(2,1)} %all-gather.5.cloned.1.call-done.own_ref, bf16[1024,1536]{1,0:T(8,128)(2,1)} %collective-permute-done.26.pair_ref, f32[128,1024]{1,0:T(8,128)} %get-tuple-element.101.base_ref), custom_call_target="tpu_custom_call" | custom-call | tf_op jit(solution)/shard_map/input_product/pallas_call | solution.py:299
  270.4 8.9 %collective-permute-done.25 = bf16[128,2048]{1,0:T(8,128)(2,1)S(1)} collective-permute-done((bf16[128,2048]{1,0:T(8,128)(2,1)S(1)}, bf16[128,2048]{1,0:T(8,128)(2,1)S(1)}, u32[]{:S(2)}, u32[]{:S(2)}) %collective-permute-start.25) | collective-permute-done | bytes 524320 | tf_op jit(solution)/shard_map/ppermute | solution.py:32
  279.3 3.5 %collective-permute-start.30 = (bf16[256,2048]{1,0:T(8,128)(2,1)S(1)}, bf16[256,2048]{1,0:T(8,128)(2,1)}, u32[]{:S(2)}, u32[]{:S(2)}) collective-permute-start(bf16[256,2048]{1,0:T(8,128)(2,1)S(1)} %pad_maximum_fusion.1.own_ref), channel_id=1, source_target_pairs={{0,8},{8,0},{1,9},{9,1},{2,10},{10,2},{3,11},{11,3},{4,12},{12,4},... | collective-permute-start | bytes 3145736 | tf_op jit(solution)/shard_map/ppermute | solution.py:32
  283.1 2.8 collective-permute-done.29.pair_ref
  285.9 2.3 assemble_rest.1
  288.7 4.0 %assemble.1 = (f32[128,4096]{1,0:T(8,128)}, f32[128,4096]{1,0:T(8,128)}) custom-call(s32[4]{0:T(128)S(1)} %pad_add_fusion.1.spots, bf16[256,2048]{1,0:T(8,128)(2,1)S(1)} %pad_maximum_fusion.1.own_ref, bf16[256,2048]{1,0:T(8,128)(2,1)} %collective-permute-done.30.pair_ref), custom_call_target="tpu_custom_call" | custom-call | tf_op jit(solution)/shard_map/assemble/pallas_call | solution.py:338
  (163 shorter events, 33.9 us)
Async XLA Ops:
  7.2 3.2 %copy-start.26 = (bf16[128]{0:T(256)(128)(2,1)S(1)}, bf16[128]{0:T(256)(128)(2,1)}, u32[]{:S(2)}) copy-start(bf16[128]{0:T(256)(128)(2,1)} %param.18) | copy-start | bytes 772
  7.2 3.2 %copy-start.27 = (bf16[128]{0:T(256)(128)(2,1)S(1)}, bf16[128]{0:T(256)(128)(2,1)}, u32[]{:S(2)}) copy-start(bf16[128]{0:T(256)(128)(2,1)} %param.17) | copy-start | bytes 772
  7.2 3.2 %copy-start.28 = (bf16[128]{0:T(256)(128)(2,1)S(1)}, bf16[128]{0:T(256)(128)(2,1)}, u32[]{:S(2)}) copy-start(bf16[128]{0:T(256)(128)(2,1)} %param.16) | copy-start | bytes 772
  7.2 3.2 %copy-start.29 = (bf16[128]{0:T(256)(128)(2,1)S(1)}, bf16[128]{0:T(256)(128)(2,1)}, u32[]{:S(2)}) copy-start(bf16[128]{0:T(256)(128)(2,1)} %param.15) | copy-start | bytes 772
  7.2 88.2 %all-gather.3.cloned.1.call-start = ((), (), s32[]{:S(2)}) async-start(), calls=%async_computation.6 | async-start | bytes 7077888 | tf_op jit(solution)/shard_map/all_gather | solution.py:542
  8.3 4.1 %copy-start.12 = (bf16[1,128,1024]{2,1,0:T(8,128)(2,1)S(1)}, bf16[1,128,1024]{2,1,0:T(8,128)(2,1)}, u32[]{:S(2)}) copy-start(bf16[1,128,1024]{2,1,0:T(8,128)(2,1)} %param.10) | copy-start | bytes 786436
  12.5 9.1 %collective-permute-start = (bf16[128,1024]{1,0:T(8,128)(2,1)S(1)}, bf16[128,1024]{1,0:T(8,128)(2,1)S(1)}, u32[]{:S(2)}, u32[]{:S(2)}) collective-permute-start(bf16[128,1024]{1,0:T(8,128)(2,1)S(1)} %bitcast.105), channel_id=1, source_target_pairs={{0,16},{16,0},{1,17},{17,1},{2,18},{18,2},{3,19},{19,3},{4,20},{20... | collective-permute-start | bytes 786440 | tf_op jit(solution)/shard_map/ppermute | solution.py:32
  16.0 7.1 %collective-permute-start.1 = (bf16[128,1024]{1,0:T(8,128)(2,1)S(1)}, bf16[128,1024]{1,0:T(8,128)(2,1)S(1)}, u32[]{:S(2)}, u32[]{:S(2)}) collective-permute-start(bf16[128,1024]{1,0:T(8,128)(2,1)S(1)} %bitcast.106), channel_id=1, source_target_pairs={{0,32},{32,0},{64,96},{96,64},{1,33},{33,1},{65,97},{97,65},{2,34}... | collective-permute-start | bytes 786440 | tf_op jit(solution)/shard_map/ppermute | solution.py:36
  21.6 16.5 %copy-start.17 = (bf16[128,1024]{1,0:T(8,128)(2,1)}, bf16[128,1024]{1,0:T(8,128)(2,1)S(1)}, u32[]{:S(2)}) copy-start(bf16[128,1024]{1,0:T(8,128)(2,1)S(1)} %collective-permute-done) | copy-start | bytes 786436
  23.1 14.1 %collective-permute-start.2 = (bf16[256,1024]{1,0:T(8,128)(2,1)S(1)}, bf16[256,1024]{1,0:T(8,128)(2,1)S(1)}, u32[]{:S(2)}, u32[]{:S(2)}) collective-permute-start(bf16[256,1024]{1,0:T(8,128)(2,1)S(1)} %pad_maximum_fusion.5), channel_id=1, source_target_pairs={{0,96},{32,64},{64,32},{96,0},{1,97},{33,65},{65,33},{97,1},{2,98}... | collective-permute-start | bytes 1572872 | tf_op jit(solution)/shard_map/ppermute | solution.py:36
  26.8 5.8 %collective-permute-start.3 = (bf16[128,1024]{1,0:T(8,128)(2,1)S(1)}, bf16[128,1024]{1,0:T(8,128)(2,1)S(1)}, u32[]{:S(2)}, u32[]{:S(2)}) collective-permute-start(bf16[128,1024]{1,0:T(8,128)(2,1)S(1)} %collective-permute-done), channel_id=1, source_target_pairs={{0,32},{32,0},{64,96},{96,64},{1,33},{33,1},{65,97},{97,65},{2,34}... | collective-permute-start | bytes 786440 | tf_op jit(solution)/shard_map/ppermute | solution.py:36
  26.8 22.9 %all-to-all-start = ((bf16[8,144,256]{2,1,0:T(8,128)(2,1)}), bf16[8,144,256]{2,1,0:T(8,128)(2,1)}, u32[]{:S(2)}, u32[]{:S(2)}) async-start(bf16[8,144,256]{2,1,0:T(8,128)(2,1)} %broadcast_in_dim.8), calls=%async_computation | async-start | bytes 1179648 | tf_op jit(solution)/shard_map/all_to_all | solution.py:538
  32.5 5.5 %copy-start.18 = (bf16[128,1024]{1,0:T(8,128)(2,1)}, bf16[128,1024]{1,0:T(8,128)(2,1)S(1)}, u32[]{:S(2)}) copy-start(bf16[128,1024]{1,0:T(8,128)(2,1)S(1)} %collective-permute-done.3) | copy-start | bytes 786436
  38.1 14.3 %collective-permute-start.5 = (bf16[256,1024]{1,0:T(8,128)(2,1)}, bf16[256,1024]{1,0:T(8,128)(2,1)}, u32[]{:S(2)}, u32[]{:S(2)}) collective-permute-start(bf16[256,1024]{1,0:T(8,128)(2,1)} %pad_maximum_fusion.6), channel_id=1, source_target_pairs={{0,96},{32,64},{64,32},{96,0},{1,97},{33,65},{65,33},{97,1},{2,98}... | collective-permute-start | bytes 1572872 | tf_op jit(solution)/shard_map/ppermute | solution.py:36
  49.7 9.4 %collective-permute-start.4 = (bf16[512,1024]{1,0:T(8,128)(2,1)S(1)}, bf16[512,1024]{1,0:T(8,128)(2,1)S(1)}, u32[]{:S(2)}, u32[]{:S(2)}) collective-permute-start(bf16[512,1024]{1,0:T(8,128)(2,1)S(1)} %pad_maximum_fusion.part_0), channel_id=1, source_target_pairs={{0,8},{8,0},{1,9},{9,1},{2,10},{10,2},{3,11},{11,3},{4,12},{12,4},... | collective-permute-start | bytes 3145736 | tf_op jit(solution)/shard_map/ppermute | solution.py:32
  53.4 6.2 %collective-permute-start.6 = (bf16[512,1024]{1,0:T(8,128)(2,1)S(1)}, bf16[512,1024]{1,0:T(8,128)(2,1)}, u32[]{:S(2)}, u32[]{:S(2)}) collective-permute-start(bf16[512,1024]{1,0:T(8,128)(2,1)S(1)} %constant_dynamic-update-slice_fusion.part_2), channel_id=1, source_target_pairs={{0,8},{8,0},{1,9},{9,1},{2,10},{10,2},{3,11},{11,3},{4,12},{12,4},... | collective-permute-start | bytes 3145736 | tf_op jit(solution)/shard_map/ppermute | solution.py:32
  55.2 6.3 %copy-start.5 = (s32[16]{0:T(128)}, s32[16]{0:T(128)S(1)}, u32[]{:S(2)}) copy-start(s32[16]{0:T(128)S(1)} %stack.142.place) | copy-start | bytes 196
  61.5 11.5 %copy-start.1 = (bf16[192,2048]{1,0:T(8,128)(2,1)}, bf16[192,2048]{1,0:T(8,128)(2,1)S(1)}, u32[]{:S(2)}) copy-start(bf16[192,2048]{1,0:T(8,128)(2,1)S(1)} %pad_maximum_fusion.3.q_ref.k_ref.v_ref) | copy-start | bytes 2359300
  74.4 16.1 %all-to-all-start.1 = ((bf16[16,64,128]{2,1,0:T(8,128)(2,1)}), bf16[16,64,128]{2,1,0:T(8,128)(2,1)S(1)}, u32[]{:S(2)}, u32[]{:S(2)}) async-start(bf16[16,64,128]{2,1,0:T(8,128)(2,1)} %get-tuple-element.69), calls=%async_computation.1 | async-start | bytes 524288 | tf_op jit(solution)/shard_map/all_to_all | solution.py:558
  79.0 81.0 %all-gather.5.cloned.1.call-start = ((), (), s32[]{:S(2)}) async-start(), calls=%async_computation.8 | async-start | bytes 3538944 | tf_op jit(solution)/shard_map/all_gather | solution.py:563
  90.5 4.9 %copy-start.16 = (bf16[16,64,128]{2,1,0:T(8,128)(2,1)}, bf16[16,64,128]{2,1,0:T(8,128)(2,1)S(1)}, u32[]{:S(2)}) copy-start(bf16[16,64,128]{2,1,0:T(8,128)(2,1)S(1)} %all-to-all-done.1.att_ref) | copy-start | bytes 786436
  99.5 7.4 %collective-permute-start.7 = (bf16[128,1024]{1,0:T(8,128)(2,1)}, bf16[128,1024]{1,0:T(8,128)(2,1)S(1)}, u32[]{:S(2)}, u32[]{:S(2)}) collective-permute-start(bf16[128,1024]{1,0:T(8,128)(2,1)} %get-tuple-element.73), channel_id=1, source_target_pairs={{0,32},{32,0},{1,33},{33,1},{2,34},{34,2},{3,35},{35,3},{4,36},{36... | collective-permute-start | bytes 786440 | tf_op jit(solution)/shard_map/ppermute | solution.py:32
  100.9 9.4 %collective-permute-start.10 = (bf16[128,1024]{1,0:T(8,128)(2,1)}, bf16[128,1024]{1,0:T(8,128)(2,1)}, u32[]{:S(2)}, u32[]{:S(2)}) collective-permute-start(bf16[128,1024]{1,0:T(8,128)(2,1)} %get-tuple-element.73), channel_id=1, source_target_pairs={{0,8},{8,0},{1,9},{9,1},{2,10},{10,2},{3,11},{11,3},{4,12},{12,4},... | collective-permute-start | bytes 786440 | tf_op jit(solution)/shard_map/ppermute | solution.py:32
  106.9 5.2 %collective-permute-start.8 = (bf16[128,1024]{1,0:T(8,128)(2,1)S(1)}, bf16[128,1024]{1,0:T(8,128)(2,1)}, u32[]{:S(2)}, u32[]{:S(2)}) collective-permute-start(bf16[128,1024]{1,0:T(8,128)(2,1)S(1)} %collective-permute-done.7), channel_id=1, source_target_pairs={{0,8},{8,0},{1,9},{9,1},{2,10},{10,2},{3,11},{11,3},{4,12},{12,4},... | collective-permute-start | bytes 786440 | tf_op jit(solution)/shard_map/ppermute | solution.py:32
  110.2 100.6 %reduce-scatter.2.cloned.1.call-start = ((), (), s32[]{:S(2)}) async-start(), calls=%async_computation.7 | async-start | bytes 4718592 | tf_op jit(solution)/shard_map/reduce_scatter | solution.py:592
  110.2 5.6 %copy-start.8 = (bf16[1024,3072]{1,0:T(8,128)(2,1)S(1)}, bf16[1024,3072]{1,0:T(8,128)(2,1)}, u32[]{:S(2)}) copy-start(bf16[1024,3072]{1,0:T(8,128)(2,1)} %all-gather.3.cloned.1.call-done.out_ref) | copy-start | bytes 18874372
  113.2 2.6 copy-start.14
  115.8 1.2 copy-start.13
  116.7 1.6 collective-permute-start.9
  117.8 2.7 copy-start.21
  118.3 8.0 %copy-start.22 = (f32[128,1024]{1,0:T(8,128)S(1)}, f32[128,1024]{1,0:T(8,128)}, u32[]{:S(2)}) copy-start(f32[128,1024]{1,0:T(8,128)} %get-tuple-element.72) | copy-start | bytes 1572868
  118.4 8.0 %collective-permute-start.12 = (bf16[128,1024]{1,0:T(8,128)(2,1)S(1)}, bf16[128,1024]{1,0:T(8,128)(2,1)S(1)}, u32[]{:S(2)}, u32[]{:S(2)}) collective-permute-start(bf16[128,1024]{1,0:T(8,128)(2,1)S(1)} %fusion.40), channel_id=1, source_target_pairs={{0,32},{32,0},{1,33},{33,1},{2,34},{34,2},{3,35},{35,3},{4,36},{36... | collective-permute-start | bytes 786440 | tf_op jit(solution)/shard_map/ppermute | solution.py:32
  120.6 6.2 %copy-start.10 = (bf16[1,128,1024]{2,1,0:T(8,128)(2,1)S(1)}, bf16[1,128,1024]{2,1,0:T(8,128)(2,1)}, u32[]{:S(2)}) copy-start(bf16[1,128,1024]{2,1,0:T(8,128)(2,1)} %param.19) | copy-start | bytes 786436
  120.6 5.7 %collective-permute-start.11 = (bf16[128,1024]{1,0:T(8,128)(2,1)S(1)}, bf16[128,1024]{1,0:T(8,128)(2,1)S(1)}, u32[]{:S(2)}, u32[]{:S(2)}) collective-permute-start(bf16[128,1024]{1,0:T(8,128)(2,1)S(1)} %slice.193), channel_id=1, source_target_pairs={{0,8},{8,0},{1,9},{9,1},{2,10},{10,2},{3,11},{11,3},{4,12},{12,4},... | collective-permute-start | bytes 786440 | tf_op jit(solution)/shard_map/ppermute | solution.py:32
  127.6 7.2 %collective-permute-start.13 = (bf16[128,1024]{1,0:T(8,128)(2,1)S(1)}, bf16[128,1024]{1,0:T(8,128)(2,1)S(1)}, u32[]{:S(2)}, u32[]{:S(2)}) collective-permute-start(bf16[128,1024]{1,0:T(8,128)(2,1)S(1)} %fusion.57), channel_id=1, source_target_pairs={{0,32},{32,0},{1,33},{33,1},{2,34},{34,2},{3,35},{35,3},{4,36},{36... | collective-permute-start | bytes 786440 | tf_op jit(solution)/shard_map/ppermute | solution.py:32
  134.7 2.8 collective-permute-start.14
  136.4 3.5 %collective-permute-start.16 = (bf16[128,1024]{1,0:T(8,128)(2,1)S(1)}, bf16[128,1024]{1,0:T(8,128)(2,1)S(1)}, u32[]{:S(2)}, u32[]{:S(2)}) collective-permute-start(bf16[128,1024]{1,0:T(8,128)(2,1)S(1)} %fusion.57), channel_id=1, source_target_pairs={{0,8},{8,0},{1,9},{9,1},{2,10},{10,2},{3,11},{11,3},{4,12},{12,4},... | collective-permute-start | bytes 786440 | tf_op jit(solution)/shard_map/ppermute | solution.py:32
  137.5 1.0 copy-start.15
  139.4 1.6 collective-permute-start.15
  140.8 1.8 copy-start.24
  142.6 1.6 collective-permute-start.17
  152.1 7.9 %collective-permute-start.18 = (bf16[128,1024]{1,0:T(8,128)(2,1)}, bf16[128,1024]{1,0:T(8,128)(2,1)}, u32[]{:S(2)}, u32[]{:S(2)}) collective-permute-start(bf16[128,1024]{1,0:T(8,128)(2,1)} %fusion.37), channel_id=1, source_target_pairs={{0,32},{32,0},{1,33},{33,1},{2,34},{34,2},{3,35},{35,3},{4,36},{36... | collective-permute-start | bytes 786440 | tf_op jit(solution)/shard_map/ppermute | solution.py:32
  160.0 6.2 %copy-start.25 = (bf16[128,1024]{1,0:T(8,128)(2,1)S(1)}, bf16[128,1024]{1,0:T(8,128)(2,1)}, u32[]{:S(2)}) copy-start(bf16[128,1024]{1,0:T(8,128)(2,1)} %get-tuple-element.92) | copy-start | bytes 786436
  167.0 12.5 %collective-permute-start.20 = (bf16[256,1024]{1,0:T(8,128)(2,1)}, bf16[256,1024]{1,0:T(8,128)(2,1)}, u32[]{:S(2)}, u32[]{:S(2)}) collective-permute-start(bf16[256,1024]{1,0:T(8,128)(2,1)} %constant_dynamic-update-slice_fusion.9.block_0), channel_id=1, source_target_pairs={{0,32},{32,0},{1,33},{33,1},{2,34},{34,2},{3,35},{35,3},{4,36},{36... | collective-permute-start | bytes 1572872 | tf_op jit(solution)/shard_map/ppermute | solution.py:32
  168.3 19.2 %all-to-all-start.2 = ((bf16[16,64,128]{2,1,0:T(8,128)(2,1)}), bf16[16,64,128]{2,1,0:T(8,128)(2,1)}, u32[]{:S(2)}, u32[]{:S(2)}) async-start(bf16[16,64,128]{2,1,0:T(8,128)(2,1)} %get-tuple-element.85), calls=%async_computation.3 | async-start | bytes 524288 | tf_op jit(solution)/shard_map/all_to_all | solution.py:597
  176.2 26.6 %collective-permute-start.19 = (bf16[256,1024]{1,0:T(8,128)(2,1)}, bf16[256,1024]{1,0:T(8,128)(2,1)}, u32[]{:S(2)}, u32[]{:S(2)}) collective-permute-start(bf16[256,1024]{1,0:T(8,128)(2,1)} %constant_dynamic-update-slice_fusion.9.block_0), channel_id=1, source_target_pairs={{0,8},{8,0},{1,9},{9,1},{2,10},{10,2},{3,11},{11,3},{4,12},{12,4},... | collective-permute-start | bytes 1572872 | tf_op jit(solution)/shard_map/ppermute | solution.py:32
  176.4 87.7 %collective-permute-start.26 = (bf16[1024,1536]{1,0:T(8,128)(2,1)}, bf16[1024,1536]{1,0:T(8,128)(2,1)}, u32[]{:S(2)}, u32[]{:S(2)}) collective-permute-start(bf16[1024,1536]{1,0:T(8,128)(2,1)} %all-gather.5.cloned.1.call-done.own_ref), channel_id=1, source_target_pairs={{0,8},{8,0},{1,9},{9,1},{2,10},{10,2},{3,11},{11,3},{4,12},{12,4},... | collective-permute-start | bytes 9437192 | tf_op jit(solution)/shard_map/ppermute | solution.py:32
  179.5 23.3 %collective-permute-start.21 = (bf16[256,1024]{1,0:T(8,128)(2,1)}, bf16[256,1024]{1,0:T(8,128)(2,1)}, u32[]{:S(2)}, u32[]{:S(2)}) collective-permute-start(bf16[256,1024]{1,0:T(8,128)(2,1)} %collective-permute-done.20.block_2), channel_id=1, source_target_pairs={{0,8},{8,0},{1,9},{9,1},{2,10},{10,2},{3,11},{11,3},{4,12},{12,4},... | collective-permute-start | bytes 1572872 | tf_op jit(solution)/shard_map/ppermute | solution.py:32
  187.6 15.3 %copy-start.4 = (f32[2,1024]{1,0:T(2,128)S(1)}, f32[2,1024]{1,0:T(2,128)}, u32[]{:S(2)}) copy-start(f32[2,1024]{1,0:T(2,128)} %get-tuple-element.93.first_ref) | copy-start | bytes 24580
  202.8 1.0 copy-start.2
  203.8 1.0 copy-start.3
  208.2 0.9 copy-start
  210.8 14.6 %copy-start.19 = (bf16[128,2048]{1,0:T(8,128)(2,1)S(1)}, bf16[128,2048]{1,0:T(8,128)(2,1)}, u32[]{:S(2)}) copy-start(bf16[128,2048]{1,0:T(8,128)(2,1)} %reduce-scatter.2.cloned.1.call-done) | copy-start | bytes 1572868
  210.8 14.6 %collective-permute-start.22 = (bf16[128,2048]{1,0:T(8,128)(2,1)}, bf16[128,2048]{1,0:T(8,128)(2,1)S(1)}, u32[]{:S(2)}, u32[]{:S(2)}) collective-permute-start(bf16[128,2048]{1,0:T(8,128)(2,1)} %reduce-scatter.2.cloned.1.call-done), channel_id=1, source_target_pairs={{0,64},{64,0},{1,65},{65,1},{2,66},{66,2},{3,67},{67,3},{4,68},{68... | collective-permute-start | bytes 1572872 | tf_op jit(solution)/shard_map/ppermute | solution.py:32
  213.6 17.1 %all-to-all-start.3 = ((bf16[8,464,128]{2,1,0:T(8,128)(2,1)}), bf16[8,464,128]{2,1,0:T(8,128)(2,1)S(1)}, u32[]{:S(2)}, u32[]{:S(2)}) async-start(bf16[8,464,128]{2,1,0:T(8,128)(2,1)} %copy-done), calls=%async_computation.4 | async-start | bytes 1900544 | tf_op jit(solution)/shard_map/all_to_all | solution.py:609
  230.8 16.5 %collective-permute-start.23 = (bf16[128,2048]{1,0:T(8,128)(2,1)S(1)}, bf16[128,2048]{1,0:T(8,128)(2,1)S(1)}, u32[]{:S(2)}, u32[]{:S(2)}) collective-permute-start(bf16[128,2048]{1,0:T(8,128)(2,1)S(1)} %add_convert_fusion.1), channel_id=1, source_target_pairs={{0,16},{16,0},{1,17},{17,1},{2,18},{18,2},{3,19},{19,3},{4,20},{20... | collective-permute-start | bytes 1572872 | tf_op jit(solution)/shard_map/ppermute | solution.py:32
  233.3 13.9 %collective-permute-start.24 = (bf16[464,128]{1,0:T(8,128)(2,1)S(1)}, bf16[464,128]{1,0:T(8,128)(2,1)S(1)}, u32[]{:S(2)}, u32[]{:S(2)}) collective-permute-start(bf16[464,128]{1,0:T(8,128)(2,1)S(1)} %reduce_sum.72), channel_id=1, source_target_pairs={{0,16},{16,0},{1,17},{17,1},{2,18},{18,2},{3,19},{19,3},{4,20},{20... | collective-permute-start | bytes 356360 | tf_op jit(solution)/shard_map/ppermute | solution.py:32
  234.0 22.7 %all-to-all-start.4 = ((bf16[16,192,128]{2,1,0:T(8,128)(2,1)}), bf16[16,192,128]{2,1,0:T(8,128)(2,1)S(1)}, u32[]{:S(2)}, u32[]{:S(2)}) async-start(bf16[16,192,128]{2,1,0:T(8,128)(2,1)} %get-tuple-element.96), calls=%async_computation.5 | async-start | bytes 1572864 | tf_op jit(solution)/shard_map/all_to_all | solution.py:624
  256.7 7.4 %copy-start.11 = (bf16[16,192,128]{2,1,0:T(8,128)(2,1)}, bf16[16,192,128]{2,1,0:T(8,128)(2,1)S(1)}, u32[]{:S(2)}) copy-start(bf16[16,192,128]{2,1,0:T(8,128)(2,1)S(1)} %all-to-all-done.4.every_ref) | copy-start | bytes 2359300
  256.7 5.8 %collective-permute-start.27 = (bf16[656,128]{1,0:T(8,128)(2,1)S(1)}, bf16[656,128]{1,0:T(8,128)(2,1)S(1)}, u32[]{:S(2)}, u32[]{:S(2)}) collective-permute-start(bf16[656,128]{1,0:T(8,128)(2,1)S(1)} %pad_maximum_fusion.9), channel_id=1, source_target_pairs={{0,64},{64,0},{1,65},{65,1},{2,66},{66,2},{3,67},{67,3},{4,68},{68... | collective-permute-start | bytes 503816 | tf_op jit(solution)/shard_map/ppermute | solution.py:32
  262.6 7.8 %collective-permute-start.28 = (bf16[1040,128]{1,0:T(8,128)(2,1)S(1)}, bf16[1040,128]{1,0:T(8,128)(2,1)S(1)}, u32[]{:S(2)}, u32[]{:S(2)}) collective-permute-start(bf16[1040,128]{1,0:T(8,128)(2,1)S(1)} %pad_maximum_fusion.8), channel_id=1, source_target_pairs={{0,32},{32,0},{1,33},{33,1},{2,34},{34,2},{3,35},{35,3},{4,36},{36... | collective-permute-start | bytes 798728 | tf_op jit(solution)/shard_map/ppermute | solution.py:32
  263.0 16.2 %collective-permute-start.25 = (bf16[128,2048]{1,0:T(8,128)(2,1)S(1)}, bf16[128,2048]{1,0:T(8,128)(2,1)S(1)}, u32[]{:S(2)}, u32[]{:S(2)}) collective-permute-start(bf16[128,2048]{1,0:T(8,128)(2,1)S(1)} %add_convert_fusion), channel_id=1, source_target_pairs={{0,32},{32,0},{1,33},{33,1},{2,34},{34,2},{3,35},{35,3},{4,36},{36... | collective-permute-start | bytes 1572872 | tf_op jit(solution)/shard_map/ppermute | solution.py:32
  279.3 9.4 %collective-permute-start.30 = (bf16[256,2048]{1,0:T(8,128)(2,1)S(1)}, bf16[256,2048]{1,0:T(8,128)(2,1)}, u32[]{:S(2)}, u32[]{:S(2)}) collective-permute-start(bf16[256,2048]{1,0:T(8,128)(2,1)S(1)} %pad_maximum_fusion.1.own_ref), channel_id=1, source_target_pairs={{0,8},{8,0},{1,9},{9,1},{2,10},{10,2},{3,11},{11,3},{4,12},{12,4},... | collective-permute-start | bytes 3145736 | tf_op jit(solution)/shard_map/ppermute | solution.py:32
  282.8 3.0 %collective-permute-start.29 = (bf16[2080,128]{1,0:T(8,128)(2,1)S(1)}, bf16[2080,128]{1,0:T(8,128)(2,1)S(1)}, u32[]{:S(2)}, u32[]{:S(2)}) collective-permute-start(bf16[2080,128]{1,0:T(8,128)(2,1)S(1)} %pad_maximum_fusion.4.own_ref), channel_id=1, source_target_pairs={{0,8},{8,0},{1,9},{9,1},{2,10},{10,2},{3,11},{11,3},{4,12},{12,4},... | collective-permute-start | bytes 1597448 | tf_op jit(solution)/shard_map/ppermute | solution.py:32
  (5 other events, 3.9 us)
Sparse Core Ops, SparseCore 0:
  10.4 84.9 all-gather.2
  110.3 39.6 all-gather.4
  152.4 58.2 reduce-scatter.1

commit v3 on v2

--- a/solution.py
+++ b/solution.py
@@ -315,13 +315,17 @@
     return (index // 4) * 4 + (index % 2) * 2 + (index // 2) % 2
 
 
-def out_kernel(spots, att_ref, out_ref, x_ref, norms_ref, att_out_ref, low_ref, hid_ref,
-               normal_ref, inverse_ref, rows_scratch):
+def out_kernel(spots, att_ref, own_ref, pair_ref, x_ref, norms_ref, att_out_ref, low_ref, hid_ref,
+               normal_ref, inverse_ref, rows_scratch, branch):
     for head in range(HEADS):
         rows_scratch[head * HEAD_DIM : (head + 1) * HEAD_DIM, :] = att_ref[head_place(head)]
     attended = rows_scratch[...].astype(FULL).T.astype(LOW)
     att_out_ref[...] = attended
-    residual = x_ref[...].astype(FULL) + dot(attended, out_ref[...], 1, 0)
+    half = own_ref.shape[1]
+    for core, part in enumerate((own_ref, pair_ref)):
+        columns = pl.ds(pl.multiple_of(spots[core] * half, half), half)
+        branch[:, columns] = dot(attended, part[...], 1, 0)
+    residual = x_ref[...].astype(FULL) + branch[...]
     normal, inverse = norm_forward(residual)
     hidden = normal * norms_ref[0:1] + norms_ref[1:2]
     hid_ref[...] = hidden
@@ -334,13 +338,13 @@
     return [pl.BlockSpec(s, lambda i, p, n=len(s): (0,) * n) for s in shapes]
 
 
-def local_call(kernel, spots, arrays, outs, scratch, name, specs=None, limit=40):
+def local_call(kernel, spots, arrays, outs, scratch, name, limit=40):
     return pl.pallas_call(
         kernel,
         grid_spec=pltpu.PrefetchScalarGridSpec(
             num_scalar_prefetch=1,
             grid=(1,),
-            in_specs=specs or whole_specs([a.shape for a in arrays]),
+            in_specs=whole_specs([a.shape for a in arrays]),
             out_specs=whole_specs([o.shape for o in outs]),
             scratch_shapes=scratch,
         ),
@@ -350,17 +354,9 @@
     )(spots, *arrays)
 
 
-def out_last(arrays, index):
-    specs = whole_specs([a.shape for a in arrays])
-    width = arrays[index].shape[0]
-    last = arrays[index].shape[1] // width - 1
-    specs[index] = pl.BlockSpec((width, width), lambda i, p: (0, last))
-    return specs
-
-
-def out_and_norm(spots, blocks, rest, inputs, norms):
+def out_and_norm(spots, blocks, out_halves, inputs, norms):
     rows, width = inputs.shape
-    arrays = [blocks, rest, inputs, norms]
+    arrays = [blocks, *out_halves, inputs, norms]
     shape = jax.ShapeDtypeStruct
     return local_call(
         out_kernel,
@@ -373,31 +369,36 @@
             shape((rows, width), FULL),
             shape((rows, BLOCK), FULL),
         ],
-        [pltpu.VMEM((width, rows), LOW)],
+        [pltpu.VMEM((width, rows), LOW), pltpu.VMEM((rows, width), FULL)],
         "out_and_norm",
-        out_last(arrays, 1),
         58,
     )
 
 
-def norm_one_kernel(spots, base_ref, late_ref, normal_ref, inverse_ref, norms_ref, out_ref,
-                    grad_ref, low_ref, blocks_ref, sums_ref, total):
+def norm_one_kernel(spots, base_ref, late_ref, normal_ref, inverse_ref, norms_ref, own_ref,
+                    pair_ref, att_ref, grad_ref, pairs_ref, blocks_ref, sums_ref, total):
     grad = base_ref[...] + late_ref[...].astype(FULL)
     normal = normal_ref[...]
     result, gain_sum, bias_sum = norm_backward(grad, normal, inverse_ref[:, :1], norms_ref[0:1])
     grad_ref[...] = result
-    low_ref[...] = result.astype(LOW)
+    low = result.astype(LOW)
+    pairs_ref[: low.shape[0]] = low
+    pairs_ref[low.shape[0] :] = att_ref[...]
     sums_ref[0:1, :] = gain_sum[None]
     sums_ref[1:2, :] = bias_sum[None]
-    total[...] = dot(out_ref[...], low_ref[...], 1, 1)
+    half = own_ref.shape[1]
+    for core, part in enumerate((own_ref, pair_ref)):
+        columns = pl.ds(pl.multiple_of(spots[core] * half, half), half)
+        term = dot(part[...], pairs_ref[: low.shape[0], columns], 1, 1)
+        total[...] = term if core == 0 else total[...] + term
     for head in range(HEADS):
         rows = slice(head * HEAD_DIM, (head + 1) * HEAD_DIM)
         blocks_ref[head_place(head)] = total[rows, :].astype(LOW)
 
 
-def norm_one_back(spots, base, late, normal, inverse, norms, rest):
+def norm_one_back(spots, base, late, normal, inverse, norms, out_halves, attended_low):
     rows, width = base.shape
-    arrays = [base, late, normal, inverse, norms, rest]
+    arrays = [base, late, normal, inverse, norms, *out_halves, attended_low]
     shape = jax.ShapeDtypeStruct
     return local_call(
         norm_one_kernel,
@@ -405,13 +406,12 @@
         arrays,
         [
             shape((rows, width), FULL),
-            shape((rows, width), LOW),
+            shape((2 * rows, width), LOW),
             shape((HEADS, HEAD_DIM, rows), LOW),
             shape((2, width), FULL),
         ],
         [pltpu.VMEM((width, rows), FULL)],
         "norm_one_back",
-        out_last(arrays, 5),
         58,
     )
 
@@ -482,10 +482,12 @@
     return result, jnp.sum(grad * normal, axis=0), jnp.sum(grad, axis=0)
 
 
-def gather_group(value):
+def gather_group(value, near_work, far_work):
     late = swap(value, "zl")
     near = with_pair(value, "core")
-    return near, with_pair(late, "core")
+    late, near, *done = lax.optimization_barrier((late, near, *near_work(near)))
+    far = with_pair(late, "core")
+    return (near, far), list(zip(done, far_work(far)))
 
 
 def product_group(parts, right, left_dim, right_dim):
@@ -538,7 +540,8 @@
     early = lax.all_to_all(early, FSDP, split_axis=0, concat_axis=0, tiled=True)
     up_mine = lax.dynamic_slice_in_dim(w_up, group * ff_part, ff_part, 1)
     down_mine = lax.dynamic_slice_in_dim(w_down, group * ff_part, ff_part, 1)
-    rest = jnp.concatenate([up_mine, down_mine, w_out], axis=1)
+    out_mine = lax.dynamic_slice_in_dim(w_out, core * (width // 2), width // 2, 1)
+    rest = jnp.concatenate([up_mine, down_mine, out_mine], axis=1)
     rest = lax.all_gather(rest, FSDP, axis=0, tiled=True)
     far, one = together((swap(inputs, "xh"), exchange(inputs, Z, 1)))
     near_two = jnp.concatenate([inputs, one], axis=0)
@@ -557,21 +560,24 @@
     low_blocks, attended, log_total = attention_forward(place, head)
     low_blocks = lax.all_to_all(low_blocks, CTX, split_axis=0, concat_axis=0, tiled=True)
     qkv_mine = lax.dynamic_slice_in_dim(w_qkv, core * (3 * width // 2), 3 * width // 2, 1)
-    rest, qkv_mine, low_blocks = together((rest, qkv_mine, low_blocks))
+    qkv_mine, log_total = together((qkv_mine, log_total))
+    rest, low_blocks = together((rest, low_blocks))
+    out_mine = rest[:, 2 * ff_part :]
+    out_halves = out_mine, swap(out_mine, "core")
     up_part = rest[:, :ff_part]
     down_part = rest[:, ff_part : 2 * ff_part]
     qkv_own = lax.all_gather(qkv_mine, FSDP, axis=0, tiled=True)
     attended_low, hidden_low, hidden, normal_one, inverse_one = out_and_norm(
-        cores, low_blocks, rest, inputs, norms
-    )
-    hidden_low = gather_group(hidden_low)
-    upward = [dot(h, up_part, 1, 0) for h in hidden_low]
-    cdf = [0.5 * (1.0 + lax.erf(u * math.sqrt(0.5))) for u in upward]
-    activated_low = [(u * c).astype(LOW) for u, c in zip(upward, cdf)]
-    slope = [
-        c + u * jnp.exp(-0.5 * u * u) * (1.0 / math.sqrt(2.0 * math.pi))
-        for u, c in zip(upward, cdf)
-    ]
+        cores, low_blocks, out_halves, inputs, norms
+    )
+
+    def raise_part(rows):
+        upward = dot(rows, up_part, 1, 0)
+        cdf = 0.5 * (1.0 + lax.erf(upward * math.sqrt(0.5)))
+        pdf = jnp.exp(-0.5 * upward * upward) * (1.0 / math.sqrt(2.0 * math.pi))
+        return (upward * cdf).astype(LOW), cdf + upward * pdf
+
+    hidden_low, (activated_low, slope) = gather_group(hidden_low, raise_part, raise_part)
     near, late, _ = product_group(activated_low, down_part, 1, 1)
     mixed = hidden + near + late.astype(FULL)
     normal_two, inverse_two = norm_forward(mixed)
@@ -580,22 +586,23 @@
     grad_mixed, gain_two_grad, bias_two_grad = norm_backward(
         cotangent[0].astype(FULL), normal_two, inverse_two, gain_two
     )
-    grad_mixed_low = gather_group(grad_mixed.astype(LOW))
-    grad_upward_low = [
-        (dot(g, down_part, 1, 0) * k).astype(LOW) for g, k in zip(grad_mixed_low, slope)
-    ]
+    lower_near, lower_far = (
+        lambda rows, k=k: ((dot(rows, down_part, 1, 0) * k).astype(LOW),) for k in slope
+    )
+    grad_mixed_low, (grad_upward_low,) = gather_group(
+        grad_mixed.astype(LOW), lower_near, lower_far
+    )
     near, late, sent = product_group(grad_upward_low, up_part, 1, 1)
-    late, qkv_own = together((late, qkv_own))
-    qkv_pair = swap(qkv_own, "core")
     near, *held = together((near, *hidden_low))
     ff_terms = ff_products(held, grad_upward_low, grad_mixed_low, activated_low)
     ff_share = lax.psum_scatter(ff_terms, FSDP, scatter_dimension=0, tiled=True)
 
-    grad_residual, grad_residual_low, grad_blocks, norm_one_sums = norm_one_back(
-        cores, grad_mixed + near, late, normal_one, inverse_one, norms, rest
+    grad_residual, pairs, grad_blocks, norm_one_sums = norm_one_back(
+        cores, grad_mixed + near, late, normal_one, inverse_one, norms, out_halves, attended_low
     )
     grad_blocks = lax.all_to_all(grad_blocks, CTX, split_axis=0, concat_axis=0, tiled=True)
-    pairs = jnp.concatenate([grad_residual_low, attended_low], axis=0)
+    pairs, qkv_own = together((pairs, qkv_own))
+    qkv_pair = swap(qkv_own, "core")
     late_pairs = swap(pairs, "zl")
     blocks = [pairs, swap(pairs, "core"), late_pairs, swap(late_pairs, "core")]
 
@@ -618,17 +625,16 @@
         summed = out_part.astype(FULL) + theirs[count:].astype(FULL)
         return jnp.concatenate([qkv_part, theirs[:count]], axis=0), summed.astype(LOW)
 
-    ff_share, grad_out = together((ff_share, grad_out, terms))[:2]
-    ff_sum, shares = together((sum_pair(ff_share, "zh"), shares))
+    ff_share, grad_out, shares = together((ff_share, grad_out, shares))
+    every = lax.all_to_all(grad_out, CTX, split_axis=0, concat_axis=0, tiled=True)
     shares = jnp.sum(shares.astype(FULL), axis=0).astype(LOW)
-    every = lax.all_to_all(grad_out, CTX, split_axis=0, concat_axis=0, tiled=True)
-    ff_sum, every, *sums = together(
-        (sum_pair(ff_sum, "xh"), every, *spread(shares[:size], shares[size:], "xh"))
-    )
+    every, *sums = together((every, *spread(shares[:size], shares[size:], "xh")))
+    sums = spread(*sums, "zh")
+    ff_sum = sum_pair(sum_pair(ff_share, "zh"), "xh")
+    ff_sum, every, *sums = together((ff_sum, every, *sums))
     input_grad = input_product(cores, every, qkv_own, qkv_pair, grad_residual)
-    rest_sum = jnp.concatenate(spread(*sums, "zh"), axis=0)
     ff_sum, input_grad, rest_sum = together(
-        (with_pair(ff_sum, "zl"), input_grad, with_pair(rest_sum, "zl"))
+        (with_pair(ff_sum, "zl"), input_grad, with_pair(jnp.concatenate(sums, axis=0), "zl"))
     )
     ff_pair, rest_pair = swap(ff_sum, "core"), swap(rest_sum, "core")
     spots = [

time: 301 us -> 292 us (0.970)
  waiting for transfers between devices: 112 us -> 91.8 us
  blocking collectives: 0 us -> 15 us
  starting transfers between devices: 69.1 us -> 61.7 us
  matrix products: 11.7 us -> 17.1 us
    all_to_all x0 -> x1, blocking collectives: none -> 15 us  [per_device(): lax.all_to_all(low_blocks, CTX, split_axis=0, concat_axis=0, tiled=True)]
    all_to_all x1 -> x0, waiting for transfers between devices: 9.06 us -> none  [per_device(): lax.all_to_all(low_blocks, CTX, split_axis=0, concat_axis=0, tiled=True)]
    all_to_all x1, waiting for transfers between devices: 5.29 us -> 12.4 us  [per_device(): lax.all_to_all(terms, FSDP, split_axis=0, concat_axis=0, tiled=True)]
    all_to_all x1, waiting for transfers between devices: 9.27 us -> 3.43 us  [per_device(): lax.all_to_all(grad_out, CTX, split_axis=0, concat_axis=0, tiled=True)]
    dot_general x12, matrix products: 11.7 us -> 17.1 us  [dot(): lax.dot_general(left, right, (((left_dim,), (right_dim,)), ((), ())), pre...]
    all_gather x1, waiting for transfers between devices: 4.85 us -> 0.01 us  [per_device(): rest = lax.all_gather(rest, FSDP, axis=0, tiled=True)]
    all_to_all x1 -> x0, starting transfers between devices: 4.53 us -> none  [per_device(): lax.all_to_all(low_blocks, CTX, split_axis=0, concat_axis=0, tiled=True)]
    all_to_all x1, waiting for transfers between devices: 4.86 us -> 0.36 us  [per_device(): lax.all_to_all(grad_blocks, CTX, split_axis=0, concat_axis=0, tiled=True)]
  transfers between devices with their start and end apart: 39 -> 39, of which waited for: 25 -> 26; matrix products, arithmetic and copies ran while one was open for 13% -> 12% of each run, Pallas kernels for 17% -> 17%
where the time goes in v3:
time: 292 us; the launch traced here: 290 us
  waiting for transfers between devices  91.8 us (31%)
  starting transfers between devices  61.7 us (21%)
  Pallas kernels  57.6 us (20%)
  local copies, waits for them, and re-layouts  22.2 us (8%)
  matrix products  17.1 us (6%)
  blocking collectives  15 us (5%)
  between operations  14.6 us (5%)
  other arithmetic  10.3 us (4%)
    ppermute x28, waiting for transfers between devices, swap(): return lax.ppermute(value, axis, [(0, 1), (1, 0)])  58.4 us
    ppermute x28, starting transfers between devices, swap(): return lax.ppermute(value, axis, [(0, 1), (1, 0)])  35.6 us
    pallas_call x5, Pallas kernels, local_call(): pl.pallas_call(kernel, grid_spec=pltpu.PrefetchScalarGridSpec(num_scalar_...  18.3 us
    dot_general x12, matrix products, dot(): lax.dot_general(left, right, (((left_dim,), (right_dim,)), ((), ())), pre...  17.1 us
    pallas_call x1, Pallas kernels, attention_backward(): pl.pallas_call(backward_kernel, grid_spec=pltpu.PrefetchScalarGridSpec(nu...  15.3 us
    all_to_all x1, blocking collectives, per_device(): lax.all_to_all(low_blocks, CTX, split_axis=0, concat_axis=0, tiled=True)  15 us
    all_to_all x1, waiting for transfers between devices, per_device(): lax.all_to_all(terms, FSDP, split_axis=0, concat_axis=0, tiled=True)  12.4 us
    pallas_call x1, Pallas kernels, attention_forward(): pl.pallas_call(forward_kernel, grid_spec=pltpu.PrefetchScalarGridSpec(num...  10.8 us
  transfers between devices with their start and end apart: 39, of which 26 were waited for; matrix products, arithmetic and copies ran while one was open for 12% of the time, Pallas kernels for 17%

profile of v3, /device:TPU:1, one launch (start us, length us, event | category | flops | bytes accessed | tf_op | source)
XLA Modules:
  0.0 290.3 jit_solution(13763511286331237956)
XLA Ops:
  8.2 1.1 constant_dynamic-slice_fusion.8
  10.3 1.1 constant_dynamic-slice_fusion.6
  12.3 3.6 %collective-permute-start = (bf16[128,1024]{1,0:T(8,128)(2,1)S(1)}, bf16[128,1024]{1,0:T(8,128)(2,1)S(1)}, u32[]{:S(2)}, u32[]{:S(2)}) collective-permute-start(bf16[128,1024]{1,0:T(8,128)(2,1)S(1)} %bitcast.105), channel_id=1, source_target_pairs={{0,16},{16,0},{1,17},{17,1},{2,18},{18,2},{3,19},{19,3},{4,20},{20... | collective-permute-start | bytes 786440 | tf_op jit(solution)/shard_map/ppermute | solution.py:32
  15.9 1.7 collective-permute-start.1
  17.6 3.8 %collective-permute-done = bf16[128,1024]{1,0:T(8,128)(2,1)S(1)} collective-permute-done((bf16[128,1024]{1,0:T(8,128)(2,1)S(1)}, bf16[128,1024]{1,0:T(8,128)(2,1)S(1)}, u32[]{:S(2)}, u32[]{:S(2)}) %collective-permute-start) | collective-permute-done | bytes 262176 | tf_op jit(solution)/shard_map/ppermute | solution.py:32
  21.5 1.8 collective-permute-done.1
  23.3 3.3 %collective-permute-start.2 = (bf16[256,1024]{1,0:T(8,128)(2,1)S(1)}, bf16[256,1024]{1,0:T(8,128)(2,1)S(1)}, u32[]{:S(2)}, u32[]{:S(2)}) collective-permute-start(bf16[256,1024]{1,0:T(8,128)(2,1)S(1)} %pad_maximum_fusion.5), channel_id=1, source_target_pairs={{0,96},{32,64},{64,32},{96,0},{1,97},{33,65},{65,33},{97,1},{2,98}... | collective-permute-start | bytes 1572872 | tf_op jit(solution)/shard_map/ppermute | solution.py:36
  26.6 4.3 %all-to-all-start = ((bf16[8,144,256]{2,1,0:T(8,128)(2,1)}), bf16[8,144,256]{2,1,0:T(8,128)(2,1)}, u32[]{:S(2)}, u32[]{:S(2)}) async-start(bf16[8,144,256]{2,1,0:T(8,128)(2,1)} %broadcast_in_dim.8), calls=%async_computation | async-start | bytes 1179648 | tf_op jit(solution)/shard_map/all_to_all | solution.py:540
  31.0 1.4 collective-permute-done.3
  32.4 4.7 %collective-permute-done.2 = bf16[256,1024]{1,0:T(8,128)(2,1)S(1)} collective-permute-done((bf16[256,1024]{1,0:T(8,128)(2,1)S(1)}, bf16[256,1024]{1,0:T(8,128)(2,1)S(1)}, u32[]{:S(2)}, u32[]{:S(2)}) %collective-permute-start.2) | collective-permute-done | bytes 524320 | tf_op jit(solution)/shard_map/ppermute | solution.py:36
  37.9 2.4 collective-permute-start.5
  40.4 9.2 %all-to-all-done = bf16[8,144,256]{2,1,0:T(8,128)(2,1)} async-done(((bf16[8,144,256]{2,1,0:T(8,128)(2,1)}), bf16[8,144,256]{2,1,0:T(8,128)(2,1)}, u32[]{:S(2)}, u32[]{:S(2)}) %all-to-all-start) | async-done | bytes 589856 | tf_op jit(solution)/shard_map/all_to_all | solution.py:540
  52.2 1.1 constant_dynamic-update-slice_fusion.part_2
  53.3 1.7 collective-permute-start.6
  55.1 1.1 slice.106
  57.7 1.7 convolution_convert_fusion
  59.6 10.8 %attention_forward.1 = (bf16[16,64,128]{2,1,0:T(8,128)(2,1)S(1)}, f32[64,2048]{1,0:T(8,128)S(1)}, f32[1,2048]{1,0:T(1,128)S(1)}) custom-call(s32[16]{0:T(128)S(1)} %stack.142.place, bf16[192,2048]{1,0:T(8,128)(2,1)S(1)} %pad_maximum_fusion.2.q_ref.k_ref.v_ref, bf16[192,2048]{1,0:T(8,128)(2,1)S(1)} %pad_maximum_fusion.2.q_ref.k_ref.v_ref, ...), custom_call_target="tpu_custom_call" | custom-call | flops 4294967296 | bytes 1310720 | tf_op jit(solution)/shard_map/attention_forward/pallas_call | solution.py:70
  71.8 15.0 %all_to_all.25.att_ref = bf16[16,64,128]{2,1,0:T(8,128)(2,1)} all-to-all(bf16[16,64,128]{2,1,0:T(8,128)(2,1)S(1)} %get-tuple-element.79), channel_id=1, replica_groups=mesh['zh'=2,'zl'=2,'xh'=2,'core'=2,'xl'=2,'y'=4] {'zh','zl','xh','core'}, dimensions={0} | all-to-all | bytes 524288 | tf_op jit(solution)/shard_map/all_to_all | solution.py:561
  86.9 2.3 slice.107.own_ref
  90.2 1.2 copy.24
  92.2 4.4 %out_and_norm.1 = (bf16[128,1024]{1,0:T(8,128)(2,1)}, bf16[128,1024]{1,0:T(8,128)(2,1)}, f32[128,1024]{1,0:T(8,128)}, f32[128,1024]{1,0:T(8,128)}, f32[128,128]{1,0:T(8,128)}) custom-call(s32[2]{0:T(128)} %pad_add_fusion.spots, bf16[16,64,128]{2,1,0:T(8,128)(2,1)} %all_to_all.25.att_ref, bf16[1024,512]{1,0:T(8,128)(2,1)} %slice.107.own_ref, ...), custom_call_target="tpu_custom_call" | custom-call | tf_op jit(solution)/shard_map/out_and_norm/pallas_call | solution.py:342
  98.4 4.0 %fusion.23 = (f32[256,1024]{1,0:T(8,128)}, bf16[256,1024]{1,0:T(8,128)(2,1)}) fusion(bf16[256,1024]{1,0:T(8,128)(2,1)S(1)} %constant_dynamic-update-slice_fusion.3.hid_a, bf16[1024,2560]{1,0:T(8,128)(2,1)} %all-gather.3.cloned.1.call-done), kind=kOutput, calls=%fused_computation.27 | convolution fusion | flops 539492352 | bytes 4194304 | tf_op jit(solution)/shard_map/dot_general | solution.py:26
  102.4 2.6 collective-permute-done.8
  105.9 1.1 collective-permute-done.10
  107.1 1.7 multiply_convert_fusion
  111.0 1.8 constant_dynamic-slice_fusion.3
  112.9 1.2 fusion.40
  114.1 2.6 fusion.2
  117.1 1.2 collective-permute-done.12
  118.4 6.5 %collective-permute-done.13 = bf16[128,1024]{1,0:T(8,128)(2,1)S(1)} collective-permute-done((bf16[128,1024]{1,0:T(8,128)(2,1)S(1)}, bf16[128,1024]{1,0:T(8,128)(2,1)S(1)}, u32[]{:S(2)}, u32[]{:S(2)}) %collective-permute-start.13) | collective-permute-done | bytes 262176 | tf_op jit(solution)/shard_map/ppermute | solution.py:32
  127.2 1.1 collective-permute-done.15
  129.2 2.4 fusion.14.up_a
  131.6 3.5 %collective-permute-done.14 = bf16[128,1024]{1,0:T(8,128)(2,1)S(1)} collective-permute-done((bf16[128,1024]{1,0:T(8,128)(2,1)S(1)}, bf16[128,1024]{1,0:T(8,128)(2,1)S(1)}, u32[]{:S(2)}, u32[]{:S(2)}) %collective-permute-start.14) | collective-permute-done | bytes 262176 | tf_op jit(solution)/shard_map/ppermute | solution.py:32
  135.9 1.1 collective-permute-done.16
  139.3 1.2 collective-permute-done.17
  142.5 1.2 collective-permute-done.18
  144.5 7.0 %ff_products.1 = bf16[1024,2048]{1,0:T(8,128)(2,1)} custom-call(bf16[256,1024]{1,0:T(8,128)(2,1)} %copy-done.17, bf16[256,1024]{1,0:T(8,128)(2,1)} %copy-done.15, bf16[256,1024]{1,0:T(8,128)(2,1)} %copy-done.24, bf16[256,1024]{1,0:T(8,128)(2,1)} %copy-done.25, bf16[256,1024]{1,0:T(8,128)(2,1)} %pad_maximum_fusion.7.mixed_a, bf16[256,1024]{1,0:T(8,128)(2,1)} %copy-done.16, ...), custom_call_target="tpu_custom_call" | custom-call | flops 2147483648 | bytes 8388608 | tf_op jit(solution)/shard_map/ff_products/pallas_call | solution.py:453
  151.6 2.3 fusion.56
  153.9 5.3 %collective-permute-done.19.late_ref = bf16[128,1024]{1,0:T(8,128)(2,1)S(1)} collective-permute-done((bf16[128,1024]{1,0:T(8,128)(2,1)}, bf16[128,1024]{1,0:T(8,128)(2,1)S(1)}, u32[]{:S(2)}, u32[]{:S(2)}) %collective-permute-start.19) | collective-permute-done | bytes 262176 | tf_op jit(solution)/shard_map/ppermute | solution.py:32
  159.9 4.4 %norm_one_back.1 = (f32[128,1024]{1,0:T(8,128)}, bf16[256,1024]{1,0:T(8,128)(2,1)}, bf16[16,64,128]{2,1,0:T(8,128)(2,1)}, f32[2,1024]{1,0:T(2,128)}) custom-call(s32[2]{0:T(128)} %pad_add_fusion.spots, f32[128,1024]{1,0:T(8,128)} %get-tuple-element.147.base_ref, bf16[128,1024]{1,0:T(8,128)(2,1)} %copy-done.26, f32[128,1024]{1,0:T(8,128)} %get-tuple-element.98.normal_ref, ...), custom_call_target="tpu_custom_call" | custom-call | tf_op jit(solution)/shard_map/norm_one_back/pallas_call | solution.py:342
  164.4 5.4 %all-to-all-start.2 = ((bf16[16,64,128]{2,1,0:T(8,128)(2,1)}), bf16[16,64,128]{2,1,0:T(8,128)(2,1)}, u32[]{:S(2)}, u32[]{:S(2)}) async-start(bf16[16,64,128]{2,1,0:T(8,128)(2,1)} %get-tuple-element.101), calls=%async_computation.3 | async-start | bytes 524288 | tf_op jit(solution)/shard_map/all_to_all | solution.py:603
  170.2 7.4 %collective-permute-done.21.block_2 = bf16[256,1024]{1,0:T(8,128)(2,1)} collective-permute-done((bf16[256,1024]{1,0:T(8,128)(2,1)}, bf16[256,1024]{1,0:T(8,128)(2,1)}, u32[]{:S(2)}, u32[]{:S(2)}) %collective-permute-start.21) | collective-permute-done | bytes 524320 | tf_op jit(solution)/shard_map/ppermute | solution.py:32
  177.6 3.5 %collective-permute-start.22 = (bf16[256,1024]{1,0:T(8,128)(2,1)}, bf16[256,1024]{1,0:T(8,128)(2,1)}, u32[]{:S(2)}, u32[]{:S(2)}) collective-permute-start(bf16[256,1024]{1,0:T(8,128)(2,1)} %collective-permute-done.21.block_2), channel_id=1, source_target_pairs={{0,8},{8,0},{1,9},{9,1},{2,10},{10,2},{3,11},{11,3},{4,12},{12,4},... | collective-permute-start | bytes 1572872 | tf_op jit(solution)/shard_map/ppermute | solution.py:32
  181.5 15.3 %attention_backward.1 = (bf16[192,1024]{1,0:T(8,128)(2,1)}, bf16[192,1024]{1,0:T(8,128)(2,1)}, bf16[16,192,128]{2,1,0:T(8,128)(2,1)}) custom-call(s32[16]{0:T(128)} %copy-done.8, bf16[192,2048]{1,0:T(8,128)(2,1)} %copy-done.3, bf16[192,2048]{1,0:T(8,128)(2,1)} %copy-done.3, bf16[192,2048]{1,0:T(8,128)(2,1)} %copy-done.3, ...), custom_call_target="tpu_custom_call" | custom-call | flops 10737418240 | bytes 2621440 | tf_op jit(solution)/shard_map/attention_backward/pallas_call | solution.py:156
  198.8 3.3 %weight_terms.1 = bf16[8,464,128]{2,1,0:T(8,128)(2,1)S(1)} custom-call(s32[1]{0:T(128)} %bitcast.29.spots, bf16[192,1024]{1,0:T(8,128)(2,1)S(1)} %copy-done.5, bf16[192,1024]{1,0:T(8,128)(2,1)S(1)} %copy-done.6, bf16[512,1024]{1,0:T(8,128)(2,1)S(1)} %pad_maximum_fusion.part_0, bf16[512,1024]{1,0:T(8,128)(2,1)S(1)} %collective-permute-done.4.part_1, ...), custom_call_target="tpu_custom_call" | custom-call | tf_op jit(solution)/shard_map/weight_terms/pallas_call | solution.py:342
  203.0 4.5 %all-to-all-start.3 = ((bf16[8,464,128]{2,1,0:T(8,128)(2,1)}), bf16[8,464,128]{2,1,0:T(8,128)(2,1)S(1)}, u32[]{:S(2)}, u32[]{:S(2)}) async-start(bf16[8,464,128]{2,1,0:T(8,128)(2,1)} %copy-done.2), calls=%async_computation.4 | async-start | bytes 1900544 | tf_op jit(solution)/shard_map/all_to_all | solution.py:616
  207.6 1.0 collective-permute-start.28
  208.6 12.4 %all-to-all-done.3 = bf16[8,464,128]{2,1,0:T(8,128)(2,1)S(1)} async-done(((bf16[8,464,128]{2,1,0:T(8,128)(2,1)}), bf16[8,464,128]{2,1,0:T(8,128)(2,1)S(1)}, u32[]{:S(2)}, u32[]{:S(2)}) %all-to-all-start.3) | async-done | bytes 950304 | tf_op jit(solution)/shard_map/all_to_all | solution.py:616
  221.0 3.0 %collective-permute-start.23 = (bf16[128,2048]{1,0:T(8,128)(2,1)}, bf16[128,2048]{1,0:T(8,128)(2,1)S(1)}, u32[]{:S(2)}, u32[]{:S(2)}) collective-permute-start(bf16[128,2048]{1,0:T(8,128)(2,1)} %reduce-scatter.2.cloned.1.call-done), channel_id=1, source_target_pairs={{0,64},{64,0},{1,65},{65,1},{2,66},{66,2},{3,67},{67,3},{4,68},{68... | collective-permute-start | bytes 1572872 | tf_op jit(solution)/shard_map/ppermute | solution.py:32
  224.2 2.5 collective-permute-start.25
  226.7 4.4 %all-to-all-start.4 = ((bf16[16,192,128]{2,1,0:T(8,128)(2,1)}), bf16[16,192,128]{2,1,0:T(8,128)(2,1)S(1)}, u32[]{:S(2)}, u32[]{:S(2)}) async-start(bf16[16,192,128]{2,1,0:T(8,128)(2,1)} %get-tuple-element.113), calls=%async_computation.5 | async-start | bytes 1572864 | tf_op jit(solution)/shard_map/all_to_all | solution.py:629
  231.2 4.7 %collective-permute-done.23 = bf16[128,2048]{1,0:T(8,128)(2,1)S(1)} collective-permute-done((bf16[128,2048]{1,0:T(8,128)(2,1)}, bf16[128,2048]{1,0:T(8,128)(2,1)S(1)}, u32[]{:S(2)}, u32[]{:S(2)}) %collective-permute-start.23) | collective-permute-done | bytes 524320 | tf_op jit(solution)/shard_map/ppermute | solution.py:32
  236.1 6.1 %collective-permute-start.24 = (bf16[128,2048]{1,0:T(8,128)(2,1)S(1)}, bf16[128,2048]{1,0:T(8,128)(2,1)S(1)}, u32[]{:S(2)}, u32[]{:S(2)}) collective-permute-start(bf16[128,2048]{1,0:T(8,128)(2,1)S(1)} %add_convert_fusion.1), channel_id=1, source_target_pairs={{0,16},{16,0},{1,17},{17,1},{2,18},{18,2},{3,19},{19,3},{4,20},{20... | collective-permute-start | bytes 1572872 | tf_op jit(solution)/shard_map/ppermute | solution.py:32
  242.2 3.4 %all-to-all-done.4.every_ref = bf16[16,192,128]{2,1,0:T(8,128)(2,1)S(1)} async-done(((bf16[16,192,128]{2,1,0:T(8,128)(2,1)}), bf16[16,192,128]{2,1,0:T(8,128)(2,1)S(1)}, u32[]{:S(2)}, u32[]{:S(2)}) %all-to-all-start.4) | async-done | bytes 786464 | tf_op jit(solution)/shard_map/all_to_all | solution.py:629
  245.6 2.4 collective-permute-start.26
  248.0 3.7 %collective-permute-done.26 = bf16[656,128]{1,0:T(8,128)(2,1)S(1)} collective-permute-done((bf16[656,128]{1,0:T(8,128)(2,1)S(1)}, bf16[656,128]{1,0:T(8,128)(2,1)S(1)}, u32[]{:S(2)}, u32[]{:S(2)}) %collective-permute-start.26) | collective-permute-done | bytes 167968 | tf_op jit(solution)/shard_map/ppermute | solution.py:32
  251.8 1.2 collective-permute-done.24
  253.1 2.0 collective-permute-start.29
  255.2 6.2 %input_product.1 = f32[128,1024]{1,0:T(8,128)} custom-call(s32[2]{0:T(128)} %pad_add_fusion.spots, bf16[16,192,128]{2,1,0:T(8,128)(2,1)} %copy-done.13, bf16[1024,1536]{1,0:T(8,128)(2,1)} %all-gather.5.cloned.1.call-done.own_ref, bf16[1024,1536]{1,0:T(8,128)(2,1)} %collective-permute-done.28.pair_ref, f32[128,1024]{1,0:T(8,128)} %get-tuple-element.121.base_ref), custom_call_target="tpu_custom_call" | custom-call | tf_op jit(solution)/shard_map/input_product/pallas_call | solution.py:299
  261.5 9.2 %collective-permute-done.27 = bf16[128,2048]{1,0:T(8,128)(2,1)S(1)} collective-permute-done((bf16[128,2048]{1,0:T(8,128)(2,1)S(1)}, bf16[128,2048]{1,0:T(8,128)(2,1)S(1)}, u32[]{:S(2)}, u32[]{:S(2)}) %collective-permute-start.27) | collective-permute-done | bytes 524320 | tf_op jit(solution)/shard_map/ppermute | solution.py:32
  270.8 3.1 %collective-permute-start.31 = (bf16[256,2048]{1,0:T(8,128)(2,1)S(1)}, bf16[256,2048]{1,0:T(8,128)(2,1)}, u32[]{:S(2)}, u32[]{:S(2)}) collective-permute-start(bf16[256,2048]{1,0:T(8,128)(2,1)S(1)} %pad_maximum_fusion.1.own_ref), channel_id=1, source_target_pairs={{0,8},{8,0},{1,9},{9,1},{2,10},{10,2},{3,11},{11,3},{4,12},{12,4},... | collective-permute-start | bytes 3145736 | tf_op jit(solution)/shard_map/ppermute | solution.py:32
  274.2 2.8 collective-permute-done.30.pair_ref
  277.0 2.3 assemble_rest.1
  279.8 4.0 %assemble.1 = (f32[128,4096]{1,0:T(8,128)}, f32[128,4096]{1,0:T(8,128)}) custom-call(s32[4]{0:T(128)S(1)} %pad_add_fusion.1.spots, bf16[256,2048]{1,0:T(8,128)(2,1)S(1)} %pad_maximum_fusion.1.own_ref, bf16[256,2048]{1,0:T(8,128)(2,1)} %collective-permute-done.31.pair_ref), custom_call_target="tpu_custom_call" | custom-call | tf_op jit(solution)/shard_map/assemble/pallas_call | solution.py:342
  (181 shorter events, 31.8 us)
Async XLA Ops:
  7.2 3.0 %copy-start.30 = (bf16[128]{0:T(256)(128)(2,1)S(1)}, bf16[128]{0:T(256)(128)(2,1)}, u32[]{:S(2)}) copy-start(bf16[128]{0:T(256)(128)(2,1)} %param.15) | copy-start | bytes 772
  7.2 3.0 %copy-start.29 = (bf16[128]{0:T(256)(128)(2,1)S(1)}, bf16[128]{0:T(256)(128)(2,1)}, u32[]{:S(2)}) copy-start(bf16[128]{0:T(256)(128)(2,1)} %param.16) | copy-start | bytes 772
  7.2 3.0 %copy-start.28 = (bf16[128]{0:T(256)(128)(2,1)S(1)}, bf16[128]{0:T(256)(128)(2,1)}, u32[]{:S(2)}) copy-start(bf16[128]{0:T(256)(128)(2,1)} %param.17) | copy-start | bytes 772
  7.2 3.0 %copy-start.27 = (bf16[128]{0:T(256)(128)(2,1)S(1)}, bf16[128]{0:T(256)(128)(2,1)}, u32[]{:S(2)}) copy-start(bf16[128]{0:T(256)(128)(2,1)} %param.18) | copy-start | bytes 772
  7.2 79.6 %all-gather.3.cloned.1.call-start = ((), (), s32[]{:S(2)}) async-start(), calls=%async_computation.6 | async-start | bytes 5898240 | tf_op jit(solution)/shard_map/all_gather | solution.py:545
  8.1 4.2 %copy-start.14 = (bf16[1,128,1024]{2,1,0:T(8,128)(2,1)S(1)}, bf16[1,128,1024]{2,1,0:T(8,128)(2,1)}, u32[]{:S(2)}) copy-start(bf16[1,128,1024]{2,1,0:T(8,128)(2,1)} %param.10) | copy-start | bytes 786436
  12.3 9.1 %collective-permute-start = (bf16[128,1024]{1,0:T(8,128)(2,1)S(1)}, bf16[128,1024]{1,0:T(8,128)(2,1)S(1)}, u32[]{:S(2)}, u32[]{:S(2)}) collective-permute-start(bf16[128,1024]{1,0:T(8,128)(2,1)S(1)} %bitcast.105), channel_id=1, source_target_pairs={{0,16},{16,0},{1,17},{17,1},{2,18},{18,2},{3,19},{19,3},{4,20},{20... | collective-permute-start | bytes 786440 | tf_op jit(solution)/shard_map/ppermute | solution.py:32
  15.9 7.4 %collective-permute-start.1 = (bf16[128,1024]{1,0:T(8,128)(2,1)S(1)}, bf16[128,1024]{1,0:T(8,128)(2,1)S(1)}, u32[]{:S(2)}, u32[]{:S(2)}) collective-permute-start(bf16[128,1024]{1,0:T(8,128)(2,1)S(1)} %bitcast.106), channel_id=1, source_target_pairs={{0,32},{32,0},{64,96},{96,64},{1,33},{33,1},{65,97},{97,65},{2,34}... | collective-permute-start | bytes 786440 | tf_op jit(solution)/shard_map/ppermute | solution.py:36
  21.5 16.5 %copy-start.18 = (bf16[128,1024]{1,0:T(8,128)(2,1)}, bf16[128,1024]{1,0:T(8,128)(2,1)S(1)}, u32[]{:S(2)}) copy-start(bf16[128,1024]{1,0:T(8,128)(2,1)S(1)} %collective-permute-done) | copy-start | bytes 786436
  23.3 13.8 %collective-permute-start.2 = (bf16[256,1024]{1,0:T(8,128)(2,1)S(1)}, bf16[256,1024]{1,0:T(8,128)(2,1)S(1)}, u32[]{:S(2)}, u32[]{:S(2)}) collective-permute-start(bf16[256,1024]{1,0:T(8,128)(2,1)S(1)} %pad_maximum_fusion.5), channel_id=1, source_target_pairs={{0,96},{32,64},{64,32},{96,0},{1,97},{33,65},{65,33},{97,1},{2,98}... | collective-permute-start | bytes 1572872 | tf_op jit(solution)/shard_map/ppermute | solution.py:36
  26.6 5.7 %collective-permute-start.3 = (bf16[128,1024]{1,0:T(8,128)(2,1)S(1)}, bf16[128,1024]{1,0:T(8,128)(2,1)S(1)}, u32[]{:S(2)}, u32[]{:S(2)}) collective-permute-start(bf16[128,1024]{1,0:T(8,128)(2,1)S(1)} %collective-permute-done), channel_id=1, source_target_pairs={{0,32},{32,0},{64,96},{96,64},{1,33},{33,1},{65,97},{97,65},{2,34}... | collective-permute-start | bytes 786440 | tf_op jit(solution)/shard_map/ppermute | solution.py:36
  26.6 22.9 %all-to-all-start = ((bf16[8,144,256]{2,1,0:T(8,128)(2,1)}), bf16[8,144,256]{2,1,0:T(8,128)(2,1)}, u32[]{:S(2)}, u32[]{:S(2)}) async-start(bf16[8,144,256]{2,1,0:T(8,128)(2,1)} %broadcast_in_dim.8), calls=%async_computation | async-start | bytes 1179648 | tf_op jit(solution)/shard_map/all_to_all | solution.py:540
  30.9 133.4 %all-gather.5.cloned.1.call-start = ((), (), s32[]{:S(2)}) async-start(), calls=%async_computation.8 | async-start | bytes 3538944 | tf_op jit(solution)/shard_map/all_gather | solution.py:569
  32.4 5.5 %copy-start.19 = (bf16[128,1024]{1,0:T(8,128)(2,1)}, bf16[128,1024]{1,0:T(8,128)(2,1)S(1)}, u32[]{:S(2)}) copy-start(bf16[128,1024]{1,0:T(8,128)(2,1)S(1)} %collective-permute-done.3) | copy-start | bytes 786436
  37.9 14.3 %collective-permute-start.5 = (bf16[256,1024]{1,0:T(8,128)(2,1)}, bf16[256,1024]{1,0:T(8,128)(2,1)}, u32[]{:S(2)}, u32[]{:S(2)}) collective-permute-start(bf16[256,1024]{1,0:T(8,128)(2,1)} %pad_maximum_fusion.6), channel_id=1, source_target_pairs={{0,96},{32,64},{64,32},{96,0},{1,97},{33,65},{65,33},{97,1},{2,98}... | collective-permute-start | bytes 1572872 | tf_op jit(solution)/shard_map/ppermute | solution.py:36
  49.5 7.7 %collective-permute-start.4 = (bf16[512,1024]{1,0:T(8,128)(2,1)S(1)}, bf16[512,1024]{1,0:T(8,128)(2,1)S(1)}, u32[]{:S(2)}, u32[]{:S(2)}) collective-permute-start(bf16[512,1024]{1,0:T(8,128)(2,1)S(1)} %pad_maximum_fusion.part_0), channel_id=1, source_target_pairs={{0,8},{8,0},{1,9},{9,1},{2,10},{10,2},{3,11},{11,3},{4,12},{12,4},... | collective-permute-start | bytes 3145736 | tf_op jit(solution)/shard_map/ppermute | solution.py:32
  53.3 4.5 %collective-permute-start.6 = (bf16[512,1024]{1,0:T(8,128)(2,1)S(1)}, bf16[512,1024]{1,0:T(8,128)(2,1)}, u32[]{:S(2)}, u32[]{:S(2)}) collective-permute-start(bf16[512,1024]{1,0:T(8,128)(2,1)S(1)} %constant_dynamic-update-slice_fusion.part_2), channel_id=1, source_target_pairs={{0,8},{8,0},{1,9},{9,1},{2,10},{10,2},{3,11},{11,3},{4,12},{12,4},... | collective-permute-start | bytes 3145736 | tf_op jit(solution)/shard_map/ppermute | solution.py:32
  55.0 4.5 %copy-start.8 = (s32[16]{0:T(128)}, s32[16]{0:T(128)S(1)}, u32[]{:S(2)}) copy-start(s32[16]{0:T(128)S(1)} %stack.142.place) | copy-start | bytes 196
  59.6 10.8 %copy-start.3 = (bf16[192,2048]{1,0:T(8,128)(2,1)}, bf16[192,2048]{1,0:T(8,128)(2,1)S(1)}, u32[]{:S(2)}) copy-start(bf16[192,2048]{1,0:T(8,128)(2,1)S(1)} %pad_maximum_fusion.2.q_ref.k_ref.v_ref) | copy-start | bytes 2359300
  89.1 3.1 %collective-permute-start.7 = (bf16[1024,512]{1,0:T(8,128)(2,1)}, bf16[1024,512]{1,0:T(8,128)(2,1)}, u32[]{:S(2)}, u32[]{:S(2)}) collective-permute-start(bf16[1024,512]{1,0:T(8,128)(2,1)} %slice.107.own_ref), channel_id=1, source_target_pairs={{0,8},{8,0},{1,9},{9,1},{2,10},{10,2},{3,11},{11,3},{4,12},{12,4},... | collective-permute-start | bytes 3145736 | tf_op jit(solution)/shard_map/ppermute | solution.py:32
  92.2 14.8 %slice-start = ((s8[5242880]{0:T(1024)(128)(4,1)}), s8[1048576]{0:T(1024)(128)(4,1)S(1)}, s32[]{:S(2)}) async-start(s8[5242880]{0:T(1024)(128)(4,1)} %bitcast.110), calls=%async_computation.9 | async-start | bytes 2097152
  96.6 1.7 collective-permute-start.9
  96.9 8.0 %collective-permute-start.8 = (bf16[128,1024]{1,0:T(8,128)(2,1)}, bf16[128,1024]{1,0:T(8,128)(2,1)S(1)}, u32[]{:S(2)}, u32[]{:S(2)}) collective-permute-start(bf16[128,1024]{1,0:T(8,128)(2,1)} %get-tuple-element.83), channel_id=1, source_target_pairs={{0,32},{32,0},{1,33},{33,1},{2,34},{34,2},{3,35},{35,3},{4,36},{36... | collective-permute-start | bytes 786440 | tf_op jit(solution)/shard_map/ppermute | solution.py:32
  98.3 4.0 %copy-start.17 = (bf16[256,1024]{1,0:T(8,128)(2,1)}, bf16[256,1024]{1,0:T(8,128)(2,1)S(1)}, u32[]{:S(2)}) copy-start(bf16[256,1024]{1,0:T(8,128)(2,1)S(1)} %constant_dynamic-update-slice_fusion.3.hid_a) | copy-start | bytes 1572868
  98.3 8.7 %slice-start.1 = ((s8[5242880]{0:T(1024)(128)(4,1)}), s8[4194304]{0:T(1024)(128)(4,1)S(1)}, s32[]{:S(2)}) async-start(s8[5242880]{0:T(1024)(128)(4,1)} %bitcast.110), calls=%async_computation.10 | async-start | bytes 8388608
  104.9 2.1 collective-permute-start.10
  108.8 1.8 copy-start.22
  110.6 2.3 collective-permute-start.11
  112.8 108.2 %reduce-scatter.2.cloned.1.call-start = ((), (), s32[]{:S(2)}) async-start(), calls=%async_computation.7 | async-start | bytes 4718592 | tf_op jit(solution)/shard_map/reduce_scatter | solution.py:598
  114.1 10.8 %copy-start.23 = (f32[128,1024]{1,0:T(8,128)S(1)}, f32[128,1024]{1,0:T(8,128)}, u32[]{:S(2)}) copy-start(f32[128,1024]{1,0:T(8,128)} %get-tuple-element.82) | copy-start | bytes 1572868
  114.1 23.0 %slice-start.2 = ((s8[5242880]{0:T(1024)(128)(4,1)}), s8[1048576]{0:T(1024)(128)(4,1)S(1)}, s32[]{:S(2)}) async-start(s8[5242880]{0:T(1024)(128)(4,1)} %bitcast.112), calls=%async_computation.11 | async-start | bytes 2097152
  116.7 8.6 %copy-start.12 = (bf16[1,128,1024]{2,1,0:T(8,128)(2,1)S(1)}, bf16[1,128,1024]{2,1,0:T(8,128)(2,1)}, u32[]{:S(2)}) copy-start(bf16[1,128,1024]{2,1,0:T(8,128)(2,1)} %param.19) | copy-start | bytes 786436
  116.8 1.6 collective-permute-start.12
  117.0 7.9 %collective-permute-start.13 = (bf16[128,1024]{1,0:T(8,128)(2,1)S(1)}, bf16[128,1024]{1,0:T(8,128)(2,1)S(1)}, u32[]{:S(2)}, u32[]{:S(2)}) collective-permute-start(bf16[128,1024]{1,0:T(8,128)(2,1)S(1)} %fusion.40), channel_id=1, source_target_pairs={{0,32},{32,0},{1,33},{33,1},{2,34},{34,2},{3,35},{35,3},{4,36},{36... | collective-permute-start | bytes 786440 | tf_op jit(solution)/shard_map/ppermute | solution.py:32
  125.1 4.1 %copy-start.31 = (f32[256,1024]{1,0:T(8,128)S(1)}, f32[256,1024]{1,0:T(8,128)}, u32[]{:S(2)}) copy-start(f32[256,1024]{1,0:T(8,128)} %get-tuple-element.88) | copy-start | bytes 3145732
  125.9 11.2 %slice-start.3 = ((s8[5242880]{0:T(1024)(128)(4,1)}), s8[4194304]{0:T(1024)(128)(4,1)S(1)}, s32[]{:S(2)}) async-start(s8[5242880]{0:T(1024)(128)(4,1)} %bitcast.112), calls=%async_computation.12 | async-start | bytes 8388608
  126.1 2.2 collective-permute-start.15
  127.2 8.0 %collective-permute-start.14 = (bf16[128,1024]{1,0:T(8,128)(2,1)S(1)}, bf16[128,1024]{1,0:T(8,128)(2,1)S(1)}, u32[]{:S(2)}, u32[]{:S(2)}) collective-permute-start(bf16[128,1024]{1,0:T(8,128)(2,1)S(1)} %fusion.57), channel_id=1, source_target_pairs={{0,32},{32,0},{1,33},{33,1},{2,34},{34,2},{3,35},{35,3},{4,36},{36... | collective-permute-start | bytes 786440 | tf_op jit(solution)/shard_map/ppermute | solution.py:32
  129.2 7.9 %copy-start.32 = (f32[256,1024]{1,0:T(8,128)S(1)}, f32[256,1024]{1,0:T(8,128)}, u32[]{:S(2)}) copy-start(f32[256,1024]{1,0:T(8,128)} %get-tuple-element.156) | copy-start | bytes 3145732
  131.6 9.6 %copy-start.24 = (bf16[256,1024]{1,0:T(8,128)(2,1)}, bf16[256,1024]{1,0:T(8,128)(2,1)S(1)}, u32[]{:S(2)}) copy-start(bf16[256,1024]{1,0:T(8,128)(2,1)S(1)} %fusion.14.up_a) | copy-start | bytes 1572868
  135.1 1.9 collective-permute-start.16
  138.8 1.6 collective-permute-start.17
  142.0 1.6 collective-permute-start.18
  151.5 7.8 %collective-permute-start.19 = (bf16[128,1024]{1,0:T(8,128)(2,1)}, bf16[128,1024]{1,0:T(8,128)(2,1)S(1)}, u32[]{:S(2)}, u32[]{:S(2)}) collective-permute-start(bf16[128,1024]{1,0:T(8,128)(2,1)} %fusion.37), channel_id=1, source_target_pairs={{0,32},{32,0},{1,33},{33,1},{2,34},{34,2},{3,35},{35,3},{4,36},{36... | collective-permute-start | bytes 786440 | tf_op jit(solution)/shard_map/ppermute | solution.py:32
  164.3 13.3 %collective-permute-start.21 = (bf16[256,1024]{1,0:T(8,128)(2,1)}, bf16[256,1024]{1,0:T(8,128)(2,1)}, u32[]{:S(2)}, u32[]{:S(2)}) collective-permute-start(bf16[256,1024]{1,0:T(8,128)(2,1)} %get-tuple-element.110.block_0), channel_id=1, source_target_pairs={{0,32},{32,0},{1,33},{33,1},{2,34},{34,2},{3,35},{35,3},{4,36},{36... | collective-permute-start | bytes 1572872 | tf_op jit(solution)/shard_map/ppermute | solution.py:32
  164.4 17.0 %all-to-all-start.2 = ((bf16[16,64,128]{2,1,0:T(8,128)(2,1)}), bf16[16,64,128]{2,1,0:T(8,128)(2,1)}, u32[]{:S(2)}, u32[]{:S(2)}) async-start(bf16[16,64,128]{2,1,0:T(8,128)(2,1)} %get-tuple-element.101), calls=%async_computation.3 | async-start | bytes 524288 | tf_op jit(solution)/shard_map/all_to_all | solution.py:603
  169.9 26.9 %collective-permute-start.20 = (bf16[256,1024]{1,0:T(8,128)(2,1)}, bf16[256,1024]{1,0:T(8,128)(2,1)}, u32[]{:S(2)}, u32[]{:S(2)}) collective-permute-start(bf16[256,1024]{1,0:T(8,128)(2,1)} %get-tuple-element.110.block_0), channel_id=1, source_target_pairs={{0,8},{8,0},{1,9},{9,1},{2,10},{10,2},{3,11},{11,3},{4,12},{12,4},... | collective-permute-start | bytes 1572872 | tf_op jit(solution)/shard_map/ppermute | solution.py:32
  177.6 19.2 %collective-permute-start.22 = (bf16[256,1024]{1,0:T(8,128)(2,1)}, bf16[256,1024]{1,0:T(8,128)(2,1)}, u32[]{:S(2)}, u32[]{:S(2)}) collective-permute-start(bf16[256,1024]{1,0:T(8,128)(2,1)} %collective-permute-done.21.block_2), channel_id=1, source_target_pairs={{0,8},{8,0},{1,9},{9,1},{2,10},{10,2},{3,11},{11,3},{4,12},{12,4},... | collective-permute-start | bytes 1572872 | tf_op jit(solution)/shard_map/ppermute | solution.py:32
  181.5 15.3 %copy-start.4 = (bf16[256,1024]{1,0:T(8,128)(2,1)S(1)}, bf16[256,1024]{1,0:T(8,128)(2,1)}, u32[]{:S(2)}) copy-start(bf16[256,1024]{1,0:T(8,128)(2,1)} %get-tuple-element.110.block_0) | copy-start | bytes 1572868
  181.5 15.3 %copy-start.7 = (f32[2,1024]{1,0:T(2,128)S(1)}, f32[2,1024]{1,0:T(2,128)}, u32[]{:S(2)}) copy-start(f32[2,1024]{1,0:T(2,128)} %get-tuple-element.111.first_ref) | copy-start | bytes 24580
  203.0 18.0 %all-to-all-start.3 = ((bf16[8,464,128]{2,1,0:T(8,128)(2,1)}), bf16[8,464,128]{2,1,0:T(8,128)(2,1)S(1)}, u32[]{:S(2)}, u32[]{:S(2)}) async-start(bf16[8,464,128]{2,1,0:T(8,128)(2,1)} %copy-done.2), calls=%async_computation.4 | async-start | bytes 1900544 | tf_op jit(solution)/shard_map/all_to_all | solution.py:616
  207.6 47.7 %collective-permute-start.28 = (bf16[1024,1536]{1,0:T(8,128)(2,1)}, bf16[1024,1536]{1,0:T(8,128)(2,1)}, u32[]{:S(2)}, u32[]{:S(2)}) collective-permute-start(bf16[1024,1536]{1,0:T(8,128)(2,1)} %all-gather.5.cloned.1.call-done.own_ref), channel_id=1, source_target_pairs={{0,8},{8,0},{1,9},{9,1},{2,10},{10,2},{3,11},{11,3},{4,12},{12,4},... | collective-permute-start | bytes 9437192 | tf_op jit(solution)/shard_map/ppermute | solution.py:32
  221.0 14.9 %copy-start.21 = (bf16[128,2048]{1,0:T(8,128)(2,1)S(1)}, bf16[128,2048]{1,0:T(8,128)(2,1)}, u32[]{:S(2)}) copy-start(bf16[128,2048]{1,0:T(8,128)(2,1)} %reduce-scatter.2.cloned.1.call-done) | copy-start | bytes 1572868
  221.0 14.9 %collective-permute-start.23 = (bf16[128,2048]{1,0:T(8,128)(2,1)}, bf16[128,2048]{1,0:T(8,128)(2,1)S(1)}, u32[]{:S(2)}, u32[]{:S(2)}) collective-permute-start(bf16[128,2048]{1,0:T(8,128)(2,1)} %reduce-scatter.2.cloned.1.call-done), channel_id=1, source_target_pairs={{0,64},{64,0},{1,65},{65,1},{2,66},{66,2},{3,67},{67,3},{4,68},{68... | collective-permute-start | bytes 1572872 | tf_op jit(solution)/shard_map/ppermute | solution.py:32
  224.2 6.9 %collective-permute-start.25 = (bf16[464,128]{1,0:T(8,128)(2,1)S(1)}, bf16[464,128]{1,0:T(8,128)(2,1)S(1)}, u32[]{:S(2)}, u32[]{:S(2)}) collective-permute-start(bf16[464,128]{1,0:T(8,128)(2,1)S(1)} %reduce_sum.72), channel_id=1, source_target_pairs={{0,16},{16,0},{1,17},{17,1},{2,18},{18,2},{3,19},{19,3},{4,20},{20... | collective-permute-start | bytes 356360 | tf_op jit(solution)/shard_map/ppermute | solution.py:32
  226.7 18.9 %all-to-all-start.4 = ((bf16[16,192,128]{2,1,0:T(8,128)(2,1)}), bf16[16,192,128]{2,1,0:T(8,128)(2,1)S(1)}, u32[]{:S(2)}, u32[]{:S(2)}) async-start(bf16[16,192,128]{2,1,0:T(8,128)(2,1)} %get-tuple-element.113), calls=%async_computation.5 | async-start | bytes 1572864 | tf_op jit(solution)/shard_map/all_to_all | solution.py:629
  236.1 16.9 %collective-permute-start.24 = (bf16[128,2048]{1,0:T(8,128)(2,1)S(1)}, bf16[128,2048]{1,0:T(8,128)(2,1)S(1)}, u32[]{:S(2)}, u32[]{:S(2)}) collective-permute-start(bf16[128,2048]{1,0:T(8,128)(2,1)S(1)} %add_convert_fusion.1), channel_id=1, source_target_pairs={{0,16},{16,0},{1,17},{17,1},{2,18},{18,2},{3,19},{19,3},{4,20},{20... | collective-permute-start | bytes 1572872 | tf_op jit(solution)/shard_map/ppermute | solution.py:32
  245.6 9.6 %copy-start.13 = (bf16[16,192,128]{2,1,0:T(8,128)(2,1)}, bf16[16,192,128]{2,1,0:T(8,128)(2,1)S(1)}, u32[]{:S(2)}) copy-start(bf16[16,192,128]{2,1,0:T(8,128)(2,1)S(1)} %all-to-all-done.4.every_ref) | copy-start | bytes 2359300
  245.6 6.1 %collective-permute-start.26 = (bf16[656,128]{1,0:T(8,128)(2,1)S(1)}, bf16[656,128]{1,0:T(8,128)(2,1)S(1)}, u32[]{:S(2)}, u32[]{:S(2)}) collective-permute-start(bf16[656,128]{1,0:T(8,128)(2,1)S(1)} %pad_maximum_fusion.10), channel_id=1, source_target_pairs={{0,64},{64,0},{1,65},{65,1},{2,66},{66,2},{3,67},{67,3},{4,68},{68... | collective-permute-start | bytes 503816 | tf_op jit(solution)/shard_map/ppermute | solution.py:32
  253.1 8.3 %collective-permute-start.29 = (bf16[1040,128]{1,0:T(8,128)(2,1)S(1)}, bf16[1040,128]{1,0:T(8,128)(2,1)S(1)}, u32[]{:S(2)}, u32[]{:S(2)}) collective-permute-start(bf16[1040,128]{1,0:T(8,128)(2,1)S(1)} %pad_maximum_fusion.8), channel_id=1, source_target_pairs={{0,32},{32,0},{1,33},{33,1},{2,34},{34,2},{3,35},{35,3},{4,36},{36... | collective-permute-start | bytes 798728 | tf_op jit(solution)/shard_map/ppermute | solution.py:32
  255.1 15.6 %collective-permute-start.27 = (bf16[128,2048]{1,0:T(8,128)(2,1)S(1)}, bf16[128,2048]{1,0:T(8,128)(2,1)S(1)}, u32[]{:S(2)}, u32[]{:S(2)}) collective-permute-start(bf16[128,2048]{1,0:T(8,128)(2,1)S(1)} %add_convert_fusion), channel_id=1, source_target_pairs={{0,32},{32,0},{1,33},{33,1},{2,34},{34,2},{3,35},{35,3},{4,36},{36... | collective-permute-start | bytes 1572872 | tf_op jit(solution)/shard_map/ppermute | solution.py:32
  270.7 13.1 %copy-start.1 = (bf16[128,1024]{1,0:T(8,128)(2,1)S(1)}, bf16[128,1024]{1,0:T(8,128)(2,1)}, u32[]{:S(2)}) copy-start(bf16[128,1024]{1,0:T(8,128)(2,1)} %param.12) | copy-start | bytes 786436
  270.8 9.0 %collective-permute-start.31 = (bf16[256,2048]{1,0:T(8,128)(2,1)S(1)}, bf16[256,2048]{1,0:T(8,128)(2,1)}, u32[]{:S(2)}, u32[]{:S(2)}) collective-permute-start(bf16[256,2048]{1,0:T(8,128)(2,1)S(1)} %pad_maximum_fusion.1.own_ref), channel_id=1, source_target_pairs={{0,8},{8,0},{1,9},{9,1},{2,10},{10,2},{3,11},{11,3},{4,12},{12,4},... | collective-permute-start | bytes 3145736 | tf_op jit(solution)/shard_map/ppermute | solution.py:32
  273.9 3.0 %collective-permute-start.30 = (bf16[2080,128]{1,0:T(8,128)(2,1)S(1)}, bf16[2080,128]{1,0:T(8,128)(2,1)S(1)}, u32[]{:S(2)}, u32[]{:S(2)}) collective-permute-start(bf16[2080,128]{1,0:T(8,128)(2,1)S(1)} %pad_maximum_fusion.4.own_ref), channel_id=1, source_target_pairs={{0,8},{8,0},{1,9},{9,1},{2,10},{10,2},{3,11},{11,3},{4,12},{12,4},... | collective-permute-start | bytes 1597448 | tf_op jit(solution)/shard_map/ppermute | solution.py:32
  (12 other events, 11.2 us)
Sparse Core Ops, SparseCore 0:
  10.3 72.6 all-gather.2
  113.0 38.1 all-gather.4
  153.5 58.3 reduce-scatter.1

commit v4 on v3

--- a/solution.py
+++ b/solution.py
@@ -19,6 +19,7 @@
 Z = ("zh", "zl")
 SCALE = HEAD_DIM**-0.5
 QUERY_BLOCK = 256
+FORWARD_BLOCK = 512
 PARTS = QUERY_BLOCK // BLOCK
 
 
@@ -61,8 +62,8 @@
     out_ref[...] = attended
     log_ref[...] = top + jnp.log(total)
     low = attended.astype(LOW)
-    for part in range(PARTS):
-        low_ref[place[step * PARTS + part]] = low[:, part * BLOCK : (part + 1) * BLOCK]
+    for part in range((FORWARD_BLOCK // BLOCK)):
+        low_ref[place[step * (FORWARD_BLOCK // BLOCK) + part]] = low[:, part * BLOCK : (part + 1) * BLOCK]
 
 
 def attention_forward(place, projected):
@@ -71,16 +72,16 @@
         forward_kernel,
         grid_spec=pltpu.PrefetchScalarGridSpec(
             num_scalar_prefetch=1,
-            grid=(length // QUERY_BLOCK,),
+            grid=(length // FORWARD_BLOCK,),
             in_specs=[
-                pl.BlockSpec((HEAD_DIM, QUERY_BLOCK), lambda i, p: (0, i)),
+                pl.BlockSpec((HEAD_DIM, FORWARD_BLOCK), lambda i, p: (0, i)),
                 pl.BlockSpec((HEAD_DIM, length), lambda i, p: (1, 0)),
                 pl.BlockSpec((HEAD_DIM, length), lambda i, p: (2, 0)),
             ],
             out_specs=[
                 pl.BlockSpec((length // BLOCK, HEAD_DIM, BLOCK), lambda i, p: (0, 0, 0)),
-                pl.BlockSpec((HEAD_DIM, QUERY_BLOCK), lambda i, p: (0, i)),
-                pl.BlockSpec((1, QUERY_BLOCK), lambda i, p: (0, i)),
+                pl.BlockSpec((HEAD_DIM, FORWARD_BLOCK), lambda i, p: (0, i)),
+                pl.BlockSpec((1, FORWARD_BLOCK), lambda i, p: (0, i)),
             ],
             scratch_shapes=[pltpu.VMEM((length, HEAD_DIM), LOW)],
         ),

time: 292 us -> 291 us (level)
  transfers between devices with their start and end apart: 39 -> 39, of which waited for: 26 -> 26; matrix products, arithmetic and copies ran while one was open for 12% -> 12% of each run, Pallas kernels for 17% -> 16%
where the time goes in v4:
time: 291 us; the launch traced here: 290 us
  waiting for transfers between devices  89.4 us (31%)
  starting transfers between devices  64.6 us (22%)
  Pallas kernels  55.7 us (19%)
  local copies, waits for them, and re-layouts  22.1 us (8%)
  matrix products  17.1 us (6%)
  blocking collectives  16.2 us (6%)
  between operations  14.6 us (5%)
  other arithmetic  10.3 us (4%)
    ppermute x28, waiting for transfers between devices, swap(): return lax.ppermute(value, axis, [(0, 1), (1, 0)])  55.5 us
    ppermute x28, starting transfers between devices, swap(): return lax.ppermute(value, axis, [(0, 1), (1, 0)])  37.5 us
    pallas_call x5, Pallas kernels, local_call(): pl.pallas_call(kernel, grid_spec=pltpu.PrefetchScalarGridSpec(num_scalar_...  18.3 us
    dot_general x12, matrix products, dot(): lax.dot_general(left, right, (((left_dim,), (right_dim,)), ((), ())), pre...  17.1 us
    all_to_all x1, blocking collectives, per_device(): lax.all_to_all(low_blocks, CTX, split_axis=0, concat_axis=0, tiled=True)  16.2 us
    pallas_call x1, Pallas kernels, attention_backward(): pl.pallas_call(backward_kernel, grid_spec=pltpu.PrefetchScalarGridSpec(nu...  15.3 us
    all_to_all x1, waiting for transfers between devices, per_device(): lax.all_to_all(terms, FSDP, split_axis=0, concat_axis=0, tiled=True)  11.2 us
    unnamed x80, local copies, waits for them, and re-layouts  10.8 us
  transfers between devices with their start and end apart: 39, of which 26 were waited for; matrix products, arithmetic and copies ran while one was open for 12% of the time, Pallas kernels for 16%

profile of v4, /device:TPU:1, one launch (start us, length us, event | category | flops | bytes accessed | tf_op | source)
XLA Modules:
  0.0 289.9 jit_solution(10723416351114496086)
XLA Ops:
  8.2 1.1 constant_dynamic-slice_fusion.8
  12.2 3.6 %collective-permute-start = (bf16[128,1024]{1,0:T(8,128)(2,1)S(1)}, bf16[128,1024]{1,0:T(8,128)(2,1)S(1)}, u32[]{:S(2)}, u32[]{:S(2)}) collective-permute-start(bf16[128,1024]{1,0:T(8,128)(2,1)S(1)} %bitcast.105), channel_id=1, source_target_pairs={{0,16},{16,0},{1,17},{17,1},{2,18},{18,2},{3,19},{19,3},{4,20},{20... | collective-permute-start | bytes 786440 | tf_op jit(solution)/shard_map/ppermute | solution.py:33
  15.8 1.7 collective-permute-start.1
  17.5 3.8 %collective-permute-done = bf16[128,1024]{1,0:T(8,128)(2,1)S(1)} collective-permute-done((bf16[128,1024]{1,0:T(8,128)(2,1)S(1)}, bf16[128,1024]{1,0:T(8,128)(2,1)S(1)}, u32[]{:S(2)}, u32[]{:S(2)}) %collective-permute-start) | collective-permute-done | bytes 262176 | tf_op jit(solution)/shard_map/ppermute | solution.py:33
  21.3 1.7 collective-permute-done.1
  23.1 3.5 %collective-permute-start.2 = (bf16[256,1024]{1,0:T(8,128)(2,1)S(1)}, bf16[256,1024]{1,0:T(8,128)(2,1)S(1)}, u32[]{:S(2)}, u32[]{:S(2)}) collective-permute-start(bf16[256,1024]{1,0:T(8,128)(2,1)S(1)} %pad_maximum_fusion.5), channel_id=1, source_target_pairs={{0,96},{32,64},{64,32},{96,0},{1,97},{33,65},{65,33},{97,1},{2,98}... | collective-permute-start | bytes 1572872 | tf_op jit(solution)/shard_map/ppermute | solution.py:37
  26.6 4.3 %all-to-all-start = ((bf16[8,144,256]{2,1,0:T(8,128)(2,1)}), bf16[8,144,256]{2,1,0:T(8,128)(2,1)}, u32[]{:S(2)}, u32[]{:S(2)}) async-start(bf16[8,144,256]{2,1,0:T(8,128)(2,1)} %broadcast_in_dim.8), calls=%async_computation | async-start | bytes 1179648 | tf_op jit(solution)/shard_map/all_to_all | solution.py:541
  30.9 1.4 collective-permute-done.3
  32.3 4.7 %collective-permute-done.2 = bf16[256,1024]{1,0:T(8,128)(2,1)S(1)} collective-permute-done((bf16[256,1024]{1,0:T(8,128)(2,1)S(1)}, bf16[256,1024]{1,0:T(8,128)(2,1)S(1)}, u32[]{:S(2)}, u32[]{:S(2)}) %collective-permute-start.2) | collective-permute-done | bytes 524320 | tf_op jit(solution)/shard_map/ppermute | solution.py:37
  37.9 2.4 collective-permute-start.5
  40.3 9.2 %all-to-all-done = bf16[8,144,256]{2,1,0:T(8,128)(2,1)} async-done(((bf16[8,144,256]{2,1,0:T(8,128)(2,1)}), bf16[8,144,256]{2,1,0:T(8,128)(2,1)}, u32[]{:S(2)}, u32[]{:S(2)}) %all-to-all-start) | async-done | bytes 589856 | tf_op jit(solution)/shard_map/all_to_all | solution.py:541
  53.2 1.7 collective-permute-start.6
  55.0 1.1 slice.106
  57.7 1.7 convolution_convert_fusion
  59.5 8.9 %attention_forward.1 = (bf16[16,64,128]{2,1,0:T(8,128)(2,1)S(1)}, f32[64,2048]{1,0:T(8,128)S(1)}, f32[1,2048]{1,0:T(1,128)S(1)}) custom-call(s32[16]{0:T(128)S(1)} %stack.142.place, bf16[192,2048]{1,0:T(8,128)(2,1)S(1)} %pad_maximum_fusion.2.q_ref.k_ref.v_ref, bf16[192,2048]{1,0:T(8,128)(2,1)S(1)} %pad_maximum_fusion.2.q_ref.k_ref.v_ref, ...), custom_call_target="tpu_custom_call" | custom-call | flops 4294967296 | bytes 1310720 | tf_op jit(solution)/shard_map/attention_forward/pallas_call | solution.py:71
  69.8 16.2 %all_to_all.25.att_ref = bf16[16,64,128]{2,1,0:T(8,128)(2,1)} all-to-all(bf16[16,64,128]{2,1,0:T(8,128)(2,1)S(1)} %get-tuple-element.79), channel_id=1, replica_groups=mesh['zh'=2,'zl'=2,'xh'=2,'core'=2,'xl'=2,'y'=4] {'zh','zl','xh','core'}, dimensions={0} | all-to-all | bytes 524288 | tf_op jit(solution)/shard_map/all_to_all | solution.py:562
  86.0 2.3 slice.107.own_ref
  88.2 1.2 collective-permute-start.7
  90.0 1.2 copy.24
  92.0 4.4 %out_and_norm.1 = (bf16[128,1024]{1,0:T(8,128)(2,1)}, bf16[128,1024]{1,0:T(8,128)(2,1)}, f32[128,1024]{1,0:T(8,128)}, f32[128,1024]{1,0:T(8,128)}, f32[128,128]{1,0:T(8,128)}) custom-call(s32[2]{0:T(128)} %pad_add_fusion.spots, bf16[16,64,128]{2,1,0:T(8,128)(2,1)} %all_to_all.25.att_ref, bf16[1024,512]{1,0:T(8,128)(2,1)} %slice.107.own_ref, ...), custom_call_target="tpu_custom_call" | custom-call | tf_op jit(solution)/shard_map/out_and_norm/pallas_call | solution.py:343
  98.2 4.0 %fusion.23 = (f32[256,1024]{1,0:T(8,128)}, bf16[256,1024]{1,0:T(8,128)(2,1)}) fusion(bf16[256,1024]{1,0:T(8,128)(2,1)S(1)} %constant_dynamic-update-slice_fusion.3.hid_a, bf16[1024,2560]{1,0:T(8,128)(2,1)} %all-gather.3.cloned.1.call-done), kind=kOutput, calls=%fused_computation.27 | convolution fusion | flops 539492352 | bytes 4194304 | tf_op jit(solution)/shard_map/dot_general | solution.py:27
  102.2 2.5 collective-permute-done.8
  105.7 1.1 collective-permute-done.10
  106.9 1.7 multiply_convert_fusion
  110.9 1.8 constant_dynamic-slice_fusion.3
  112.9 1.2 fusion.40
  114.1 2.6 fusion.2
  117.1 1.3 collective-permute-done.12
  118.4 6.2 %collective-permute-done.13 = bf16[128,1024]{1,0:T(8,128)(2,1)S(1)} collective-permute-done((bf16[128,1024]{1,0:T(8,128)(2,1)S(1)}, bf16[128,1024]{1,0:T(8,128)(2,1)S(1)}, u32[]{:S(2)}, u32[]{:S(2)}) %collective-permute-start.13) | collective-permute-done | bytes 262176 | tf_op jit(solution)/shard_map/ppermute | solution.py:33
  125.9 1.2 collective-permute-start.15
  129.0 2.4 fusion.14.up_a
  131.5 3.5 %collective-permute-done.14 = bf16[128,1024]{1,0:T(8,128)(2,1)S(1)} collective-permute-done((bf16[128,1024]{1,0:T(8,128)(2,1)S(1)}, bf16[128,1024]{1,0:T(8,128)(2,1)S(1)}, u32[]{:S(2)}, u32[]{:S(2)}) %collective-permute-start.14) | collective-permute-done | bytes 262176 | tf_op jit(solution)/shard_map/ppermute | solution.py:33
  135.8 1.1 collective-permute-done.16
  139.1 1.2 collective-permute-done.17
  142.3 1.2 collective-permute-done.18
  144.3 7.0 %ff_products.1 = bf16[1024,2048]{1,0:T(8,128)(2,1)} custom-call(bf16[256,1024]{1,0:T(8,128)(2,1)} %copy-done.17, bf16[256,1024]{1,0:T(8,128)(2,1)} %copy-done.15, bf16[256,1024]{1,0:T(8,128)(2,1)} %copy-done.24, bf16[256,1024]{1,0:T(8,128)(2,1)} %copy-done.25, bf16[256,1024]{1,0:T(8,128)(2,1)} %pad_maximum_fusion.7.mixed_a, bf16[256,1024]{1,0:T(8,128)(2,1)} %copy-done.16, ...), custom_call_target="tpu_custom_call" | custom-call | flops 2147483648 | bytes 8388608 | tf_op jit(solution)/shard_map/ff_products/pallas_call | solution.py:454
  151.5 2.3 fusion.56
  153.8 5.3 %collective-permute-done.19.late_ref = bf16[128,1024]{1,0:T(8,128)(2,1)S(1)} collective-permute-done((bf16[128,1024]{1,0:T(8,128)(2,1)}, bf16[128,1024]{1,0:T(8,128)(2,1)S(1)}, u32[]{:S(2)}, u32[]{:S(2)}) %collective-permute-start.19) | collective-permute-done | bytes 262176 | tf_op jit(solution)/shard_map/ppermute | solution.py:33
  159.8 4.4 %norm_one_back.1 = (f32[128,1024]{1,0:T(8,128)}, bf16[256,1024]{1,0:T(8,128)(2,1)}, bf16[16,64,128]{2,1,0:T(8,128)(2,1)}, f32[2,1024]{1,0:T(2,128)}) custom-call(s32[2]{0:T(128)} %pad_add_fusion.spots, f32[128,1024]{1,0:T(8,128)} %get-tuple-element.147.base_ref, bf16[128,1024]{1,0:T(8,128)(2,1)} %copy-done.26, f32[128,1024]{1,0:T(8,128)} %get-tuple-element.98.normal_ref, ...), custom_call_target="tpu_custom_call" | custom-call | tf_op jit(solution)/shard_map/norm_one_back/pallas_call | solution.py:343
  164.3 7.0 %all-to-all-start.2 = ((bf16[16,64,128]{2,1,0:T(8,128)(2,1)}), bf16[16,64,128]{2,1,0:T(8,128)(2,1)}, u32[]{:S(2)}, u32[]{:S(2)}) async-start(bf16[16,64,128]{2,1,0:T(8,128)(2,1)} %get-tuple-element.101), calls=%async_computation.3 | async-start | bytes 524288 | tf_op jit(solution)/shard_map/all_to_all | solution.py:604
  171.7 5.0 %collective-permute-done.21.block_2 = bf16[256,1024]{1,0:T(8,128)(2,1)} collective-permute-done((bf16[256,1024]{1,0:T(8,128)(2,1)}, bf16[256,1024]{1,0:T(8,128)(2,1)}, u32[]{:S(2)}, u32[]{:S(2)}) %collective-permute-start.21) | collective-permute-done | bytes 524320 | tf_op jit(solution)/shard_map/ppermute | solution.py:33
  176.7 3.8 %collective-permute-start.22 = (bf16[256,1024]{1,0:T(8,128)(2,1)}, bf16[256,1024]{1,0:T(8,128)(2,1)}, u32[]{:S(2)}, u32[]{:S(2)}) collective-permute-start(bf16[256,1024]{1,0:T(8,128)(2,1)} %collective-permute-done.21.block_2), channel_id=1, source_target_pairs={{0,8},{8,0},{1,9},{9,1},{2,10},{10,2},{3,11},{11,3},{4,12},{12,4},... | collective-permute-start | bytes 1572872 | tf_op jit(solution)/shard_map/ppermute | solution.py:33
  180.5 2.4 all-to-all-done.2.grad_ref
  182.9 15.3 %attention_backward.1 = (bf16[192,1024]{1,0:T(8,128)(2,1)}, bf16[192,1024]{1,0:T(8,128)(2,1)}, bf16[16,192,128]{2,1,0:T(8,128)(2,1)}) custom-call(s32[16]{0:T(128)} %copy-done.8, bf16[192,2048]{1,0:T(8,128)(2,1)} %copy-done.3, bf16[192,2048]{1,0:T(8,128)(2,1)} %copy-done.3, bf16[192,2048]{1,0:T(8,128)(2,1)} %copy-done.3, ...), custom_call_target="tpu_custom_call" | custom-call | flops 10737418240 | bytes 2621440 | tf_op jit(solution)/shard_map/attention_backward/pallas_call | solution.py:157
  200.2 3.3 %weight_terms.1 = bf16[8,464,128]{2,1,0:T(8,128)(2,1)S(1)} custom-call(s32[1]{0:T(128)} %bitcast.29.spots, bf16[192,1024]{1,0:T(8,128)(2,1)S(1)} %copy-done.5, bf16[192,1024]{1,0:T(8,128)(2,1)S(1)} %copy-done.6, bf16[512,1024]{1,0:T(8,128)(2,1)S(1)} %pad_maximum_fusion.part_0, bf16[512,1024]{1,0:T(8,128)(2,1)S(1)} %collective-permute-done.4.part_1, ...), custom_call_target="tpu_custom_call" | custom-call | tf_op jit(solution)/shard_map/weight_terms/pallas_call | solution.py:343
  204.4 3.6 %all-to-all-start.3 = ((bf16[8,464,128]{2,1,0:T(8,128)(2,1)}), bf16[8,464,128]{2,1,0:T(8,128)(2,1)S(1)}, u32[]{:S(2)}, u32[]{:S(2)}) async-start(bf16[8,464,128]{2,1,0:T(8,128)(2,1)} %copy-done.2), calls=%async_computation.4 | async-start | bytes 1900544 | tf_op jit(solution)/shard_map/all_to_all | solution.py:617
  208.0 1.5 collective-permute-start.28
  209.4 11.2 %all-to-all-done.3 = bf16[8,464,128]{2,1,0:T(8,128)(2,1)S(1)} async-done(((bf16[8,464,128]{2,1,0:T(8,128)(2,1)}), bf16[8,464,128]{2,1,0:T(8,128)(2,1)S(1)}, u32[]{:S(2)}, u32[]{:S(2)}) %all-to-all-start.3) | async-done | bytes 950304 | tf_op jit(solution)/shard_map/all_to_all | solution.py:617
  220.6 3.0 %collective-permute-start.23 = (bf16[128,2048]{1,0:T(8,128)(2,1)}, bf16[128,2048]{1,0:T(8,128)(2,1)S(1)}, u32[]{:S(2)}, u32[]{:S(2)}) collective-permute-start(bf16[128,2048]{1,0:T(8,128)(2,1)} %reduce-scatter.2.cloned.1.call-done), channel_id=1, source_target_pairs={{0,64},{64,0},{1,65},{65,1},{2,66},{66,2},{3,67},{67,3},{4,68},{68... | collective-permute-start | bytes 1572872 | tf_op jit(solution)/shard_map/ppermute | solution.py:33
  223.8 2.5 collective-permute-start.25
  226.3 4.4 %all-to-all-start.4 = ((bf16[16,192,128]{2,1,0:T(8,128)(2,1)}), bf16[16,192,128]{2,1,0:T(8,128)(2,1)S(1)}, u32[]{:S(2)}, u32[]{:S(2)}) async-start(bf16[16,192,128]{2,1,0:T(8,128)(2,1)} %get-tuple-element.113), calls=%async_computation.5 | async-start | bytes 1572864 | tf_op jit(solution)/shard_map/all_to_all | solution.py:630
  230.8 4.7 %collective-permute-done.23 = bf16[128,2048]{1,0:T(8,128)(2,1)S(1)} collective-permute-done((bf16[128,2048]{1,0:T(8,128)(2,1)}, bf16[128,2048]{1,0:T(8,128)(2,1)S(1)}, u32[]{:S(2)}, u32[]{:S(2)}) %collective-permute-start.23) | collective-permute-done | bytes 524320 | tf_op jit(solution)/shard_map/ppermute | solution.py:33
  235.7 6.3 %collective-permute-start.24 = (bf16[128,2048]{1,0:T(8,128)(2,1)S(1)}, bf16[128,2048]{1,0:T(8,128)(2,1)S(1)}, u32[]{:S(2)}, u32[]{:S(2)}) collective-permute-start(bf16[128,2048]{1,0:T(8,128)(2,1)S(1)} %add_convert_fusion.1), channel_id=1, source_target_pairs={{0,16},{16,0},{1,17},{17,1},{2,18},{18,2},{3,19},{19,3},{4,20},{20... | collective-permute-start | bytes 1572872 | tf_op jit(solution)/shard_map/ppermute | solution.py:33
  242.0 3.2 %all-to-all-done.4.every_ref = bf16[16,192,128]{2,1,0:T(8,128)(2,1)S(1)} async-done(((bf16[16,192,128]{2,1,0:T(8,128)(2,1)}), bf16[16,192,128]{2,1,0:T(8,128)(2,1)S(1)}, u32[]{:S(2)}, u32[]{:S(2)}) %all-to-all-start.4) | async-done | bytes 786464 | tf_op jit(solution)/shard_map/all_to_all | solution.py:630
  245.2 2.3 collective-permute-start.26
  247.6 3.7 %collective-permute-done.26 = bf16[656,128]{1,0:T(8,128)(2,1)S(1)} collective-permute-done((bf16[656,128]{1,0:T(8,128)(2,1)S(1)}, bf16[656,128]{1,0:T(8,128)(2,1)S(1)}, u32[]{:S(2)}, u32[]{:S(2)}) %collective-permute-start.26) | collective-permute-done | bytes 167968 | tf_op jit(solution)/shard_map/ppermute | solution.py:33
  251.4 1.2 collective-permute-done.24
  252.7 2.0 collective-permute-start.29
  254.8 6.2 %input_product.1 = f32[128,1024]{1,0:T(8,128)} custom-call(s32[2]{0:T(128)} %pad_add_fusion.spots, bf16[16,192,128]{2,1,0:T(8,128)(2,1)} %copy-done.13, bf16[1024,1536]{1,0:T(8,128)(2,1)} %all-gather.5.cloned.1.call-done.own_ref, bf16[1024,1536]{1,0:T(8,128)(2,1)} %collective-permute-done.28.pair_ref, f32[128,1024]{1,0:T(8,128)} %get-tuple-element.121.base_ref), custom_call_target="tpu_custom_call" | custom-call | tf_op jit(solution)/shard_map/input_product/pallas_call | solution.py:300
  261.1 9.2 %collective-permute-done.27 = bf16[128,2048]{1,0:T(8,128)(2,1)S(1)} collective-permute-done((bf16[128,2048]{1,0:T(8,128)(2,1)S(1)}, bf16[128,2048]{1,0:T(8,128)(2,1)S(1)}, u32[]{:S(2)}, u32[]{:S(2)}) %collective-permute-start.27) | collective-permute-done | bytes 524320 | tf_op jit(solution)/shard_map/ppermute | solution.py:33
  270.4 3.1 %collective-permute-start.31 = (bf16[256,2048]{1,0:T(8,128)(2,1)S(1)}, bf16[256,2048]{1,0:T(8,128)(2,1)}, u32[]{:S(2)}, u32[]{:S(2)}) collective-permute-start(bf16[256,2048]{1,0:T(8,128)(2,1)S(1)} %pad_maximum_fusion.1.own_ref), channel_id=1, source_target_pairs={{0,8},{8,0},{1,9},{9,1},{2,10},{10,2},{3,11},{11,3},{4,12},{12,4},... | collective-permute-start | bytes 3145736 | tf_op jit(solution)/shard_map/ppermute | solution.py:33
  273.7 2.8 collective-permute-done.30.pair_ref
  276.5 2.3 assemble_rest.1
  279.4 4.0 %assemble.1 = (f32[128,4096]{1,0:T(8,128)}, f32[128,4096]{1,0:T(8,128)}) custom-call(s32[4]{0:T(128)S(1)} %pad_add_fusion.1.spots, bf16[256,2048]{1,0:T(8,128)(2,1)S(1)} %pad_maximum_fusion.1.own_ref, bf16[256,2048]{1,0:T(8,128)(2,1)} %collective-permute-done.31.pair_ref), custom_call_target="tpu_custom_call" | custom-call | tf_op jit(solution)/shard_map/assemble/pallas_call | solution.py:343
  (181 shorter events, 33.3 us)
Async XLA Ops:
  7.2 3.0 %copy-start.30 = (bf16[128]{0:T(256)(128)(2,1)S(1)}, bf16[128]{0:T(256)(128)(2,1)}, u32[]{:S(2)}) copy-start(bf16[128]{0:T(256)(128)(2,1)} %param.15) | copy-start | bytes 772
  7.2 3.0 %copy-start.29 = (bf16[128]{0:T(256)(128)(2,1)S(1)}, bf16[128]{0:T(256)(128)(2,1)}, u32[]{:S(2)}) copy-start(bf16[128]{0:T(256)(128)(2,1)} %param.16) | copy-start | bytes 772
  7.2 3.0 %copy-start.28 = (bf16[128]{0:T(256)(128)(2,1)S(1)}, bf16[128]{0:T(256)(128)(2,1)}, u32[]{:S(2)}) copy-start(bf16[128]{0:T(256)(128)(2,1)} %param.17) | copy-start | bytes 772
  7.2 3.0 %copy-start.27 = (bf16[128]{0:T(256)(128)(2,1)S(1)}, bf16[128]{0:T(256)(128)(2,1)}, u32[]{:S(2)}) copy-start(bf16[128]{0:T(256)(128)(2,1)} %param.18) | copy-start | bytes 772
  7.2 78.7 %all-gather.3.cloned.1.call-start = ((), (), s32[]{:S(2)}) async-start(), calls=%async_computation.6 | async-start | bytes 5898240 | tf_op jit(solution)/shard_map/all_gather | solution.py:546
  8.1 4.1 %copy-start.14 = (bf16[1,128,1024]{2,1,0:T(8,128)(2,1)S(1)}, bf16[1,128,1024]{2,1,0:T(8,128)(2,1)}, u32[]{:S(2)}) copy-start(bf16[1,128,1024]{2,1,0:T(8,128)(2,1)} %param.10) | copy-start | bytes 786436
  12.2 9.0 %collective-permute-start = (bf16[128,1024]{1,0:T(8,128)(2,1)S(1)}, bf16[128,1024]{1,0:T(8,128)(2,1)S(1)}, u32[]{:S(2)}, u32[]{:S(2)}) collective-permute-start(bf16[128,1024]{1,0:T(8,128)(2,1)S(1)} %bitcast.105), channel_id=1, source_target_pairs={{0,16},{16,0},{1,17},{17,1},{2,18},{18,2},{3,19},{19,3},{4,20},{20... | collective-permute-start | bytes 786440 | tf_op jit(solution)/shard_map/ppermute | solution.py:33
  15.8 7.2 %collective-permute-start.1 = (bf16[128,1024]{1,0:T(8,128)(2,1)S(1)}, bf16[128,1024]{1,0:T(8,128)(2,1)S(1)}, u32[]{:S(2)}, u32[]{:S(2)}) collective-permute-start(bf16[128,1024]{1,0:T(8,128)(2,1)S(1)} %bitcast.106), channel_id=1, source_target_pairs={{0,32},{32,0},{64,96},{96,64},{1,33},{33,1},{65,97},{97,65},{2,34}... | collective-permute-start | bytes 786440 | tf_op jit(solution)/shard_map/ppermute | solution.py:37
  21.3 16.6 %copy-start.18 = (bf16[128,1024]{1,0:T(8,128)(2,1)}, bf16[128,1024]{1,0:T(8,128)(2,1)S(1)}, u32[]{:S(2)}) copy-start(bf16[128,1024]{1,0:T(8,128)(2,1)S(1)} %collective-permute-done) | copy-start | bytes 786436
  23.1 13.9 %collective-permute-start.2 = (bf16[256,1024]{1,0:T(8,128)(2,1)S(1)}, bf16[256,1024]{1,0:T(8,128)(2,1)S(1)}, u32[]{:S(2)}, u32[]{:S(2)}) collective-permute-start(bf16[256,1024]{1,0:T(8,128)(2,1)S(1)} %pad_maximum_fusion.5), channel_id=1, source_target_pairs={{0,96},{32,64},{64,32},{96,0},{1,97},{33,65},{65,33},{97,1},{2,98}... | collective-permute-start | bytes 1572872 | tf_op jit(solution)/shard_map/ppermute | solution.py:37
  26.6 5.7 %collective-permute-start.3 = (bf16[128,1024]{1,0:T(8,128)(2,1)S(1)}, bf16[128,1024]{1,0:T(8,128)(2,1)S(1)}, u32[]{:S(2)}, u32[]{:S(2)}) collective-permute-start(bf16[128,1024]{1,0:T(8,128)(2,1)S(1)} %collective-permute-done), channel_id=1, source_target_pairs={{0,32},{32,0},{64,96},{96,64},{1,33},{33,1},{65,97},{97,65},{2,34}... | collective-permute-start | bytes 786440 | tf_op jit(solution)/shard_map/ppermute | solution.py:37
  26.6 22.9 %all-to-all-start = ((bf16[8,144,256]{2,1,0:T(8,128)(2,1)}), bf16[8,144,256]{2,1,0:T(8,128)(2,1)}, u32[]{:S(2)}, u32[]{:S(2)}) async-start(bf16[8,144,256]{2,1,0:T(8,128)(2,1)} %broadcast_in_dim.8), calls=%async_computation | async-start | bytes 1179648 | tf_op jit(solution)/shard_map/all_to_all | solution.py:541
  30.9 133.3 %all-gather.5.cloned.1.call-start = ((), (), s32[]{:S(2)}) async-start(), calls=%async_computation.8 | async-start | bytes 3538944 | tf_op jit(solution)/shard_map/all_gather | solution.py:570
  32.3 5.5 %copy-start.19 = (bf16[128,1024]{1,0:T(8,128)(2,1)}, bf16[128,1024]{1,0:T(8,128)(2,1)S(1)}, u32[]{:S(2)}) copy-start(bf16[128,1024]{1,0:T(8,128)(2,1)S(1)} %collective-permute-done.3) | copy-start | bytes 786436
  37.9 14.3 %collective-permute-start.5 = (bf16[256,1024]{1,0:T(8,128)(2,1)}, bf16[256,1024]{1,0:T(8,128)(2,1)}, u32[]{:S(2)}, u32[]{:S(2)}) collective-permute-start(bf16[256,1024]{1,0:T(8,128)(2,1)} %pad_maximum_fusion.6), channel_id=1, source_target_pairs={{0,96},{32,64},{64,32},{96,0},{1,97},{33,65},{65,33},{97,1},{2,98}... | collective-permute-start | bytes 1572872 | tf_op jit(solution)/shard_map/ppermute | solution.py:37
  49.5 7.7 %collective-permute-start.4 = (bf16[512,1024]{1,0:T(8,128)(2,1)S(1)}, bf16[512,1024]{1,0:T(8,128)(2,1)S(1)}, u32[]{:S(2)}, u32[]{:S(2)}) collective-permute-start(bf16[512,1024]{1,0:T(8,128)(2,1)S(1)} %pad_maximum_fusion.part_0), channel_id=1, source_target_pairs={{0,8},{8,0},{1,9},{9,1},{2,10},{10,2},{3,11},{11,3},{4,12},{12,4},... | collective-permute-start | bytes 3145736 | tf_op jit(solution)/shard_map/ppermute | solution.py:33
  53.2 4.5 %collective-permute-start.6 = (bf16[512,1024]{1,0:T(8,128)(2,1)S(1)}, bf16[512,1024]{1,0:T(8,128)(2,1)}, u32[]{:S(2)}, u32[]{:S(2)}) collective-permute-start(bf16[512,1024]{1,0:T(8,128)(2,1)S(1)} %constant_dynamic-update-slice_fusion.part_2), channel_id=1, source_target_pairs={{0,8},{8,0},{1,9},{9,1},{2,10},{10,2},{3,11},{11,3},{4,12},{12,4},... | collective-permute-start | bytes 3145736 | tf_op jit(solution)/shard_map/ppermute | solution.py:33
  55.0 4.5 %copy-start.8 = (s32[16]{0:T(128)}, s32[16]{0:T(128)S(1)}, u32[]{:S(2)}) copy-start(s32[16]{0:T(128)S(1)} %stack.142.place) | copy-start | bytes 196
  59.5 8.9 %copy-start.3 = (bf16[192,2048]{1,0:T(8,128)(2,1)}, bf16[192,2048]{1,0:T(8,128)(2,1)S(1)}, u32[]{:S(2)}) copy-start(bf16[192,2048]{1,0:T(8,128)(2,1)S(1)} %pad_maximum_fusion.2.q_ref.k_ref.v_ref) | copy-start | bytes 2359300
  88.2 3.8 %collective-permute-start.7 = (bf16[1024,512]{1,0:T(8,128)(2,1)}, bf16[1024,512]{1,0:T(8,128)(2,1)}, u32[]{:S(2)}, u32[]{:S(2)}) collective-permute-start(bf16[1024,512]{1,0:T(8,128)(2,1)} %slice.107.own_ref), channel_id=1, source_target_pairs={{0,8},{8,0},{1,9},{9,1},{2,10},{10,2},{3,11},{11,3},{4,12},{12,4},... | collective-permute-start | bytes 3145736 | tf_op jit(solution)/shard_map/ppermute | solution.py:33
  92.0 14.8 %slice-start = ((s8[5242880]{0:T(1024)(128)(4,1)}), s8[1048576]{0:T(1024)(128)(4,1)S(1)}, s32[]{:S(2)}) async-start(s8[5242880]{0:T(1024)(128)(4,1)} %bitcast.110), calls=%async_computation.9 | async-start | bytes 2097152
  96.4 1.7 collective-permute-start.9
  96.8 8.0 %collective-permute-start.8 = (bf16[128,1024]{1,0:T(8,128)(2,1)}, bf16[128,1024]{1,0:T(8,128)(2,1)S(1)}, u32[]{:S(2)}, u32[]{:S(2)}) collective-permute-start(bf16[128,1024]{1,0:T(8,128)(2,1)} %get-tuple-element.83), channel_id=1, source_target_pairs={{0,32},{32,0},{1,33},{33,1},{2,34},{34,2},{3,35},{35,3},{4,36},{36... | collective-permute-start | bytes 786440 | tf_op jit(solution)/shard_map/ppermute | solution.py:33
  98.2 4.0 %copy-start.17 = (bf16[256,1024]{1,0:T(8,128)(2,1)}, bf16[256,1024]{1,0:T(8,128)(2,1)S(1)}, u32[]{:S(2)}) copy-start(bf16[256,1024]{1,0:T(8,128)(2,1)S(1)} %constant_dynamic-update-slice_fusion.3.hid_a) | copy-start | bytes 1572868
  98.2 8.7 %slice-start.1 = ((s8[5242880]{0:T(1024)(128)(4,1)}), s8[4194304]{0:T(1024)(128)(4,1)S(1)}, s32[]{:S(2)}) async-start(s8[5242880]{0:T(1024)(128)(4,1)} %bitcast.110), calls=%async_computation.10 | async-start | bytes 8388608
  104.7 2.1 collective-permute-start.10
  108.6 1.8 copy-start.22
  110.4 2.5 collective-permute-start.11
  112.7 108.0 %reduce-scatter.2.cloned.1.call-start = ((), (), s32[]{:S(2)}) async-start(), calls=%async_computation.7 | async-start | bytes 4718592 | tf_op jit(solution)/shard_map/reduce_scatter | solution.py:599
  114.1 10.5 %copy-start.23 = (f32[128,1024]{1,0:T(8,128)S(1)}, f32[128,1024]{1,0:T(8,128)}, u32[]{:S(2)}) copy-start(f32[128,1024]{1,0:T(8,128)} %get-tuple-element.82) | copy-start | bytes 1572868
  114.1 22.9 %slice-start.2 = ((s8[5242880]{0:T(1024)(128)(4,1)}), s8[1048576]{0:T(1024)(128)(4,1)S(1)}, s32[]{:S(2)}) async-start(s8[5242880]{0:T(1024)(128)(4,1)} %bitcast.112), calls=%async_computation.11 | async-start | bytes 2097152
  116.7 8.4 %copy-start.12 = (bf16[1,128,1024]{2,1,0:T(8,128)(2,1)S(1)}, bf16[1,128,1024]{2,1,0:T(8,128)(2,1)}, u32[]{:S(2)}) copy-start(bf16[1,128,1024]{2,1,0:T(8,128)(2,1)} %param.19) | copy-start | bytes 786436
  116.8 1.6 collective-permute-start.12
  117.0 7.6 %collective-permute-start.13 = (bf16[128,1024]{1,0:T(8,128)(2,1)S(1)}, bf16[128,1024]{1,0:T(8,128)(2,1)S(1)}, u32[]{:S(2)}, u32[]{:S(2)}) collective-permute-start(bf16[128,1024]{1,0:T(8,128)(2,1)S(1)} %fusion.40), channel_id=1, source_target_pairs={{0,32},{32,0},{1,33},{33,1},{2,34},{34,2},{3,35},{35,3},{4,36},{36... | collective-permute-start | bytes 786440 | tf_op jit(solution)/shard_map/ppermute | solution.py:33
  124.8 4.2 %copy-start.31 = (f32[256,1024]{1,0:T(8,128)S(1)}, f32[256,1024]{1,0:T(8,128)}, u32[]{:S(2)}) copy-start(f32[256,1024]{1,0:T(8,128)} %get-tuple-element.88) | copy-start | bytes 3145732
  125.6 11.4 %slice-start.3 = ((s8[5242880]{0:T(1024)(128)(4,1)}), s8[4194304]{0:T(1024)(128)(4,1)S(1)}, s32[]{:S(2)}) async-start(s8[5242880]{0:T(1024)(128)(4,1)} %bitcast.112), calls=%async_computation.12 | async-start | bytes 8388608
  125.9 2.3 collective-permute-start.15
  127.0 8.0 %collective-permute-start.14 = (bf16[128,1024]{1,0:T(8,128)(2,1)S(1)}, bf16[128,1024]{1,0:T(8,128)(2,1)S(1)}, u32[]{:S(2)}, u32[]{:S(2)}) collective-permute-start(bf16[128,1024]{1,0:T(8,128)(2,1)S(1)} %fusion.57), channel_id=1, source_target_pairs={{0,32},{32,0},{1,33},{33,1},{2,34},{34,2},{3,35},{35,3},{4,36},{36... | collective-permute-start | bytes 786440 | tf_op jit(solution)/shard_map/ppermute | solution.py:33
  129.0 7.9 %copy-start.32 = (f32[256,1024]{1,0:T(8,128)S(1)}, f32[256,1024]{1,0:T(8,128)}, u32[]{:S(2)}) copy-start(f32[256,1024]{1,0:T(8,128)} %get-tuple-element.156) | copy-start | bytes 3145732
  131.5 9.6 %copy-start.24 = (bf16[256,1024]{1,0:T(8,128)(2,1)}, bf16[256,1024]{1,0:T(8,128)(2,1)S(1)}, u32[]{:S(2)}) copy-start(bf16[256,1024]{1,0:T(8,128)(2,1)S(1)} %fusion.14.up_a) | copy-start | bytes 1572868
  135.0 1.9 collective-permute-start.16
  138.7 1.6 collective-permute-start.17
  141.9 1.6 collective-permute-start.18
  151.3 7.8 %collective-permute-start.19 = (bf16[128,1024]{1,0:T(8,128)(2,1)}, bf16[128,1024]{1,0:T(8,128)(2,1)S(1)}, u32[]{:S(2)}, u32[]{:S(2)}) collective-permute-start(bf16[128,1024]{1,0:T(8,128)(2,1)} %fusion.37), channel_id=1, source_target_pairs={{0,32},{32,0},{1,33},{33,1},{2,34},{34,2},{3,35},{35,3},{4,36},{36... | collective-permute-start | bytes 786440 | tf_op jit(solution)/shard_map/ppermute | solution.py:33
  164.2 12.5 %collective-permute-start.21 = (bf16[256,1024]{1,0:T(8,128)(2,1)}, bf16[256,1024]{1,0:T(8,128)(2,1)}, u32[]{:S(2)}, u32[]{:S(2)}) collective-permute-start(bf16[256,1024]{1,0:T(8,128)(2,1)} %get-tuple-element.110.block_0), channel_id=1, source_target_pairs={{0,32},{32,0},{1,33},{33,1},{2,34},{34,2},{3,35},{35,3},{4,36},{36... | collective-permute-start | bytes 1572872 | tf_op jit(solution)/shard_map/ppermute | solution.py:33
  164.3 18.5 %all-to-all-start.2 = ((bf16[16,64,128]{2,1,0:T(8,128)(2,1)}), bf16[16,64,128]{2,1,0:T(8,128)(2,1)}, u32[]{:S(2)}, u32[]{:S(2)}) async-start(bf16[16,64,128]{2,1,0:T(8,128)(2,1)} %get-tuple-element.101), calls=%async_computation.3 | async-start | bytes 524288 | tf_op jit(solution)/shard_map/all_to_all | solution.py:604
  171.4 26.7 %collective-permute-start.20 = (bf16[256,1024]{1,0:T(8,128)(2,1)}, bf16[256,1024]{1,0:T(8,128)(2,1)}, u32[]{:S(2)}, u32[]{:S(2)}) collective-permute-start(bf16[256,1024]{1,0:T(8,128)(2,1)} %get-tuple-element.110.block_0), channel_id=1, source_target_pairs={{0,8},{8,0},{1,9},{9,1},{2,10},{10,2},{3,11},{11,3},{4,12},{12,4},... | collective-permute-start | bytes 1572872 | tf_op jit(solution)/shard_map/ppermute | solution.py:33
  176.7 21.5 %collective-permute-start.22 = (bf16[256,1024]{1,0:T(8,128)(2,1)}, bf16[256,1024]{1,0:T(8,128)(2,1)}, u32[]{:S(2)}, u32[]{:S(2)}) collective-permute-start(bf16[256,1024]{1,0:T(8,128)(2,1)} %collective-permute-done.21.block_2), channel_id=1, source_target_pairs={{0,8},{8,0},{1,9},{9,1},{2,10},{10,2},{3,11},{11,3},{4,12},{12,4},... | collective-permute-start | bytes 1572872 | tf_op jit(solution)/shard_map/ppermute | solution.py:33
  182.9 15.3 %copy-start.4 = (bf16[256,1024]{1,0:T(8,128)(2,1)S(1)}, bf16[256,1024]{1,0:T(8,128)(2,1)}, u32[]{:S(2)}) copy-start(bf16[256,1024]{1,0:T(8,128)(2,1)} %get-tuple-element.110.block_0) | copy-start | bytes 1572868
  182.9 15.3 %copy-start.7 = (f32[2,1024]{1,0:T(2,128)S(1)}, f32[2,1024]{1,0:T(2,128)}, u32[]{:S(2)}) copy-start(f32[2,1024]{1,0:T(2,128)} %get-tuple-element.111.first_ref) | copy-start | bytes 24580
  204.4 16.2 %all-to-all-start.3 = ((bf16[8,464,128]{2,1,0:T(8,128)(2,1)}), bf16[8,464,128]{2,1,0:T(8,128)(2,1)S(1)}, u32[]{:S(2)}, u32[]{:S(2)}) async-start(bf16[8,464,128]{2,1,0:T(8,128)(2,1)} %copy-done.2), calls=%async_computation.4 | async-start | bytes 1900544 | tf_op jit(solution)/shard_map/all_to_all | solution.py:617
  208.0 46.9 %collective-permute-start.28 = (bf16[1024,1536]{1,0:T(8,128)(2,1)}, bf16[1024,1536]{1,0:T(8,128)(2,1)}, u32[]{:S(2)}, u32[]{:S(2)}) collective-permute-start(bf16[1024,1536]{1,0:T(8,128)(2,1)} %all-gather.5.cloned.1.call-done.own_ref), channel_id=1, source_target_pairs={{0,8},{8,0},{1,9},{9,1},{2,10},{10,2},{3,11},{11,3},{4,12},{12,4},... | collective-permute-start | bytes 9437192 | tf_op jit(solution)/shard_map/ppermute | solution.py:33
  220.6 14.9 %copy-start.21 = (bf16[128,2048]{1,0:T(8,128)(2,1)S(1)}, bf16[128,2048]{1,0:T(8,128)(2,1)}, u32[]{:S(2)}) copy-start(bf16[128,2048]{1,0:T(8,128)(2,1)} %reduce-scatter.2.cloned.1.call-done) | copy-start | bytes 1572868
  220.6 14.9 %collective-permute-start.23 = (bf16[128,2048]{1,0:T(8,128)(2,1)}, bf16[128,2048]{1,0:T(8,128)(2,1)S(1)}, u32[]{:S(2)}, u32[]{:S(2)}) collective-permute-start(bf16[128,2048]{1,0:T(8,128)(2,1)} %reduce-scatter.2.cloned.1.call-done), channel_id=1, source_target_pairs={{0,64},{64,0},{1,65},{65,1},{2,66},{66,2},{3,67},{67,3},{4,68},{68... | collective-permute-start | bytes 1572872 | tf_op jit(solution)/shard_map/ppermute | solution.py:33
  223.8 6.9 %collective-permute-start.25 = (bf16[464,128]{1,0:T(8,128)(2,1)S(1)}, bf16[464,128]{1,0:T(8,128)(2,1)S(1)}, u32[]{:S(2)}, u32[]{:S(2)}) collective-permute-start(bf16[464,128]{1,0:T(8,128)(2,1)S(1)} %reduce_sum.72), channel_id=1, source_target_pairs={{0,16},{16,0},{1,17},{17,1},{2,18},{18,2},{3,19},{19,3},{4,20},{20... | collective-permute-start | bytes 356360 | tf_op jit(solution)/shard_map/ppermute | solution.py:33
  226.3 18.9 %all-to-all-start.4 = ((bf16[16,192,128]{2,1,0:T(8,128)(2,1)}), bf16[16,192,128]{2,1,0:T(8,128)(2,1)S(1)}, u32[]{:S(2)}, u32[]{:S(2)}) async-start(bf16[16,192,128]{2,1,0:T(8,128)(2,1)} %get-tuple-element.113), calls=%async_computation.5 | async-start | bytes 1572864 | tf_op jit(solution)/shard_map/all_to_all | solution.py:630
  235.7 16.9 %collective-permute-start.24 = (bf16[128,2048]{1,0:T(8,128)(2,1)S(1)}, bf16[128,2048]{1,0:T(8,128)(2,1)S(1)}, u32[]{:S(2)}, u32[]{:S(2)}) collective-permute-start(bf16[128,2048]{1,0:T(8,128)(2,1)S(1)} %add_convert_fusion.1), channel_id=1, source_target_pairs={{0,16},{16,0},{1,17},{17,1},{2,18},{18,2},{3,19},{19,3},{4,20},{20... | collective-permute-start | bytes 1572872 | tf_op jit(solution)/shard_map/ppermute | solution.py:33
  245.2 9.6 %copy-start.13 = (bf16[16,192,128]{2,1,0:T(8,128)(2,1)}, bf16[16,192,128]{2,1,0:T(8,128)(2,1)S(1)}, u32[]{:S(2)}) copy-start(bf16[16,192,128]{2,1,0:T(8,128)(2,1)S(1)} %all-to-all-done.4.every_ref) | copy-start | bytes 2359300
  245.2 6.1 %collective-permute-start.26 = (bf16[656,128]{1,0:T(8,128)(2,1)S(1)}, bf16[656,128]{1,0:T(8,128)(2,1)S(1)}, u32[]{:S(2)}, u32[]{:S(2)}) collective-permute-start(bf16[656,128]{1,0:T(8,128)(2,1)S(1)} %pad_maximum_fusion.10), channel_id=1, source_target_pairs={{0,64},{64,0},{1,65},{65,1},{2,66},{66,2},{3,67},{67,3},{4,68},{68... | collective-permute-start | bytes 503816 | tf_op jit(solution)/shard_map/ppermute | solution.py:33
  252.7 8.3 %collective-permute-start.29 = (bf16[1040,128]{1,0:T(8,128)(2,1)S(1)}, bf16[1040,128]{1,0:T(8,128)(2,1)S(1)}, u32[]{:S(2)}, u32[]{:S(2)}) collective-permute-start(bf16[1040,128]{1,0:T(8,128)(2,1)S(1)} %pad_maximum_fusion.8), channel_id=1, source_target_pairs={{0,32},{32,0},{1,33},{33,1},{2,34},{34,2},{3,35},{35,3},{4,36},{36... | collective-permute-start | bytes 798728 | tf_op jit(solution)/shard_map/ppermute | solution.py:33
  254.7 15.6 %collective-permute-start.27 = (bf16[128,2048]{1,0:T(8,128)(2,1)S(1)}, bf16[128,2048]{1,0:T(8,128)(2,1)S(1)}, u32[]{:S(2)}, u32[]{:S(2)}) collective-permute-start(bf16[128,2048]{1,0:T(8,128)(2,1)S(1)} %add_convert_fusion), channel_id=1, source_target_pairs={{0,32},{32,0},{1,33},{33,1},{2,34},{34,2},{3,35},{35,3},{4,36},{36... | collective-permute-start | bytes 1572872 | tf_op jit(solution)/shard_map/ppermute | solution.py:33
  270.3 13.1 %copy-start.1 = (bf16[128,1024]{1,0:T(8,128)(2,1)S(1)}, bf16[128,1024]{1,0:T(8,128)(2,1)}, u32[]{:S(2)}) copy-start(bf16[128,1024]{1,0:T(8,128)(2,1)} %param.12) | copy-start | bytes 786436
  270.4 9.0 %collective-permute-start.31 = (bf16[256,2048]{1,0:T(8,128)(2,1)S(1)}, bf16[256,2048]{1,0:T(8,128)(2,1)}, u32[]{:S(2)}, u32[]{:S(2)}) collective-permute-start(bf16[256,2048]{1,0:T(8,128)(2,1)S(1)} %pad_maximum_fusion.1.own_ref), channel_id=1, source_target_pairs={{0,8},{8,0},{1,9},{9,1},{2,10},{10,2},{3,11},{11,3},{4,12},{12,4},... | collective-permute-start | bytes 3145736 | tf_op jit(solution)/shard_map/ppermute | solution.py:33
  273.5 3.0 %collective-permute-start.30 = (bf16[2080,128]{1,0:T(8,128)(2,1)S(1)}, bf16[2080,128]{1,0:T(8,128)(2,1)S(1)}, u32[]{:S(2)}, u32[]{:S(2)}) collective-permute-start(bf16[2080,128]{1,0:T(8,128)(2,1)S(1)} %pad_maximum_fusion.4.own_ref), channel_id=1, source_target_pairs={{0,8},{8,0},{1,9},{9,1},{2,10},{10,2},{3,11},{11,3},{4,12},{12,4},... | collective-permute-start | bytes 1597448 | tf_op jit(solution)/shard_map/ppermute | solution.py:33
  (12 other events, 11.2 us)
Sparse Core Ops, SparseCore 0:
  10.3 74.5 all-gather.2
  112.8 38.0 all-gather.4
  153.3 58.2 reduce-scatter.1
